TPU v7x, 32 devices: a whole 2x2x4 slice. The times are simulated.
32 devices in a mesh: seq: 16 (over z, y, core), wsh: 2 (over x).
Axes of the slice: x: 2, y: 2, z: 4, core: 2. Of those that a mesh axis runs over, the one named last changes fastest.
Arguments:
- hidden: bfloat16 [8, 1024, 2048], P('wsh', 'seq'), may hold values from -6 to 6
- cotangent: bfloat16 [8, 1024, 2048], P('wsh', 'seq'), may hold values from -6 to 6
- norm_gain: float32 [2048], replicated, may hold values from 0.1 to 1.9
- in_proj: bfloat16 [2048, 8512], P('wsh'), may hold values from -0.088388348 to 0.088388348
- conv_weight: float32 [4, 4352], replicated, may hold values from -3 to 3
- conv_bias: float32 [4352], replicated, may hold values from -1.5 to 1.5
- dt_bias: float32 [64], replicated, may hold values from -1.5 to 0.5
- a_log: float32 [64], replicated, may hold values from -12 to -3.4
- d_skip: float32 [64], replicated, may hold values from 0.5 to 1.5
- gate_gain: float32 [4096], replicated, may hold values from 0.1 to 1.9
- out_proj: bfloat16 [4096, 2048], P('wsh'), may hold values from -0.09375 to 0.09375
Outputs:
- block_out: bfloat16 [8, 1024, 2048], P('wsh', 'seq')
- hidden_grad: float32 [8, 1024, 2048], P('wsh', 'seq')
- norm_gain_grad: float32 [2048], replicated
- in_proj_grad: float32 [2048, 8512], P(('seq', 'wsh'))
- conv_weight_grad: float32 [4, 4352], replicated
- conv_bias_grad: float32 [4352], replicated
- dt_bias_grad: float32 [64], replicated
- a_log_grad: float32 [64], replicated
- d_skip_grad: float32 [64], replicated
- gate_gain_grad: float32 [4096], replicated
- out_proj_grad: float32 [4096, 2048], P(('seq', 'wsh'))
All inputs are finite; a program needn't handle non-finite values.
Results may differ from a plain program's by a relative error of at most 0.02.
The roundings to bfloat16 on the way count: a program that leaves them out, or rounds other values in their place, can miss the bound.
Values may be sent and summed in bfloat16 or wider, within the bound.
No kernel may reach another device: no remote copies, remote signals or barrier semaphores. Data moves between devices by JAX's collectives and lax.ppermute only.
A program may use at most 384 MiB of HBM per device.

v0:
```python
import jax
import jax.numpy as jnp
from jax import lax
from jax.sharding import PartitionSpec as P

STATE = 128
HEADDIM = 64
SPAN = 256
INNER = 4096


EPS = 1e-05
HIGH = lax.Precision.HIGHEST


def rms_norm(values, scale_vec):
    return values * lax.rsqrt(jnp.mean(values * values, axis=-1, keepdims=True) + EPS) * scale_vec


def gated_norm(mixed, gate_part, scale_vec):
    return rms_norm(mixed * jax.nn.silu(gate_part), scale_vec)


def causal_conv(signal, weight, bias_vec):
    tap_count = weight.shape[0]
    length = signal.shape[0]
    padded = jnp.concatenate([jnp.zeros((tap_count - 1, signal.shape[1]), jnp.float32), signal], 0)
    running = bias_vec[None, :] + padded[0:length] * weight[0]
    for offset in range(1, tap_count):
        running = running + padded[offset : offset + length] * weight[offset]
    return running


def span_step(carry, block):
    state, neg_rate = carry
    x_block, step_block, b_block, c_block = block
    cums = jnp.cumsum(step_block * neg_rate[None, :], axis=0)
    cums_head = cums.T
    scores = jnp.dot(c_block, b_block.T, precision=HIGH)
    rows = lax.broadcasted_iota(jnp.int32, (SPAN, SPAN), 0)
    cols = lax.broadcasted_iota(jnp.int32, (SPAN, SPAN), 1)
    causal = (rows >= cols)[None, :, :]
    spread = jnp.where(causal, cums_head[:, :, None] - cums_head[:, None, :], 0.0)
    decay = jnp.where(causal, jnp.exp(spread), 0.0)
    weights = decay * scores[None, :, :] * step_block.T[:, None, :]
    inner = jnp.einsum("hij,jhp->ihp", weights, x_block, precision=HIGH)
    carried = jnp.einsum("in,hnp->ihp", c_block, state, precision=HIGH) * jnp.exp(cums)[:, :, None]
    tail = jnp.exp(cums[-1][None, :] - cums) * step_block
    fresh = jnp.einsum("jh,jn,jhp->hnp", tail, b_block, x_block, precision=HIGH)
    state = state * jnp.exp(cums[-1])[:, None, None] + fresh
    return ((state, neg_rate), inner + carried)


def scan_spans(x_heads, steps, bmat, cmat, neg_rate):
    length, head_count, head_width = x_heads.shape
    count = length // SPAN
    blocks = (
        x_heads.reshape(count, SPAN, head_count, head_width),
        steps.reshape(count, SPAN, head_count),
        bmat.reshape(count, SPAN, bmat.shape[1]),
        cmat.reshape(count, SPAN, cmat.shape[1]),
    )
    start_state = jnp.zeros((head_count, bmat.shape[1], head_width), jnp.float32)
    carry, outputs = lax.scan(jax.checkpoint(span_step), (start_state, neg_rate), blocks)
    return outputs.reshape(length, head_count, head_width)


def local_mixer(x_in, dt_in, bc_in, conv_x, bias_x, conv_bc, bias_bc, dt_shift, log_rate, skip):
    length = x_in.shape[0]
    head_count = dt_in.shape[1]
    x_act = jax.nn.silu(causal_conv(x_in, conv_x, bias_x))
    bc_act = jax.nn.silu(causal_conv(bc_in, conv_bc, bias_bc))
    steps = jax.nn.softplus(dt_in + dt_shift[None, :])
    x_heads = x_act.reshape(length, head_count, x_act.shape[1] // head_count)
    state_size = bc_act.shape[1] // 2
    outputs = scan_spans(
        x_heads, steps, bc_act[:, :state_size], bc_act[:, state_size:], -jnp.exp(log_rate)
    )
    outputs = outputs + skip[None, :, None] * x_heads
    return outputs.reshape(length, x_act.shape[1])


def contract_rows(left, right):
    return lax.dot_general(
        left, right, (((0,), (0,)), ((), ())), preferred_element_type=jnp.float32
    )


def contract_cols(left, right):
    return lax.dot_general(
        left, right, (((1,), (1,)), ((), ())), preferred_element_type=jnp.float32
    )


def shards(
    hidden,
    cotangent,
    norm_gain,
    in_proj,
    conv_weight,
    conv_bias,
    dt_bias,
    a_log,
    d_skip,
    gate_gain,
    out_proj,
):
    seq_parts = lax.axis_size("seq")
    seq_place = lax.axis_index("seq")
    wsh_parts = lax.axis_size("wsh")
    wsh_place = lax.axis_index("wsh")
    owner_count = seq_parts * wsh_parts
    head_width = INNER // seq_parts
    local_heads = head_width // HEADDIM
    micro_count = hidden.shape[0]
    proj_width = in_proj.shape[1]
    model_width = hidden.shape[2]
    conv_x = lax.dynamic_slice_in_dim(conv_weight, seq_place * head_width, head_width, 1)
    bias_x = lax.dynamic_slice_in_dim(conv_bias, seq_place * head_width, head_width, 0)
    conv_bc = conv_weight[:, INNER:]
    bias_bc = conv_bias[INNER:]
    shift_local = lax.dynamic_slice_in_dim(dt_bias, seq_place * local_heads, local_heads, 0)
    rate_local = lax.dynamic_slice_in_dim(a_log, seq_place * local_heads, local_heads, 0)
    skip_local = lax.dynamic_slice_in_dim(d_skip, seq_place * local_heads, local_heads, 0)
    zero_index = jnp.zeros((), jnp.int32)

    def owned_columns(values):
        row_count, width = values.shape
        block = width // owner_count
        grouped = values.reshape(row_count, seq_parts, wsh_parts, block)
        picked = lax.dynamic_slice_in_dim(grouped, wsh_place, 1, 2)
        return picked.reshape(row_count, seq_parts * block)

    in_grad_rows = jnp.zeros((model_width // wsh_parts, proj_width), jnp.float32)
    out_grad_rows = jnp.zeros((INNER // wsh_parts, model_width), jnp.float32)
    ngain_sum = jnp.zeros((model_width,), jnp.float32)
    ggain_sum = jnp.zeros((INNER,), jnp.float32)
    conv_sum = jnp.zeros(conv_weight.shape, jnp.float32)
    cbias_sum = jnp.zeros(conv_bias.shape, jnp.float32)
    shift_sum = jnp.zeros(dt_bias.shape, jnp.float32)
    rate_sum = jnp.zeros(a_log.shape, jnp.float32)
    skip_sum = jnp.zeros(d_skip.shape, jnp.float32)
    layer_outs = []
    input_grads = []
    for micro_index in range(micro_count):
        tokens = hidden[micro_index].astype(jnp.float32)
        normed, norm_pull = jax.vjp(rms_norm, tokens, norm_gain)
        normed_low = normed.astype(jnp.bfloat16)
        proj_low = jnp.dot(
            normed_low,
            lax.all_gather(in_proj, "wsh", axis=0, tiled=True),
            preferred_element_type=jnp.float32,
        ).astype(jnp.bfloat16)
        gate_low = proj_low[:, :INNER]
        x_heads, dt_heads = (
            lax.all_to_all(
                proj_low[:, INNER : 2 * INNER], "seq", split_axis=1, concat_axis=0, tiled=True
            ),
            lax.all_to_all(
                proj_low[:, 2 * INNER + 2 * STATE :], "seq", split_axis=1, concat_axis=0, tiled=True
            ),
        )
        bc_seq = lax.all_gather(
            proj_low[:, 2 * INNER : 2 * INNER + 2 * STATE], "seq", axis=0, tiled=True
        )
        mixed, mixer_pull = jax.vjp(
            local_mixer,
            x_heads.astype(jnp.float32),
            dt_heads.astype(jnp.float32),
            bc_seq.astype(jnp.float32),
            conv_x,
            bias_x,
            conv_bc,
            bias_bc,
            shift_local,
            rate_local,
            skip_local,
        )
        mixed_tokens = lax.all_to_all(
            mixed.astype(jnp.bfloat16), "seq", split_axis=0, concat_axis=1, tiled=True
        )
        gated, gate_pull = jax.vjp(
            gated_norm, mixed_tokens.astype(jnp.float32), gate_low.astype(jnp.float32), gate_gain
        )
        gated_low = gated.astype(jnp.bfloat16)
        layer_outs.append(
            (
                tokens
                + jnp.dot(
                    gated_low,
                    lax.all_gather(out_proj, "wsh", axis=0, tiled=True),
                    preferred_element_type=jnp.float32,
                )
            ).astype(jnp.bfloat16)
        )
        grad_out = cotangent[micro_index]
        d_gated = contract_cols(grad_out, lax.all_gather(out_proj, "wsh", axis=0, tiled=True))
        d_mixed, d_gate, d_ggain = gate_pull(d_gated)
        d_heads = lax.all_to_all(
            d_mixed.astype(jnp.bfloat16), "seq", split_axis=1, concat_axis=0, tiled=True
        )
        d_x, d_dt, d_bc, g_cx, g_bx, g_cbc, g_bbc, g_shift, g_rate, g_skip = mixer_pull(
            d_heads.astype(jnp.float32)
        )
        d_x_tokens, d_dt_tokens = (
            lax.all_to_all(
                d_x.astype(jnp.bfloat16), "seq", split_axis=0, concat_axis=1, tiled=True
            ),
            lax.all_to_all(
                d_dt.astype(jnp.bfloat16), "seq", split_axis=0, concat_axis=1, tiled=True
            ),
        )
        d_bc_tokens = lax.psum_scatter(
            d_bc.astype(jnp.bfloat16), "seq", scatter_dimension=0, tiled=True
        )
        d_proj = jnp.concatenate(
            [d_gate.astype(jnp.bfloat16), d_x_tokens, d_bc_tokens, d_dt_tokens], 1
        )
        d_normed = contract_cols(d_proj, lax.all_gather(in_proj, "wsh", axis=0, tiled=True))
        d_tokens, d_ngain = norm_pull(d_normed)
        input_grads.append(grad_out.astype(jnp.float32) + d_tokens)
        normed_all, gated_all, dproj_all, grad_all = (
            lax.all_gather(normed_low, "wsh", axis=0, tiled=True),
            lax.all_gather(gated_low, "wsh", axis=0, tiled=True),
            lax.all_gather(d_proj, "wsh", axis=0, tiled=True),
            lax.all_gather(grad_out, "wsh", axis=0, tiled=True),
        )
        in_grad_rows = in_grad_rows + contract_rows(owned_columns(normed_all), dproj_all)
        out_grad_rows = out_grad_rows + contract_rows(owned_columns(gated_all), grad_all)
        ngain_sum = ngain_sum + d_ngain
        ggain_sum = ggain_sum + d_ggain
        conv_placed = lax.dynamic_update_slice(
            jnp.zeros((conv_weight.shape[0], INNER), jnp.float32),
            g_cx,
            (zero_index, seq_place * head_width),
        )
        conv_sum = conv_sum + jnp.concatenate([conv_placed, g_cbc], 1)
        cbias_placed = lax.dynamic_update_slice(
            jnp.zeros((INNER,), jnp.float32), g_bx, (seq_place * head_width,)
        )
        cbias_sum = cbias_sum + jnp.concatenate([cbias_placed, g_bbc], 0)
        shift_sum = shift_sum + lax.dynamic_update_slice(
            jnp.zeros(dt_bias.shape, jnp.float32), g_shift, (seq_place * local_heads,)
        )
        rate_sum = rate_sum + lax.dynamic_update_slice(
            jnp.zeros(a_log.shape, jnp.float32), g_rate, (seq_place * local_heads,)
        )
        skip_sum = skip_sum + lax.dynamic_update_slice(
            jnp.zeros(d_skip.shape, jnp.float32), g_skip, (seq_place * local_heads,)
        )
    in_grad_shard, out_grad_shard = (
        lax.psum_scatter(
            in_grad_rows.astype(jnp.bfloat16), "seq", scatter_dimension=0, tiled=True
        ).astype(jnp.float32),
        lax.psum_scatter(
            out_grad_rows.astype(jnp.bfloat16), "seq", scatter_dimension=0, tiled=True
        ).astype(jnp.float32),
    )
    ngain_all, conv_all, cbias_all, shift_all, rate_all, skip_all, ggain_all = lax.psum(
        (ngain_sum, conv_sum, cbias_sum, shift_sum, rate_sum, skip_sum, ggain_sum), ("seq", "wsh")
    )
    return (
        jnp.stack(layer_outs, 0),
        jnp.stack(input_grads, 0),
        ngain_all,
        in_grad_shard,
        conv_all,
        cbias_all,
        shift_all,
        rate_all,
        skip_all,
        ggain_all,
        out_grad_shard,
    )


def solution(mesh):
    placed = (
        P("wsh", "seq", None),
        P("wsh", "seq", None),
        P(),
        P("wsh", None),
        P(),
        P(),
        P(),
        P(),
        P(),
        P(),
        P("wsh", None),
    )
    return jax.shard_map(
        shards,
        mesh=mesh,
        in_specs=placed,
        out_specs=(
            P("wsh", "seq", None),
            P("wsh", "seq", None),
            P(),
            P(("seq", "wsh"), None),
            P(),
            P(),
            P(),
            P(),
            P(),
            P(),
            P(("seq", "wsh"), None),
        ),
        check_vma=False,
    )
```

profile of v0, /device:TPU:0, one launch (start us, length us, event | category | flops | bytes accessed | tf_op | source)
XLA Modules:
  0.0 2463.1 jit_solution(18416494728522179146)
XLA Ops:
  9.7 408.1 %all-gather.15.cloned.1.call-done = bf16[2048,8512]{0,1:T(8,128)(2,1)} async-done(((bf16[1024,8512]{0,1:T(8,128)(2,1)}), bf16[2048,8512]{0,1:T(8,128)(2,1)}) %all-gather.15.cloned.1.call-update) | async-done | bytes 34865168 | tf_op jit(solution)/shard_map/all_gather | solution.py:151
  417.8 15.4 convolution_convert_fusion.1
  440.7 15.4 convolution_convert_fusion.2
  463.1 15.4 convolution_convert_fusion
  485.5 15.4 convolution_convert_fusion.3
  537.4 26.7 %all_gather.81 = bf16[1024,256]{1,0:T(8,128)(2,1)S(1)} all-gather(bf16[64,256]{1,0:T(8,128)(2,1)S(1)} %slice-done.8), channel_id=1, replica_groups=mesh['seq'=16,'wsh'=2] {'seq'}, dimensions={0}, use_global_device_ids=true | all-gather | bytes 557056 | tf_op jit(solution)/shard_map/all_gather | solution.py:163
  564.2 21.1 all_gather.85
  585.5 18.9 all_gather.83
  605.5 20.2 all_gather.84
  690.0 47.1 %while.186 = (s32[]{:T(128)}, f32[4,128,64]{1,2,0:T(8,128)S(1)}, f32[4,256,4,64]{1,3,2,0:T(8,128)}, f32[4,4,128,64]{2,3,1,0:T(8,128)}, f32[4,4]{1,0:T(4,128)S(1)...) while((s32[]{:T(128)}, f32[4,128,64]{1,2,0:T(8,128)S(1)}, ...), condition=%wide.region_16.18_spmd.clone.clone, body=%wide.region_13.17_spmd.clone.clone.sunk | while | flops 505056256 | bytes 3301047 | solution.py:64
  745.7 52.4 %while.185 = (s32[]{:T(128)}, f32[4,128,64]{1,2,0:T(8,128)S(1)}, f32[4,256,4,64]{1,3,2,0:T(8,128)}, f32[4,4,128,64]{2,3,1,0:T(8,128)}, f32[4,4]{1,0:T(4,128)}, /...) while((s32[]{:T(128)}, f32[4,128,64]{1,2,0:T(8,128)S(1)}, ...), condition=%wide.region_10.12_spmd.clone.clone, body=%wide.region_7.11_spmd.clone.clone.sunk | while | flops 505056256 | bytes 3301047 | solution.py:64
  805.9 47.2 %while.184 = (s32[]{:T(128)}, f32[4,128,64]{1,2,0:T(8,128)S(1)}, f32[4,256,4,64]{1,3,2,0:T(8,128)}, f32[4,4,128,64]{2,3,1,0:T(8,128)}, f32[4,4]{1,0:T(4,128)S(1)...) while((s32[]{:T(128)}, f32[4,128,64]{1,2,0:T(8,128)S(1)}, ...), condition=%wide.region_4.6_spmd.clone.clone, body=%wide.region_1.5_spmd.clone.clone.sunk | while | flops 505056256 | bytes 3301047 | solution.py:64
  862.7 18.4 all_to_all.360
  944.6 16.0 multiply_reduce_fusion.21
  970.7 39.6 %while.187 = (s32[]{:T(128)}, f32[4,128,64]{1,2,0:T(8,128)S(1)}, f32[4,256,4,64]{1,3,2,0:T(8,128)}, f32[4,4,128,64]{2,3,1,0:T(8,128)}, f32[4,4]{1,0:T(4,128)S(1)...) while((s32[]{:T(128)}, f32[4,128,64]{1,2,0:T(8,128)S(1)}, ...), condition=%wide.region_22.24_spmd.clone.clone, body=%wide.region_19.23_spmd.clone.clone.sunk | while | flops 505056256 | bytes 3301543 | solution.py:64
  1026.0 130.4 %while.181 = (s32[]{:T(128)}, f32[4,128,64]{1,2,0:T(8,128)}, f32[4]{0:T(128)S(1)}, f32[4,256,4,64]{1,3,2,0:T(8,128)}, f32[4,256,4]{1,2,0:T(4,128)}, /*index=5*/f...) while((s32[]{:T(128)}, f32[4,128,64]{1,2,0:T(8,128)}, ...), condition=%wide.region_55.57_spmd.clone, body=%wide.region_42.56_spmd.clone.sunk | while | flops 1214300160 | bytes 9763656 | solution.py:64
  1237.9 95.1 %while.183 = (s32[]{:T(128)}, f32[4,128,64]{1,2,0:T(8,128)S(1)}, f32[4]{0:T(128)}, f32[4,256,4,64]{1,3,2,0:T(8,128)}, f32[4,256,4]{1,2,0:T(4,128)S(1)}, /*index=...) while((s32[]{:T(128)}, f32[4,128,64]{1,2,0:T(8,128)S(1)}, ...), condition=%wide.region_89.91_spmd.clone, body=%wide.region_76.90_spmd.clone.sunk | while | flops 1214300160 | bytes 9714052 | solution.py:64
  1347.7 84.5 %while.182 = (s32[]{:T(128)}, f32[4,128,64]{1,2,0:T(8,128)S(1)}, f32[4]{0:T(128)S(1)}, f32[4,256,4,64]{1,3,2,0:T(8,128)}, f32[4,256,4]{1,2,0:T(4,128)S(1)}, /*in...) while((s32[]{:T(128)}, f32[4,128,64]{1,2,0:T(8,128)S(1)}, ...), condition=%wide.region_72.74_spmd.clone, body=%wide.region_59.73_spmd.clone.sunk | while | flops 1214300160 | bytes 9713960 | solution.py:64
  1440.8 84.9 %while.180 = (s32[]{:T(128)}, f32[4,128,64]{1,2,0:T(8,128)S(1)}, f32[4]{0:T(128)S(1)}, f32[4,256,4,64]{1,3,2,0:T(8,128)}, f32[4,256,4]{1,2,0:T(4,128)S(1)}, /*in...) while((s32[]{:T(128)}, f32[4,128,64]{1,2,0:T(8,128)S(1)}, ...), condition=%wide.region_38.40_spmd.clone, body=%wide.region_25.39_spmd.clone.sunk | while | flops 1214300160 | bytes 9713960 | solution.py:64
  1721.7 15.9 all-gather.31.cloned.1.call-done
  1753.9 43.1 %reduce-scatter.11.cloned.1.call-done = bf16[64,256]{1,0:T(8,128)(2,1)} async-done(((bf16[1024,256]{1,0:T(8,128)(2,1)}), bf16[64,256]{1,0:T(8,128)(2,1)}) %reduce-scatter.11.cloned.1.call-update) | async-done | bytes 32784 | tf_op jit(solution)/shard_map/reduce_scatter | solution.py:213
  1841.5 37.2 %reduce-scatter.13.cloned.1.call-done = bf16[64,256]{1,0:T(8,128)(2,1)} async-done(((bf16[1024,256]{1,0:T(8,128)(2,1)}), bf16[64,256]{1,0:T(8,128)(2,1)}) %reduce-scatter.13.cloned.1.call-update) | async-done | bytes 32784 | tf_op jit(solution)/shard_map/reduce_scatter | solution.py:213
  1891.5 20.1 add_convert_fusion.1
  1960.5 16.4 fusion.528
  1998.1 16.2 fusion.529
  2014.4 19.4 all-gather.25.cloned.1.call-done
  2033.8 44.5 %add_convert_fusion = bf16[1024,8512]{1,0:T(8,128)(2,1)} fusion(f32[1024,8512]{1,0:T(8,128)} %fusion.529, f32[1024,8512]{1,0:T(8,128)} %fusion.527, f32[1024,8512]{1,0:T(8,128)} %fusion.528, bf16[128,1024]{0,1:T(8,128)(2,1)S(1)} %bitcast.1980, bf16[128,8512]{1,0:T(8,128)(2,1)} %all-gather.25.cloned.1.call-done), kind=kOutput, calls=%fused_computation.516 | convolution fusion | flops 2266234880 | bytes 124469248 | tf_op jit(solution)/shard_map/dot_general | solution.py:84
  2156.5 21.6 fusion.490
  2178.2 19.6 fusion.417
  2202.2 44.6 %all-reduce.88 = (f32[2048]{0:T(1024)}, f32[4352]{0:T(1024)}, f32[64]{0:T(128)}, f32[64]{0:T(128)}, f32[64]{0:T(128)}, /*index=5*/f32[4096]{0:T(1024)}) all-reduce(f32[2048]{0:T(1024)S(1)} %add_add_fusion.9, f32[4352]{0:T(1024)S(1)} %fusion.462, ...), channel_id=1, replica_groups=mesh['seq'=16,'wsh'=2] {'seq','wsh'}, use_global_device_ids=true, to_apply=%region_96.98 | all-reduce | flops 10688 | bytes 85504 | tf_op jit(solution)/shard_map/psum | solution.py:259
  2248.9 83.0 %reduce-scatter.15.cloned.1.call-done = bf16[64,8512]{1,0:T(8,128)(2,1)} async-done(((bf16[1024,8512]{1,0:T(8,128)(2,1)}), bf16[64,8512]{1,0:T(8,128)(2,1)}) %reduce-scatter.15.cloned.1.call-update) | async-done | bytes 1089552 | tf_op jit(solution)/shard_map/reduce_scatter | solution.py:252
  2334.6 120.2 %all-reduce.91.cloned.1.call-done = f32[4,4352]{1,0:T(4,128)} async-done(((f32[4,4352]{1,0:T(4,128)}), f32[4,4352]{1,0:T(4,128)}) %all-reduce.91.cloned.1.call-update) | async-done | bytes 69648 | tf_op jit(solution)/shard_map/psum | solution.py:259
  (1967 shorter events, 1349.8 us)
Async XLA Ops:
  7.2 410.6 %all-gather.15.cloned.1.call-start = ((), (), s32[]{:S(2)}) async-start(), calls=%async_computation.30 | async-start | bytes 52297728 | tf_op jit(solution)/shard_map/all_gather | solution.py:151
  435.0 22.1 all-to-all-start.6
  457.1 22.4 all-to-all-start.3
  479.5 23.3 all-to-all-start.9
  518.7 385.2 %all-gather.17.cloned.1.call-start = ((), (), s32[]{:S(2)}) async-start(), calls=%async_computation.31 | async-start | bytes 25165824 | tf_op jit(solution)/shard_map/all_gather | solution.py:191
  533.1 93.5 %all-to-all-start.10 = ((bf16[64,16,256]{2,0,1:T(8,128)(2,1)}), bf16[64,16,256]{2,0,1:T(8,128)(2,1)}, u32[]{:S(2)}, u32[]{:S(2)}) async-start(bf16[64,16,256]{2,0,1:T(8,128)(2,1)} %bitcast.1286), calls=%async_computation.10 | async-start | bytes 1048576 | tf_op jit(solution)/shard_map/all_to_all | solution.py:156
  626.6 19.2 all-to-all-start.1
  899.7 25.3 %all-to-all-start.5 = ((bf16[16,64,256]{2,1,0:T(8,128)(2,1)}), bf16[16,64,256]{2,1,0:T(8,128)(2,1)}, u32[]{:S(2)}, u32[]{:S(2)}) async-start(bf16[16,64,256]{2,1,0:T(8,128)(2,1)} %bitcast.1944), calls=%async_computation.5 | async-start | bytes 1048576 | tf_op jit(solution)/shard_map/all_to_all | solution.py:179
  962.5 54.1 %all-to-all-start.15 = ((bf16[64,16,256]{2,0,1:T(8,128)(2,1)}), bf16[64,16,256]{2,0,1:T(8,128)(2,1)}, u32[]{:S(2)}, u32[]{:S(2)}) async-start(bf16[64,16,256]{2,0,1:T(8,128)(2,1)} %bitcast.1958), calls=%async_computation.16 | async-start | bytes 1048576 | tf_op jit(solution)/shard_map/all_to_all | solution.py:199
  1167.5 21.1 all-to-all-start.11
  1226.1 106.9 %all-to-all-start.18 = ((bf16[64,16,256]{2,0,1:T(8,128)(2,1)}), bf16[64,16,256]{2,0,1:T(8,128)(2,1)}, u32[]{:S(2)}, u32[]{:S(2)}) async-start(bf16[64,16,256]{2,0,1:T(8,128)(2,1)} %bitcast.1283), calls=%async_computation.20 | async-start | bytes 1048576 | tf_op jit(solution)/shard_map/all_to_all | solution.py:199
  1333.0 99.2 %all-to-all-start.12 = ((bf16[64,16,256]{2,0,1:T(8,128)(2,1)}), bf16[64,16,256]{2,0,1:T(8,128)(2,1)}, u32[]{:S(2)}, u32[]{:S(2)}) async-start(bf16[64,16,256]{2,0,1:T(8,128)(2,1)} %bitcast.1957), calls=%async_computation.12 | async-start | bytes 1048576 | tf_op jit(solution)/shard_map/all_to_all | solution.py:199
  1339.0 269.9 %reduce-scatter.9.cloned.1.call-start = ((), (), s32[]{:S(2)}) async-start(), calls=%async_computation.33 | async-start | bytes 557056 | tf_op jit(solution)/shard_map/reduce_scatter | solution.py:213
  1539.0 118.0 %reduce-scatter.7.cloned.1.call-start = ((), (), s32[]{:S(2)}) async-start(), calls=%async_computation.32 | async-start | bytes 557056 | tf_op jit(solution)/shard_map/reduce_scatter | solution.py:213
  1542.4 172.5 %all-gather.29.cloned.1.call-start = ((), (), s32[]{:S(2)}) async-start(), calls=%async_computation.43 | async-start | bytes 1572864 | tf_op jit(solution)/shard_map/all_gather | solution.py:224
  1542.9 177.0 %all-gather.33.cloned.1.call-start = ((), (), s32[]{:S(2)}) async-start(), calls=%async_computation.45 | async-start | bytes 1572864 | tf_op jit(solution)/shard_map/all_gather | solution.py:224
  1543.5 194.2 %all-gather.31.cloned.1.call-start = ((), (), s32[]{:S(2)}) async-start(), calls=%async_computation.44 | async-start | bytes 1572864 | tf_op jit(solution)/shard_map/all_gather | solution.py:224
  1544.3 252.7 %reduce-scatter.11.cloned.1.call-start = ((), (), s32[]{:S(2)}) async-start(), calls=%async_computation.34 | async-start | bytes 557056 | tf_op jit(solution)/shard_map/reduce_scatter | solution.py:213
  1547.1 271.9 %all-gather.27.cloned.1.call-start = ((), (), s32[]{:S(2)}) async-start(), calls=%async_computation.42 | async-start | bytes 1572864 | tf_op jit(solution)/shard_map/all_gather | solution.py:224
  1549.6 34.2 %all-to-all-start.17 = ((bf16[16,2,128]{2,1,0:T(2,128)(2,1)}), bf16[16,2,128]{2,1,0:T(2,128)(2,1)S(1)}, u32[]{:S(2)}, u32[]{:S(2)}) async-start(bf16[16,2,128]{2,1,0:T(2,128)(2,1)} %reshape.1813), calls=%async_computation.19 | async-start | bytes 16384 | tf_op jit(solution)/shard_map/all_to_all | solution.py:209
  1583.8 20.6 all-to-all-start.16
  1589.9 288.8 %reduce-scatter.13.cloned.1.call-start = ((), (), s32[]{:S(2)}) async-start(), calls=%async_computation.35 | async-start | bytes 557056 | tf_op jit(solution)/shard_map/reduce_scatter | solution.py:213
  1608.7 351.8 %all-gather.21.cloned.1.call-start = ((), (), s32[]{:S(2)}) async-start(), calls=%async_computation.37 | async-start | bytes 3293184 | tf_op jit(solution)/shard_map/all_gather | solution.py:225
  1615.1 20.5 all-to-all-start.13
  1649.8 327.2 %all-gather.19.cloned.1.call-start = ((), (), s32[]{:S(2)}) async-start(), calls=%async_computation.36 | async-start | bytes 3293184 | tf_op jit(solution)/shard_map/all_gather | solution.py:225
  1659.1 87.9 %all-to-all-start.19 = ((bf16[16,64,256]{2,1,0:T(8,128)(2,1)}), bf16[16,64,256]{2,1,0:T(8,128)(2,1)}, u32[]{:S(2)}, u32[]{:S(2)}) async-start(bf16[16,64,256]{2,1,0:T(8,128)(2,1)} %bitcast.88), calls=%async_computation.21 | async-start | bytes 1048576 | tf_op jit(solution)/shard_map/all_to_all | solution.py:206
  1747.0 93.4 %all-to-all-start.22 = ((bf16[16,64,256]{2,1,0:T(8,128)(2,1)}), bf16[16,64,256]{2,1,0:T(8,128)(2,1)}, u32[]{:S(2)}, u32[]{:S(2)}) async-start(bf16[16,64,256]{2,1,0:T(8,128)(2,1)} %bitcast.1943), calls=%async_computation.25 | async-start | bytes 1048576 | tf_op jit(solution)/shard_map/all_to_all | solution.py:206
  1752.7 245.4 %all-gather.23.cloned.1.call-start = ((), (), s32[]{:S(2)}) async-start(), calls=%async_computation.38 | async-start | bytes 3293184 | tf_op jit(solution)/shard_map/all_gather | solution.py:225
  1799.2 234.6 %all-gather.25.cloned.1.call-start = ((), (), s32[]{:S(2)}) async-start(), calls=%async_computation.39 | async-start | bytes 3293184 | tf_op jit(solution)/shard_map/all_gather | solution.py:225
  1880.5 366.3 %reduce-scatter.17.cloned.1.call-start = ((), (), s32[]{:S(2)}) async-start(), calls=%async_computation.46 | async-start | bytes 8912896 | tf_op jit(solution)/shard_map/reduce_scatter | solution.py:255
  1911.7 420.2 %reduce-scatter.15.cloned.1.call-start = ((), (), s32[]{:S(2)}) async-start(), calls=%async_computation.40 | async-start | bytes 18661376 | tf_op jit(solution)/shard_map/reduce_scatter | solution.py:252
  2078.3 376.5 %all-reduce.91.cloned.1.call-start = ((), (), s32[]{:S(2)}) async-start(), calls=%async_computation.41 | async-start | bytes 139264 | tf_op jit(solution)/shard_map/psum | solution.py:259
  (274 other events, 7479.6 us)
Sparse Core Ops, SparseCore 0:
  9.6 408.1 all-gather.14
  521.1 199.2 all-gather.16
  1539.1 57.6 reduce-scatter.8
  1600.6 56.3 reduce-scatter.6
  1658.3 26.1 all-gather.28
  1685.9 27.8 all-gather.32
  1715.4 22.2 all-gather.30
  1741.2 55.7 reduce-scatter.10
  1798.6 20.3 all-gather.26
  1822.8 55.7 reduce-scatter.12
  1880.2 33.2 all-gather.20
  1915.5 46.4 all-gather.18
  1964.1 33.9 all-gather.22
  1999.5 34.2 all-gather.24
  2037.7 104.5 reduce-scatter.16
  2146.3 185.5 reduce-scatter.14
  2337.9 116.9 all-reduce.90
where the time goes:
time: 2480 us; the launch traced here: 2460 us
  waiting for transfers between devices  846 us (34%)
  matrix products  622 us (25%)
  other arithmetic  326 us (13%)
  local copies, waits for them, and re-layouts  289 us (12%)
  blocking collectives  245 us (10%)
  starting transfers between devices  116 us (5%)
    all_gather x1, waiting for transfers between devices, shards(): lax.all_gather(in_proj, 'wsh', axis=0, tiled=True)  408 us
    another operation x152, other arithmetic  155 us
    dot_general x8, matrix products, contract_rows(): lax.dot_general(left, right, (((0,), (0,)), ((), ())), preferred_element_...  141 us
    dot_general x8, matrix products, contract_cols(): lax.dot_general(left, right, (((1,), (1,)), ((), ())), preferred_element_...  124 us
    psum x1, waiting for transfers between devices, shards(): lax.psum((ngain_sum, conv_sum, cbias_sum, shift_sum, rate_sum, skip_sum,...  120 us
    dot_general x48, matrix products, span_step(): inner = jnp.einsum('hij,jhp->ihp', weights, x_block, precision=HIGH)  117 us
    reduce_scatter x4, waiting for transfers between devices, shards(): lax.psum_scatter(d_bc.astype(jnp.bfloat16), 'seq', scatter_dimension=0, t...  87.4 us
    all_gather x4, blocking collectives, shards(): lax.all_gather(proj_low[:, 2 * INNER:2 * INNER + 2 * STATE], 'seq', axis=...  86.9 us
  transfers between devices with their start and end apart: 40, of which 21 were waited for; matrix products, arithmetic and copies ran while one was open for 36% of the time, Pallas kernels for 0%

commit v1 on v0

v1 whole, which is shorter than its diff:
```python
import functools
import jax
import jax.numpy as jnp
from jax import lax
from jax.experimental import pallas as pl
from jax.experimental.pallas import tpu as pltpu
from jax.sharding import Mesh
from jax.sharding import PartitionSpec as P

STATE = 128
HEADDIM = 64
SPAN = 256
INNER = 4096
EPS = 1e-05
HIGH = lax.Precision.HIGHEST
NEG = -1e30
F32 = jnp.float32
BF16 = jnp.bfloat16


def dot_plain(left, right, precision=None):
    return lax.dot_general(
        left, right, (((1,), (0,)), ((), ())), preferred_element_type=F32, precision=precision
    )


def dot_lanes(left, right):
    return lax.dot_general(left, right, (((1,), (1,)), ((), ())), preferred_element_type=F32)


def dot_rows(left, right):
    return lax.dot_general(left, right, (((0,), (0,)), ((), ())), preferred_element_type=F32)


def softplus(values):
    return jnp.maximum(values, 0.0) + jnp.log1p(jnp.exp(-jnp.abs(values)))


def sigmoid(values):
    return 1.0 / (1.0 + jnp.exp(-values))


def head_rows(raw_steps, shift, neg_rate):
    span, heads = raw_steps.shape
    wide = jnp.concatenate([raw_steps, jnp.zeros((span, 128 - heads), F32)], 1)
    raw = wide.T[:heads] + shift
    step = softplus(raw)
    order = lax.broadcasted_iota(jnp.int32, (span, span), 0)
    until = lax.broadcasted_iota(jnp.int32, (span, span), 1)
    upper = jnp.where(order <= until, 1.0, 0.0)
    cum = dot_plain(step * neg_rate, upper, HIGH)
    last = cum[:, span - 1 :]
    return raw, step, cum, jnp.exp(cum), jnp.exp(last - cum)


def as_columns(rows):
    count, span = rows.shape
    return jnp.concatenate([rows, jnp.zeros((128 - count, span), F32)], 0).T


def spread_lanes(columns, start, heads):
    span = columns.shape[0]
    low = lax.broadcasted_iota(jnp.int32, (span, 2 * HEADDIM), 1) < HEADDIM
    pieces = []
    for pair in range(heads // 2):
        at = start + 2 * pair
        pieces.append(jnp.where(low, columns[:, at : at + 1], columns[:, at + 1 : at + 2]))
    return jnp.concatenate(pieces, 1)


def pair_halves(values, pair):
    slab = values[:, 2 * HEADDIM * pair : 2 * HEADDIM * (pair + 1)]
    low = lax.broadcasted_iota(jnp.int32, slab.shape, 1) < HEADDIM
    zero = jnp.zeros_like(slab)
    return slab, (jnp.where(low, slab, zero), jnp.where(low, zero, slab))


def convolve(window, taps, offset, span):
    running = None
    for k in range(taps.shape[0]):
        term = window[pl.ds(offset(k), span), :] * taps[k : k + 1, :]
        running = term if running is None else running + term
    return running


def scan_forward_body(
    heads,
    raw_ref,
    taps_ref,
    bias_ref,
    shift_ref,
    rate_ref,
    skip_ref,
    mixed_ref,
    start_ref,
    edge_ref,
    state,
    window,
):
    span = raw_ref.shape[0]
    inner = heads * HEADDIM
    wide = inner + 2 * STATE
    first = pl.program_id(1) == 0

    @pl.when(first)
    def _():
        state[...] = jnp.zeros_like(state)
        window[0:8, :] = jnp.zeros((8, wide), F32)

    @pl.when(jnp.logical_not(first))
    def _():
        window[0:8, :] = window[span : span + 8, :]

    edge_ref[...] = window[0:8, :]
    window[8 : 8 + span, :] = raw_ref[:, :wide].astype(F32)
    conv = convolve(window, taps_ref[...], lambda k: 5 + k, span) + bias_ref[...]
    act = conv * sigmoid(conv)
    x_act = act[:, :inner]
    b_low = act[:, inner : inner + STATE].astype(BF16)
    c_act = act[:, inner + STATE :]
    c_low = c_act.astype(BF16)
    c_both = jnp.concatenate([c_low, (c_act - c_low.astype(F32)).astype(BF16)], 1)
    raw, step, cum, grown, tail = head_rows(
        raw_ref[:, wide:].astype(F32), shift_ref[...], -jnp.exp(rate_ref[...])
    )
    columns = as_columns(jnp.concatenate([cum, step, grown, tail], 0))
    step_wide = spread_lanes(columns, heads, heads)
    grown_wide = spread_lanes(columns, 2 * heads, heads)
    tail_wide = spread_lanes(columns, 3 * heads, heads)
    stepped = x_act * step_wide
    stepped_low = stepped.astype(BF16)
    held = state[...]
    start_ref[...] = held
    held_low = held.astype(BF16)
    scores = dot_lanes(c_both, jnp.concatenate([b_low, b_low], 1))
    carried = dot_plain(c_both, jnp.concatenate([held_low, held_low], 0)) * grown_wide
    carried = carried + skip_ref[...] * x_act
    rows = lax.broadcasted_iota(jnp.int32, (span, span), 0)
    cols = lax.broadcasted_iota(jnp.int32, (span, span), 1)
    causal = rows >= cols
    for pair in range(heads // 2):
        _, halves = pair_halves(stepped_low, pair)
        total = carried[:, 2 * HEADDIM * pair : 2 * HEADDIM * (pair + 1)]
        for half in range(2):
            head = 2 * pair + half
            spread = columns[:, head : head + 1] - cum[head : head + 1, :]
            weights = jnp.exp(jnp.where(causal, spread, NEG)) * scores
            total = total + dot_plain(weights.astype(BF16), halves[half])
        mixed_ref[:, 2 * HEADDIM * pair : 2 * HEADDIM * (pair + 1)] = total.astype(BF16)
    fresh = dot_rows(b_low, (stepped * tail_wide).astype(BF16))
    state[...] = held * grown_wide[span - 1 : span, :] + fresh


def scan_forward(raw, at, taps, bias, shift, log_rate, skip_wide):
    _, length, width = raw.shape
    seqs = 1
    heads = shift.shape[0]
    inner = heads * HEADDIM
    wide = inner + 2 * STATE
    spans = length // SPAN
    whole = lambda shape: pl.BlockSpec(shape, lambda s, i: (0,) * len(shape))
    return pl.pallas_call(
        functools.partial(scan_forward_body, heads),
        grid=(seqs, spans),
        in_specs=[
            pl.BlockSpec((None, SPAN, width), lambda s, i: (at, i, 0)),
            whole(taps.shape),
            whole(bias.shape),
            whole(shift.shape),
            whole(log_rate.shape),
            whole(skip_wide.shape),
        ],
        out_specs=[
            pl.BlockSpec((None, SPAN, inner), lambda s, i: (s, i, 0)),
            pl.BlockSpec((None, None, STATE, inner), lambda s, i: (s, i, 0, 0)),
            pl.BlockSpec((None, None, 8, wide), lambda s, i: (s, i, 0, 0)),
        ],
        out_shape=[
            jax.ShapeDtypeStruct((seqs, length, inner), BF16),
            jax.ShapeDtypeStruct((seqs, spans, STATE, inner), F32),
            jax.ShapeDtypeStruct((seqs, spans, 8, wide), F32),
        ],
        scratch_shapes=[pltpu.VMEM((STATE, inner), F32), pltpu.VMEM((SPAN + 8, wide), F32)],
        compiler_params=kernel_params(),
        cost_estimate=light_cost(length),
        name="scan_forward",
    )(raw, taps, bias, shift, log_rate, skip_wide)


def scan_backward_body(
    heads,
    raw_ref,
    down_ref,
    start_ref,
    edge_ref,
    taps_ref,
    bias_ref,
    shift_ref,
    rate_ref,
    skip_ref,
    draw_ref,
    dtaps_ref,
    dskip_ref,
    dhead_ref,
    dstate,
    window,
    ahead,
):
    span = raw_ref.shape[0]
    inner = heads * HEADDIM
    wide = inner + 2 * STATE
    step_at = pl.program_id(1)

    @pl.when((pl.program_id(0) == 0) & (step_at == 0))
    def _():
        dtaps_ref[...] = jnp.zeros_like(dtaps_ref)
        dskip_ref[...] = jnp.zeros_like(dskip_ref)
        dhead_ref[...] = jnp.zeros_like(dhead_ref)

    @pl.when(step_at == 0)
    def _():
        dstate[...] = jnp.zeros_like(dstate)
        ahead[span : span + 8, :] = jnp.zeros((8, wide), F32)

    @pl.when(step_at != 0)
    def _():
        ahead[span : span + 8, :] = ahead[0:8, :]

    taps = taps_ref[...]
    window[0:8, :] = edge_ref[...]
    window[8 : 8 + span, :] = raw_ref[:, :wide].astype(F32)
    conv = convolve(window, taps, lambda k: 5 + k, span) + bias_ref[...]
    sig = sigmoid(conv)
    act = conv * sig
    x_act = act[:, :inner]
    b_low = act[:, inner : inner + STATE].astype(BF16)
    c_low = act[:, inner + STATE :].astype(BF16)
    neg_rate = -jnp.exp(rate_ref[...])
    raw, step, cum, grown, tail = head_rows(raw_ref[:, wide:].astype(F32), shift_ref[...], neg_rate)
    columns = as_columns(jnp.concatenate([cum, step, grown, tail], 0))
    step_wide = spread_lanes(columns, heads, heads)
    grown_wide = spread_lanes(columns, 2 * heads, heads)
    tail_wide = spread_lanes(columns, 3 * heads, heads)
    stepped = x_act * step_wide
    stepped_low = stepped.astype(BF16)
    down_low = down_ref[...]
    down = down_low.astype(F32)
    held = start_ref[...]
    held_low = held.astype(BF16)
    dheld = dstate[...]
    dheld_low = dheld.astype(BF16)
    scores = dot_lanes(b_low, c_low)
    rows = lax.broadcasted_iota(jnp.int32, (span, span), 0)
    cols = lax.broadcasted_iota(jnp.int32, (span, span), 1)
    causal = cols >= rows
    dscores = jnp.zeros((span, span), F32)
    dstepped_parts = []
    gained = []
    lost = []
    for pair in range(heads // 2):
        _, x_halves = pair_halves(stepped_low, pair)
        down_pair, down_halves = pair_halves(down_low, pair)
        total = jnp.zeros((span, 2 * HEADDIM), F32)
        for half in range(2):
            head = 2 * pair + half
            spread = cum[head : head + 1, :] - columns[:, head : head + 1]
            decay = jnp.exp(jnp.where(causal, spread, NEG))
            weights = decay * scores
            dweights = dot_lanes(x_halves[half], down_pair)
            dscores = dscores + decay * dweights
            both = weights * dweights
            gained.append(jnp.sum(both, axis=0, keepdims=True))
            lost.append(jnp.sum(both, axis=1, keepdims=True))
            total = total + dot_plain(weights.astype(BF16), down_halves[half])
        dstepped_parts.append(total)
    dscores_low = dscores.astype(BF16)
    dtail = dot_plain(b_low, dheld_low) * tail_wide
    dstepped = jnp.concatenate(dstepped_parts, 1) + dtail
    down_grown = (down * grown_wide).astype(BF16)
    d_b = dot_plain(dscores_low, c_low) + dot_lanes((stepped * tail_wide).astype(BF16), dheld_low)
    d_c = dot_rows(dscores_low, b_low) + dot_lanes(down_grown, held_low)
    carried = dot_plain(c_low, held_low) * grown_wide
    member = lax.broadcasted_iota(jnp.int32, (heads, inner), 1) // HEADDIM
    which = lax.broadcasted_iota(jnp.int32, (heads, inner), 0)
    pick = jnp.where(member == which, 1.0, 0.0)
    pick_low = pick.astype(BF16)
    carried_sum = dot_lanes(pick_low, (down * carried).astype(BF16))
    tail_sum = dot_lanes(pick_low, (stepped * dtail).astype(BF16))
    step_sum = dot_lanes(pick_low, (x_act * dstepped).astype(BF16))
    lost_rows = as_columns_back(jnp.concatenate(lost, 1))
    state_sum = jnp.sum(pick * jnp.sum(held * dheld, axis=0, keepdims=True), axis=1, keepdims=True)
    dcum = jnp.concatenate(gained, 0) + carried_sum - lost_rows - tail_sum
    since = jnp.where(rows >= cols, 1.0, 0.0)
    whole_part = jnp.sum(tail_sum, axis=1, keepdims=True) + grown[:, span - 1 :] * state_sum
    dlog = dot_plain(dcum, since, HIGH) + whole_part
    draw_step = (step_sum + neg_rate * dlog) * sigmoid(raw)
    dhead_ref[0] += neg_rate * jnp.sum(step * dlog, axis=1, keepdims=True)
    dhead_ref[1] += jnp.sum(draw_step, axis=1, keepdims=True)
    dskip_ref[...] += jnp.sum(down * x_act, axis=0, keepdims=True)
    d_x = dstepped * step_wide + skip_ref[...] * down
    dconv = jnp.concatenate([d_x, d_b, d_c], 1) * (sig * (1.0 + conv * (1.0 - sig)))
    ahead[0:span, :] = dconv
    draw = convolve(ahead, taps, lambda k: 3 - k, span)
    draw_ref[:, :wide] = draw.astype(BF16)
    draw_ref[:, wide:] = as_columns(draw_step)[:, :heads].astype(BF16)
    for k in range(taps.shape[0]):
        dtaps_ref[k : k + 1, :] += jnp.sum(
            dconv * window[pl.ds(5 + k, span), :], axis=0, keepdims=True
        )
    dtaps_ref[4:5, :] += jnp.sum(dconv, axis=0, keepdims=True)
    dstate[...] = dheld * grown_wide[span - 1 : span, :] + dot_rows(c_low, down_grown)


def as_columns_back(columns):
    span, heads = columns.shape
    return jnp.concatenate([columns, jnp.zeros((span, 128 - heads), F32)], 1).T[:heads]


def scan_backward(raw, at, down, starts, edges, taps, bias, shift, log_rate, skip_wide):
    _, length, width = raw.shape
    seqs = 1
    heads = shift.shape[0]
    inner = heads * HEADDIM
    wide = inner + 2 * STATE
    spans = length // SPAN
    whole = lambda shape: pl.BlockSpec(shape, lambda s, i: (0,) * len(shape))
    turned = lambda s, i: (s, spans - 1 - i, 0)
    return pl.pallas_call(
        functools.partial(scan_backward_body, heads),
        grid=(seqs, spans),
        in_specs=[
            pl.BlockSpec((None, SPAN, width), lambda s, i: (at, spans - 1 - i, 0)),
            pl.BlockSpec((None, SPAN, inner), turned),
            pl.BlockSpec((None, None, STATE, inner), lambda s, i: (s, spans - 1 - i, 0, 0)),
            pl.BlockSpec((None, None, 8, wide), lambda s, i: (s, spans - 1 - i, 0, 0)),
            whole(taps.shape),
            whole(bias.shape),
            whole(shift.shape),
            whole(log_rate.shape),
            whole(skip_wide.shape),
        ],
        out_specs=[
            pl.BlockSpec((None, SPAN, width), turned),
            whole((8, wide)),
            whole((1, inner)),
            whole((2, heads, 1)),
        ],
        out_shape=[
            jax.ShapeDtypeStruct((seqs, length, width), BF16),
            jax.ShapeDtypeStruct((8, wide), F32),
            jax.ShapeDtypeStruct((1, inner), F32),
            jax.ShapeDtypeStruct((2, heads, 1), F32),
        ],
        scratch_shapes=[
            pltpu.VMEM((STATE, inner), F32),
            pltpu.VMEM((SPAN + 8, wide), F32),
            pltpu.VMEM((SPAN + 8, wide), F32),
        ],
        compiler_params=kernel_params(),
        cost_estimate=light_cost(length),
        name="scan_backward",
    )(raw, down, starts, edges, taps, bias, shift, log_rate, skip_wide)


def kernel_params():
    return pltpu.CompilerParams(vmem_limit_bytes=30 * 1024 * 1024)


def light_cost(count):
    return pl.CostEstimate(flops=count, bytes_accessed=count, transcendentals=0)


def project_body(inner, tokens_ref, weight_ref, gate_ref, raw_ref, turned_ref):
    _, _, tokens, model = tokens_ref.shape
    values = tokens_ref[...].reshape(4 * tokens, model)
    put_by_member(gate_ref, dot_lanes(values, weight_ref[:inner, :]))
    put_by_member(raw_ref, dot_lanes(values, weight_ref[inner:, :]))
    for half in range(2):
        pair = jnp.concatenate([tokens_ref[core, half] for core in range(2)], 0)
        turned_ref[half] = pair.T


def project_tokens(values, weight, inner):
    team, _, tokens, model = values.shape
    width = weight.shape[0]

    def natural(size):
        return pl.BlockSpec((2, 2, tokens, size), lambda i: (0, i, 0, 0))

    return pl.pallas_call(
        functools.partial(project_body, inner),
        grid=(team // 2,),
        in_specs=[
            pl.BlockSpec((2, 2, tokens, model), lambda i: (i, 0, 0, 0)),
            pl.BlockSpec((width, model), lambda i: (0, 0)),
        ],
        out_specs=[
            natural(inner),
            natural(width - inner),
            pl.BlockSpec((2, model, 2 * tokens), lambda i: (0, 0, i)),
        ],
        out_shape=[
            jax.ShapeDtypeStruct((2, team, tokens, inner), BF16),
            jax.ShapeDtypeStruct((2, team, tokens, width - inner), BF16),
            jax.ShapeDtypeStruct((2, model, team * tokens), BF16),
        ],
        compiler_params=kernel_params(),
        cost_estimate=light_cost(team),
        name="project_tokens",
    )(values, weight)


def by_member(ref):
    return jnp.concatenate(
        [ref[half, member] for member in range(ref.shape[1]) for half in range(2)], 0
    )


def put_by_member(ref, rows):
    tokens = ref.shape[2]
    for member in range(ref.shape[1]):
        for half in range(2):
            at = (member * 2 + half) * tokens
            ref[half, member] = rows[at : at + tokens].astype(ref.dtype)


def gate_stats_body(grad_ref, weight_ref, mixed_ref, gate_ref, gain_ref, down_ref, sums_ref):
    pair, _, tokens, model = grad_ref.shape
    d_gated = dot_lanes(grad_ref[...].reshape(pair * 2 * tokens, model), weight_ref[...])
    gate = by_member(gate_ref).astype(F32)
    unit = by_member(mixed_ref).astype(F32) * gate * sigmoid(gate)
    put_by_member(down_ref, d_gated)
    square = jnp.sum(unit * unit, axis=1, keepdims=True)
    cross = jnp.sum(d_gated * gain_ref[...] * unit, axis=1, keepdims=True)
    sums_ref[...] = as_columns_back(jnp.concatenate([square, cross], 1))


def gate_stats(grad, weight, mixed, gate, gain):
    team, _, tokens, model = grad.shape
    inner = weight.shape[0]
    pair = 2
    rows = pair * 2 * tokens
    natural = pl.BlockSpec((2, pair, tokens, inner), lambda i: (0, i, 0, 0))
    return pl.pallas_call(
        gate_stats_body,
        grid=(team // pair,),
        in_specs=[
            pl.BlockSpec((pair, 2, tokens, model), lambda i: (i, 0, 0, 0)),
            pl.BlockSpec((inner, model), lambda i: (0, 0)),
            natural,
            natural,
            pl.BlockSpec((1, inner), lambda i: (0, 0)),
        ],
        out_specs=[
            natural,
            pl.BlockSpec((2, rows), lambda i: (0, i)),
        ],
        out_shape=[
            jax.ShapeDtypeStruct((2, team, tokens, inner), F32),
            jax.ShapeDtypeStruct((2, team * 2 * tokens), F32),
        ],
        compiler_params=kernel_params(),
        cost_estimate=light_cost(team),
        name="gate_stats",
    )(grad, weight, mixed, gate, gain)


def put_by_core(own, keep_ref, send_ref, rows):
    tokens = keep_ref.shape[1]
    first, second = rows[: 2 * tokens], rows[2 * tokens :]
    kept = jnp.where(own == 0, first, second)
    sent = jnp.where(own == 0, second, first)
    for half in range(2):
        keep_ref[half] = kept[half * tokens : (half + 1) * tokens].astype(BF16)
        send_ref[half] = sent[half * tokens : (half + 1) * tokens].astype(BF16)


def gate_back_body(
    table_ref,
    mixed_ref,
    gate_ref,
    down_ref,
    sums_ref,
    gain_ref,
    weight_ref,
    turned_ref,
    d_mixed_ref,
    d_gate_ref,
    keep_ref,
    send_ref,
    d_gain_ref,
):
    @pl.when(pl.program_id(0) == 0)
    def _():
        d_gain_ref[...] = jnp.zeros_like(d_gain_ref)

    columns = as_columns(sums_ref[...])
    gain = gain_ref[...]
    scale = lax.rsqrt(columns[:, 0:1] / INNER + EPS)
    pull = columns[:, 1:2] * (scale * scale * scale / INNER)
    mixed = by_member(mixed_ref).astype(F32)
    gate = by_member(gate_ref).astype(F32)
    down = by_member(down_ref)
    sig = sigmoid(gate)
    act = gate * sig
    unit = mixed * act
    scaled = unit * scale
    gated_wide = scaled * gain
    turned_ref[...] = gated_wide.T.astype(BF16)
    out = dot_plain(gated_wide.astype(BF16), weight_ref[...])
    put_by_core(table_ref[0], keep_ref, send_ref, out)
    d_unit = down * gain * scale - unit * pull
    put_by_member(d_mixed_ref, d_unit * act)
    put_by_member(d_gate_ref, d_unit * mixed * (sig * (1.0 + gate * (1.0 - sig))))
    d_gain_ref[...] += jnp.sum(down * scaled, axis=0, keepdims=True)


def gate_back(table, mixed, gate, down, sums, gain, weight):
    _, team, tokens, inner = down.shape
    model = weight.shape[1]
    chips = team // 2
    rows = 4 * tokens
    natural = pl.BlockSpec((2, 2, tokens, inner), lambda i, t: (0, t[1 + i], 0, 0))
    block = pl.BlockSpec((None, 2, tokens, model), lambda i, t: (i, 0, 0, 0))
    one = pl.BlockSpec((1, inner), lambda i, t: (0, 0))
    return pl.pallas_call(
        gate_back_body,
        grid_spec=pltpu.PrefetchScalarGridSpec(
            num_scalar_prefetch=1,
            grid=(chips,),
            in_specs=[
                natural,
                natural,
                natural,
                pl.BlockSpec((2, rows), lambda i, t: (0, t[1 + i])),
                one,
                pl.BlockSpec((inner, model), lambda i, t: (0, 0)),
            ],
            out_specs=[
                pl.BlockSpec((inner, rows), lambda i, t: (0, t[1 + i])),
                natural,
                natural,
                block,
                block,
                one,
            ],
        ),
        out_shape=[
            jax.ShapeDtypeStruct((inner, team * 2 * tokens), BF16),
            jax.ShapeDtypeStruct((2, team, tokens, inner), BF16),
            jax.ShapeDtypeStruct((2, team, tokens, inner), BF16),
            jax.ShapeDtypeStruct((chips, 2, tokens, model), BF16),
            jax.ShapeDtypeStruct((chips, 2, tokens, model), BF16),
            jax.ShapeDtypeStruct((1, inner), F32),
        ],
        compiler_params=kernel_params(),
        cost_estimate=light_cost(team),
        name="gate_back",
    )(table, mixed, gate, down, sums, gain, weight)


def row_grad_body(pairs, cols, has_base, *refs):
    out_ref = refs[-1]
    total = None
    for k in range(pairs):
        left_ref = refs[2 * k]
        right_ref = refs[2 * k + 1]
        count, _, depth = left_ref.shape
        for part in range(count):
            right = right_ref[part * depth : (part + 1) * depth, :]
            if cols is not None:
                right = right[:, cols[0] : cols[1]]
            term = dot_plain(left_ref[part], right)
            total = term if total is None else total + term
    if has_base:
        base = refs[2 * pairs][...]
        if cols is not None:
            base = base[:, cols[0] : cols[1]]
        total = total + base
    out_ref[...] = total.astype(out_ref.dtype)


def row_grad(operands, kind, cols=None, base=None):
    rows = operands[0][0].shape[1]
    width = operands[0][1].shape[1]
    got = width if cols is None else cols[1] - cols[0]
    tile = min(512, rows)
    if got > 1024:
        tile = min(256, rows)
    specs, args = [], []
    for left, right in operands:
        specs.append(pl.BlockSpec((left.shape[0], tile, left.shape[2]), lambda i: (0, i, 0)))
        specs.append(pl.BlockSpec(right.shape, lambda i: (0, 0)))
        args += [left, right]
    if base is not None:
        specs.append(pl.BlockSpec((tile, width), lambda i: (i, 0)))
        args.append(base)
    return pl.pallas_call(
        functools.partial(row_grad_body, len(operands), cols, base is not None),
        grid=(rows // tile,),
        in_specs=specs,
        out_specs=pl.BlockSpec((tile, got), lambda i: (i, 0)),
        out_shape=jax.ShapeDtypeStruct((rows, got), kind),
        compiler_params=kernel_params(),
        cost_estimate=light_cost(rows),
        name="row_grad",
    )(*args)


def norm_part_body(
    table_ref, d_gate_ref, d_raw_ref, normed_ref, weight_ref, keep_ref, send_ref, gain_ref
):
    @pl.when(pl.program_id(0) == 0)
    def _():
        gain_ref[...] = jnp.zeros_like(gain_ref)

    inner = d_gate_ref.shape[-1]
    tokens = keep_ref.shape[1]
    model = keep_ref.shape[2]
    part = dot_plain(by_member(d_gate_ref), weight_ref[:inner, :])
    part = part + dot_plain(by_member(d_raw_ref), weight_ref[inner:, :])
    normed = normed_ref[...].reshape(4 * tokens, model).astype(F32)
    gain_ref[...] += jnp.sum(part * normed, axis=0, keepdims=True)
    put_by_core(table_ref[0], keep_ref, send_ref, part)


def norm_part(table, d_gate, d_raw, normed, weight):
    _, team, tokens, inner = d_gate.shape
    chips = team // 2
    width = d_raw.shape[-1]
    model = weight.shape[1]

    def natural(size):
        return pl.BlockSpec((2, 2, tokens, size), lambda i, t: (0, t[1 + i], 0, 0))

    block = pl.BlockSpec((None, 2, tokens, model), lambda i, t: (i, 0, 0, 0))
    return pl.pallas_call(
        norm_part_body,
        grid_spec=pltpu.PrefetchScalarGridSpec(
            num_scalar_prefetch=1,
            grid=(chips,),
            in_specs=[
                natural(inner),
                natural(width),
                pl.BlockSpec((2, 2, tokens, model), lambda i, t: (t[1 + i], 0, 0, 0)),
                pl.BlockSpec((inner + width, model), lambda i, t: (0, 0)),
            ],
            out_specs=[block, block, pl.BlockSpec((1, model), lambda i, t: (0, 0))],
        ),
        out_shape=[
            jax.ShapeDtypeStruct((chips, 2, tokens, model), BF16),
            jax.ShapeDtypeStruct((chips, 2, tokens, model), BF16),
            jax.ShapeDtypeStruct((1, model), F32),
        ],
        compiler_params=kernel_params(),
        cost_estimate=light_cost(chips),
        name="norm_part",
    )(table, d_gate, d_raw, normed, weight)


TEAM = ("chip", "core")
ALL = ("half", "chip", "core")
EVERY = ALL + ("wsh",)


def after(values, *done):
    leaves, tree = jax.tree.flatten(values)
    others = jax.tree.leaves(done)
    out = lax.optimization_barrier(tuple(leaves) + tuple(others))
    return jax.tree.unflatten(tree, out[: len(leaves)])


def join(*values):
    leaves, tree = jax.tree.flatten(values)
    return jax.tree.unflatten(tree, lax.optimization_barrier(tuple(leaves)))


class Layout:
    def __init__(self):
        self.chips = lax.axis_size("chip")
        self.wsh = lax.axis_size("wsh")
        self.team = 2 * self.chips
        self.parts = 2 * self.team
        self.half = lax.axis_index("half")
        self.chip = lax.axis_index("chip")
        self.core = lax.axis_index("core")
        self.wplace = lax.axis_index("wsh")
        self.member = self.chip * 2 + self.core
        self.block = self.core * self.chips + self.chip

    def other_core(self, values):
        return lax.ppermute(values, "core", [(0, 1), (1, 0)])

    def other_half(self, values):
        return lax.ppermute(values, "half", [(0, 1), (1, 0)])

    def chip_flip(self, values, bits):
        return lax.ppermute(values, "chip", [(i, i ^ bits) for i in range(self.chips)])

    def wsh_shift(self, values, shift):
        size = self.wsh
        return lax.ppermute(values, "wsh", [(i, (i + shift) % size) for i in range(size)])


def pick(values, at, axis):
    return lax.dynamic_index_in_dim(values, at, axis, keepdims=False)


def split_halves(own, lay):
    count = own.shape[0] // 2
    keep = lax.dynamic_slice_in_dim(own, lay.half * count, count, 0)
    away = lax.dynamic_slice_in_dim(own, (1 - lay.half) * count, count, 0)
    return keep, away


def team_gather(keep, came, lay):
    pair = jnp.where(lay.half == 0, jnp.stack([keep, came]), jnp.stack([came, keep]))
    return lax.all_gather(pair, TEAM, axis=0)


def both_halves(mine, other, lay):
    first = jnp.where(lay.half == 0, mine, other)
    second = jnp.where(lay.half == 0, other, mine)
    return jnp.concatenate([first, second], 0)


def core_sum(keep, came):
    return (keep.astype(F32) + came.astype(F32)).astype(BF16)


def chip_parts(added, lay):
    return [added[0]] + [lay.chip_flip(added[bits], bits) for bits in range(1, lay.chips)]


def chip_sum(parts, lay):
    own = add_all([part.astype(F32) for part in parts]).astype(BF16)
    return pick(own, lay.half, 0), pick(own, 1 - lay.half, 0)


def columns_in_place(local, came, lay):
    wide = local.shape[1]
    full = jnp.zeros((local.shape[0], lay.wsh * wide), local.dtype)
    full = lax.dynamic_update_slice_in_dim(full, local, lay.wplace * wide, 1)
    for start, pieces in came:
        for shift, piece in enumerate(pieces):
            at = ((lay.wplace - shift - 1) % lay.wsh) * wide
            full = lax.dynamic_update_slice(full, piece, (start, at))
    return full


def team_parts(values, lay):
    values = values + lay.other_core(values)
    return [values] + [lay.chip_flip(values, bits) for bits in range(1, lay.chips)]


def add_all(parts):
    while len(parts) > 1:
        parts = [parts[k] + parts[k + 1] for k in range(0, len(parts), 2)]
    return parts[0]


class Order:
    def __init__(self):
        self.last = ()

    def __call__(self, step, first, *rest):
        first = after(first, self.last)
        out = step(first, *rest)
        self.last = (jax.tree.leaves(out)[0],)
        return out


def shards(
    hidden,
    cotangent,
    norm_gain,
    in_proj,
    conv_weight,
    conv_bias,
    dt_bias,
    a_log,
    d_skip,
    gate_gain,
    out_proj,
):
    lay = Layout()
    seqs, tokens, model = hidden.shape
    count = seqs // 2
    length = tokens * lay.parts
    inner = INNER // lay.team
    heads = inner // HEADDIM
    block = lay.block
    steps_at = 2 * INNER + 2 * STATE

    def columns(values, start, width, axis=1):
        return lax.dynamic_slice_in_dim(values, start, width, axis)

    hidden_wide = hidden.astype(F32)
    norm_scale = lax.rsqrt(jnp.mean(hidden_wide * hidden_wide, axis=-1, keepdims=True) + EPS)
    normed = (hidden_wide * norm_scale * norm_gain).astype(BF16)

    turned = in_proj.T
    local = jnp.concatenate(
        [
            columns(turned, block * inner, inner, 0),
            columns(turned, INNER + block * inner, inner, 0),
            turned[2 * INNER : steps_at],
            columns(turned, steps_at + block * heads, heads, 0),
        ],
        0,
    )

    def to_wsh(values):
        return [lay.wsh_shift(values, shift) for shift in range(1, lay.wsh)]

    cut = (inner // 128 + 1) * 128
    keep, away = split_halves(normed, lay)
    came_first, came = join(to_wsh(local[:cut]), lay.other_half(away))
    keep_grad, away_grad = split_halves(cotangent, lay)
    normeds = [team_gather(keep[0], came[0], lay)]
    came_last, came_grad = join(
        to_wsh(after(local[cut:], came_first)), lay.other_half(after(away_grad, came))
    )
    weight = columns_in_place(local, [(0, came_first), (cut, came_last)], lay)
    rows_held = INNER // lay.wsh
    owner = (block * inner) // rows_held
    at_row = jnp.where(owner == lay.wplace, block * inner - owner * rows_held, 0)
    rows_here = after(columns(out_proj, at_row, inner, 0), came_last)
    w_out = jnp.where(owner == lay.wplace, rows_here, jnp.zeros_like(rows_here))
    for shift in range(1, lay.wsh):
        pairs = []
        for place in range(lay.team):
            head_block = (place % 2) * lay.chips + place // 2
            holder = (head_block * inner) // rows_held
            source = place * lay.wsh + holder
            pairs.append((source, place * lay.wsh + (holder + shift) % lay.wsh))
        w_out = w_out + lax.ppermute(rows_here, TEAM + ("wsh",), pairs)
    keep_grad = after(keep_grad, came_last)
    grads = [team_gather(keep_grad[0], came_grad[0], lay)]
    for s in range(1, count):
        normeds.append(team_gather(*after((keep[s], came[s]), came_last), lay))
        grads.append(team_gather(keep_grad[s], came_grad[s], lay))

    taps = jnp.concatenate(
        [columns(conv_weight, block * inner, inner), conv_weight[:, INNER:]], 1
    )
    bias = jnp.concatenate([columns(conv_bias, block * inner, inner, 0), conv_bias[INNER:]], 0)
    shift_own = columns(dt_bias, block * heads, heads, 0)[:, None]
    rate_own = columns(a_log, block * heads, heads, 0)[:, None]
    skip_own = jnp.repeat(columns(d_skip, block * heads, heads, 0), HEADDIM)[None]
    gain_own = columns(gate_gain, block * inner, inner, 0)[None]
    params = (taps, bias[None], shift_own, rate_own, skip_own)
    table = jnp.stack([lay.core] + [lay.chip ^ d for d in range(lay.chips)]).astype(jnp.int32)

    kernel = conv_weight.shape[0]
    shapes = [norm_gain.shape, conv_weight.shape, conv_bias.shape]
    shapes += [dt_bias.shape, a_log.shape, d_skip.shape, gate_gain.shape]

    def placed(values, width):
        full = jnp.zeros(values.shape[:-1] + (width,), F32)
        return lax.dynamic_update_slice_in_dim(
            full, values, block * values.shape[-1], values.ndim - 1
        )

    def pack_small(norm_gain1):
        d_taps, d_skip_wide, d_head = jax.tree.map(lambda *v: sum(v[1:], v[0]), *small_scan)
        small = [
            (norm_gain0 + norm_gain1)[0] / norm_gain,
            jnp.concatenate([placed(d_taps[:kernel, :inner], INNER), d_taps[:kernel, inner:]], 1),
            jnp.concatenate([placed(d_taps[kernel, :inner], INNER), d_taps[kernel, inner:]], 0),
            placed(d_head[1, :, 0], dt_bias.shape[0]),
            placed(d_head[0, :, 0], a_log.shape[0]),
            placed(d_skip_wide.reshape(heads, HEADDIM).sum(1), d_skip.shape[0]),
            placed((gain0 + gain1)[0], INNER),
        ]
        return jnp.concatenate([s.reshape(-1) for s in small])

    def unpack_small(packed):
        summed, at = [], 0
        for shape in shapes:
            size = 1
            for extent in shape:
                size *= extent
            summed.append(packed[at : at + size].reshape(shape))
            at += size
        return summed

    team = lay.team
    natural = (2, team, tokens)
    out_rows = INNER // (lay.parts * lay.wsh)
    in_rows = model // (lay.parts * lay.wsh)
    run = Order()

    gates, raws, turned_normed = [], [], []
    mixed, starts, edges, downs = [], [], [], []
    turned_gated, d_gates, d_raws, small_scan = [], [], [], []

    def project_step(at):
        gate, raw, flat = run(lambda v: project_tokens(v, weight, inner), normeds[at])
        gates.append(gate)
        raws.append(raw.reshape(1, length, raw.shape[-1]))
        turned_normed.append(flat)

    def forward_step(at):
        got = run(lambda p: scan_forward(raws[at], 0, p, *params[1:]), params[0])
        mixed.append(got[0].reshape(natural + (inner,)))
        starts.append(got[1])
        edges.append(got[2])

    def stats_step(at):
        down, own = run(lambda m: gate_stats(grads[at], w_out, m, gates[at], gain_own), mixed[at])
        downs.append(down)
        return own

    def back_step(at, sums):
        flat, d_mixed, d_gate, keep, send, gain = run(
            lambda v: gate_back(table, mixed[at], gates[at], downs[at], v, gain_own, w_out), sums
        )
        turned_gated.append(flat[None])
        d_gates.append(d_gate)
        return d_mixed, keep, send, gain

    def scan_step(at, d_mixed):
        d_raw, *small = run(
            lambda d: scan_backward(
                raws[at], 0, d.reshape(1, length, inner), starts[at], edges[at], *params
            ),
            d_mixed,
        )
        d_raws.append(d_raw[0])
        small_scan.append(small)

    def norm_step(at):
        return run(
            lambda v: norm_part(
                table, d_gates[at], v.reshape(natural + (v.shape[-1],)), normeds[at], weight
            ),
            d_raws[at],
        )

    def owned_parts(part):
        blocks = part.reshape(lay.parts, lay.wsh, in_rows, part.shape[1])
        kept = pick(blocks, lay.wplace, 1)
        away = [pick(blocks, (lay.wplace + d) % lay.wsh, 1) for d in range(1, lay.wsh)]
        return kept, [lay.wsh_shift(a, d + 1) for d, a in enumerate(away)]

    def to_owners(kept):
        return lax.all_to_all(kept, ALL, split_axis=0, concat_axis=0, tiled=True)

    def add_owned(kept, came):
        total = kept.astype(F32)
        for part in came:
            total = total + part.astype(F32)
        return total.astype(BF16)

    def chip_step(keep, came):
        return run(lambda v: chip_parts(core_sum(keep, v), lay), came)

    def finish(parts):
        mine, away = run(lambda v: chip_sum([v] + parts[1:], lay), parts[0])
        return mine, lay.other_half(away)

    project_step(0)
    forward_step(0)
    parts = run(lambda v: team_parts(v, lay), stats_step(0))
    sums = run(add_all, parts)
    d_mixed0, out_keep0, send, gain0 = back_step(0, sums)
    out_came0 = lay.other_core(send)
    scan_step(0, d_mixed0)
    out_parts0 = chip_step(out_keep0, out_came0)
    project_step(1)
    forward_step(1)
    own = stats_step(1)
    sum0 = finish(out_parts0)
    parts = run(lambda v: team_parts(v, lay), own)
    scan_base = run(lambda v: row_grad([(turned_normed[0], v)], F32), d_raws[0])
    keep0, send, norm_gain0 = norm_step(0)
    came0 = lay.other_core(send)
    parts, sum0 = join(parts, sum0)
    sums = run(add_all, parts)
    d_mixed1, out_keep1, send, gain1 = back_step(1, sums)
    norm_parts0 = chip_step(keep0, came0)
    out_came1 = lay.other_core(send)
    flat_gates = [d.reshape(length, inner) for d in d_gates]
    gate_grad = run(
        lambda v: row_grad([(turned_normed[0], v), (turned_normed[1], flat_gates[1])], BF16),
        flat_gates[0],
    )
    out_parts1 = chip_step(out_keep1, out_came1)
    gate_kept, gate_came = run(owned_parts, gate_grad)
    flat_grads = [g.reshape(length, model) for g in grads]
    out_grad = run(
        lambda v: row_grad([(v, flat_grads[0]), (turned_gated[1], flat_grads[1])], BF16),
        turned_gated[0],
    )
    blocks = out_grad.reshape(2, lay.wsh, out_rows, model)

    def out_split(values):
        kept = pick(values, lay.wplace, 1)
        away = [pick(values, (lay.wplace + d) % lay.wsh, 1) for d in range(1, lay.wsh)]
        return kept, [lay.wsh_shift(a, d + 1) for d, a in enumerate(away)]

    out_kept, out_came = run(out_split, blocks)
    scan_step(1, d_mixed1)
    norm_parts0, out_parts1, gate_came, out_came, run.last = join(
        norm_parts0, out_parts1, gate_came, out_came, run.last
    )
    norm0 = finish(norm_parts0)
    gate_kept = run(add_owned, gate_kept, gate_came)
    out_kept = run(add_owned, out_kept, out_came)
    cross, first_pairs, second_pairs = [], [], []
    for half in range(2):
        for chip in range(lay.chips):
            source = (half * lay.chips + chip) * 2 + half
            peer = ((1 - half) * lay.chips + chip) * 2 + half
            head_block = half * lay.chips + chip
            cross.append((peer, source))
            first_pairs.append((source, 2 * head_block))
            second_pairs.append((source, 2 * head_block + 1))
    out_came = lax.ppermute(out_kept, ALL, cross)
    sum1 = finish(out_parts1)
    keep1, send, norm_gain1 = norm_step(1)
    came1 = lay.other_core(send)
    scan_grad = run(lambda v: row_grad([(turned_normed[1], v)], BF16, None, scan_base), d_raws[1])
    scan_kept, scan_came = run(owned_parts, scan_grad)
    norm_parts1 = chip_step(keep1, came1)
    by_gate = to_owners(gate_kept)
    small = run(lambda v: pack_small(v), norm_gain1)
    small = run(lambda v: v + lay.other_core(v), small)
    small = [small] + [lay.chip_flip(small, b) for b in range(1, lay.chips)]
    scan_came, norm_parts1, by_gate, small, out_came, norm0, sum1, run.last = join(
        scan_came, norm_parts1, by_gate, small, out_came, norm0, sum1, run.last
    )
    scan_kept = run(add_owned, scan_kept, scan_came)
    by_scan = to_owners(scan_kept)
    norm1 = finish(norm_parts1)
    small = run(add_all, small)
    out_held = run(lambda v: (v.astype(F32) + out_came.astype(F32)).astype(BF16), out_kept)
    out_first = lax.ppermute(out_held[0], ALL, first_pairs)
    out_second = lax.ppermute(out_held[1], ALL, second_pairs)
    small = run(lambda v: v + lay.other_half(v), small)
    bit = 1
    while bit < lay.wsh:
        small = run(
            lambda v: v + lax.ppermute(v, "wsh", [(i, i ^ bit) for i in range(lay.wsh)]), small
        )
        bit *= 2
    out_proj_grad = run(lambda v: v.astype(F32) + out_second.astype(F32), out_first)

    def whole_place(first, second):
        mine = jnp.stack([first[0], second[0]], 0)
        other = jnp.stack([first[1], second[1]], 0)
        return both_halves(mine, other, lay)

    block_out = run(
        lambda v: (hidden_wide + whole_place((v, sum0[1]), sum1).astype(F32)).astype(BF16), sum0[0]
    )

    def hidden_step(value):
        d_scaled = whole_place((value, norm0[1]), norm1).astype(F32) * norm_gain
        inward = jnp.mean(d_scaled * hidden_wide, axis=-1, keepdims=True)
        return (
            cotangent.astype(F32)
            + norm_scale * d_scaled
            - hidden_wide * (norm_scale * norm_scale * norm_scale * inward)
        )

    hidden_grad = run(hidden_step, norm0[0])

    def assemble(scan_parts):
        def owned(parts):
            view = parts.reshape(2, team, in_rows, parts.shape[-1])
            return jnp.sum(view.astype(F32), axis=0)

        by_block = [(b % lay.chips) * 2 + b // lay.chips for b in range(team)]
        scan_sums = owned(scan_parts)
        gate_sums = owned(by_gate)
        bc_sum = jnp.sum(scan_sums[:, :, inner : inner + 2 * STATE], axis=0)
        return jnp.concatenate(
            [gate_sums[m] for m in by_block]
            + [scan_sums[m, :, :inner] for m in by_block]
            + [bc_sum]
            + [scan_sums[m, :, inner + 2 * STATE :] for m in by_block],
            1,
        )

    in_proj_grad = run(assemble, by_scan)
    ngain_all, conv_all, cbias_all, shift_all, rate_all, skip_all, ggain_all = unpack_small(small)
    return (
        block_out,
        hidden_grad,
        ngain_all,
        in_proj_grad,
        conv_all,
        cbias_all,
        shift_all,
        rate_all,
        skip_all,
        ggain_all,
        out_proj_grad,
    )


def solution(mesh):
    parts, wsh = mesh.devices.shape
    fine = Mesh(mesh.devices.reshape(2, parts // 4, 2, wsh), ("half", "chip", "core", "wsh"))
    by_token = P("wsh", ALL, None)
    by_row = P("wsh", None)
    owned = P(ALL + ("wsh",), None)
    whole = P()
    return jax.shard_map(
        shards,
        mesh=fine,
        in_specs=(by_token, by_token, whole, by_row) + (whole,) * 6 + (by_row,),
        out_specs=(by_token, by_token, whole, owned) + (whole,) * 6 + (owned,),
        check_vma=False,
    )
```

time: 2480 us -> 569 us (0.23)
  waiting for transfers between devices: 846 us -> 208 us
  matrix products: 622 us -> 0 us
  other arithmetic: 326 us -> 41.8 us
  blocking collectives: 245 us -> 0 us
  local copies, waits for them, and re-layouts: 289 us -> 87.8 us
  Pallas kernels: 0 us -> 137 us
  starting transfers between devices: 116 us -> 70.6 us
    dot_general x216 -> x0, matrix products: 596 us -> none  [the longest x8 141 us: contract_rows(): lax.dot_general(left, right, (((0,), (0,)), ((), ())), preferred_element_...]
    all_gather x10 -> x4, waiting for transfers between devices: 460 us -> 0.01 us  [team_gather(): return lax.all_gather(pair, TEAM, axis=0)]
    ppermute x0 -> x45, waiting for transfers between devices: none -> 208 us  [the longest x7 127 us: other_half(): return lax.ppermute(values, 'half', [(0, 1), (1, 0)])]
    all_gather x12 -> x0, blocking collectives: 182 us -> none  [the longest x4 86.9 us: shards(): lax.all_gather(proj_low[:, 2 * INNER:2 * INNER + 2 * STATE], 'seq', axis=...]
    reduce_scatter x6 -> x0, waiting for transfers between devices: 170 us -> none  [the longest x4 87.4 us: shards(): lax.psum_scatter(d_bc.astype(jnp.bfloat16), 'seq', scatter_dimension=0, t...]
    another operation x188 -> x0, other arithmetic: 170 us -> none
    pallas_call x0 -> x16, Pallas kernels: none -> 137 us  [the longest x2 41.2 us: scan_backward(): pl.pallas_call(functools.partial(scan_backward_body, heads), grid=(seqs,...]
    psum x1 -> x0, waiting for transfers between devices: 120 us -> none  [shards(): lax.psum((ngain_sum, conv_sum, cbias_sum, shift_sum, rate_sum, skip_sum,...]
  transfers between devices with their start and end apart: 40 -> 51, of which waited for: 21 -> 24; matrix products, arithmetic and copies ran while one was open for 36% -> 10% of each run, Pallas kernels for 0% -> 20%
where the time goes in v1:
time: 569 us; the launch traced here: 560 us
  waiting for transfers between devices  208 us (37%)
  Pallas kernels  137 us (24%)
  local copies, waits for them, and re-layouts  87.8 us (15%)
  starting transfers between devices  70.6 us (12%)
  other arithmetic  41.8 us (7%)
  between operations  15.4 us (3%)
    ppermute x7, waiting for transfers between devices, other_half(): return lax.ppermute(values, 'half', [(0, 1), (1, 0)])  127 us
    unnamed x170, local copies, waits for them, and re-layouts  54.3 us
    pallas_call x2, Pallas kernels, scan_backward(): pl.pallas_call(functools.partial(scan_backward_body, heads), grid=(seqs,...  41.2 us
    ppermute x21, waiting for transfers between devices, chip_flip(): lax.ppermute(values, 'chip', [(i, i ^ bits) for i in range(self.chips)])  37.4 us
    ppermute x5, waiting for transfers between devices, wsh_shift(): lax.ppermute(values, 'wsh', [(i, (i + shift) % size) for i in range(size)])  22.9 us
    pallas_call x4, Pallas kernels, row_grad(): pl.pallas_call(functools.partial(row_grad_body, len(operands), cols, base...  21.3 us
    ppermute x21, starting transfers between devices, chip_flip(): lax.ppermute(values, 'chip', [(i, i ^ bits) for i in range(self.chips)])  19.7 us
    pallas_call x2, Pallas kernels, norm_part(): pl.pallas_call(norm_part_body, grid_spec=pltpu.PrefetchScalarGridSpec(num...  18.3 us
  transfers between devices with their start and end apart: 51, of which 24 were waited for; matrix products, arithmetic and copies ran while one was open for 10% of the time, Pallas kernels for 20%

profile of v1, /device:TPU:0, one launch (start us, length us, event | category | flops | bytes accessed | tf_op | source)
XLA Modules:
  0.0 560.1 jit_solution(14305354893195490204)
XLA Ops:
  19.5 21.9 %collective-permute-done.1 = bf16[2,64,2048]{2,1,0:T(8,128)(2,1)S(1)} collective-permute-done((bf16[2,64,2048]{2,1,0:T(8,128)(2,1)S(1)}, bf16[2,64,2048]{2,1,0:T(8,128)(2,1)S(1)}, u32[]{:S(2)}, u32[]{:S(2)}) %collective-permute-start.1) | collective-permute-done | bytes 524320 | tf_op jit(solution)/shard_map/ppermute | solution.py:695
  50.4 22.1 %collective-permute-done.3 = bf16[2,64,2048]{2,1,0:T(8,128)(2,1)S(1)} collective-permute-done((bf16[2,64,2048]{2,1,0:T(8,128)(2,1)S(1)}, bf16[2,64,2048]{2,1,0:T(8,128)(2,1)S(1)}, u32[]{:S(2)}, u32[]{:S(2)}) %collective-permute-start.3) | collective-permute-done | bytes 524320 | tf_op jit(solution)/shard_map/ppermute | solution.py:695
  72.5 3.7 collective-permute-done.2
  84.7 4.7 collective-permute-start.4
  96.3 15.6 %collective-permute-done.4 = bf16[512,2048]{1,0:T(8,128)(2,1)} collective-permute-done((bf16[512,2048]{1,0:T(8,128)(2,1)}, bf16[512,2048]{1,0:T(8,128)(2,1)}, u32[]{:S(2)}, u32[]{:S(2)}) %collective-permute-start.4) | collective-permute-done | bytes 2097184 | tf_op jit(solution)/shard_map/ppermute | solution.py:837
  116.6 8.2 %project_tokens.2 = (bf16[2,8,64,512]{3,2,1,0:T(8,128)(2,1)S(1)}, bf16[2,8,64,776]{3,2,1,0:T(8,128)(2,1)S(1)}, bf16[2,2048,512]{2,1,0:T(8,128)(2,1)S(1)}) custom-call(bf16[8,2,64,2048]{3,2,1,0:T(8,128)(2,1)S(1)} %copy-done.14, bf16[1288,2048]{1,0:T(8,128)(2,1)S(1)} %copy-done.1), custom_call_target="tpu_custom_call" | custom-call | flops 8 | bytes 8 | tf_op jit(solution)/shard_map/project_tokens/pallas_call | solution.py:390
  126.7 9.1 %scan_forward.2 = (bf16[1,1024,512]{2,1,0:T(8,128)(2,1)S(1)}, f32[1,4,128,512]{3,2,1,0:T(8,128)S(1)}, f32[1,4,8,768]{3,2,1,0:T(8,128)S(1)}) custom-call(bf16[1,1024,776]{2,1,0:T(8,128)(2,1)S(1)} %bitcast.194, f32[4,768]{1,0:T(4,128)S(1)} %pad_maximum_fusion.9.taps_ref, f32[1,768]{1,0:T(1,128)S(1)} %broadcast_in_dim.36.bias_ref, f32[8,1]{1,0:T(8,128)S(1)} %copy.38.shift_ref, ...), custom_call_target="tpu_custom_call" | custom-call | flops 1024 | bytes 1024 | tf_op jit(solution)/shard_map/scan_forward/pallas_call | solution.py:162
  142.5 3.9 gate_stats.2
  160.7 6.3 %gate_back.2 = (bf16[512,1024]{1,0:T(8,128)(2,1)S(1)}, bf16[2,8,64,512]{3,2,1,0:T(8,128)(2,1)S(1)}, bf16[2,8,64,512]{3,2,1,0:T(8,128)(2,1)S(1)}, bf16[4,2,64,204...) custom-call(s32[5]{0:T(128)S(1)} %stack.109.table_ref, ...), custom_call_target="tpu_custom_call" | custom-call | flops 8 | bytes 8 | tf_op jit(solution)/shard_map/gate_back/pallas_call | solution.py:526
  167.2 20.8 %scan_backward.2 = (bf16[1,1024,776]{2,1,0:T(8,128)(2,1)S(1)}, f32[8,768]{1,0:T(8,128)S(1)}, f32[1,512]{1,0:T(1,128)S(1)}, f32[2,8,1]{2,1,0:T(8,128)S(1)}) custom-call(bf16[1,1024,776]{2,1,0:T(8,128)(2,1)S(1)} %bitcast.195, bf16[1,1024,512]{2,1,0:T(8,128)(2,1)S(1)} %bitcast.205, f32[1,4,128,512]{3,2,1,0:T(8,128)S(1)} %copy-done.54, ...), custom_call_target="tpu_custom_call" | custom-call | flops 1024 | bytes 1024 | tf_op jit(solution)/shard_map/scan_backward/pallas_call | solution.py:328
  198.7 8.2 %project_tokens.3 = (bf16[2,8,64,512]{3,2,1,0:T(8,128)(2,1)S(1)}, bf16[2,8,64,776]{3,2,1,0:T(8,128)(2,1)S(1)}, bf16[2,2048,512]{2,1,0:T(8,128)(2,1)S(1)}) custom-call(bf16[8,2,64,2048]{3,2,1,0:T(8,128)(2,1)S(1)} %copy-done.12, bf16[1288,2048]{1,0:T(8,128)(2,1)S(1)} %copy-done.2), custom_call_target="tpu_custom_call" | custom-call | flops 8 | bytes 8 | tf_op jit(solution)/shard_map/project_tokens/pallas_call | solution.py:390
  209.0 9.1 %scan_forward.3 = (bf16[1,1024,512]{2,1,0:T(8,128)(2,1)S(1)}, f32[1,4,128,512]{3,2,1,0:T(8,128)S(1)}, f32[1,4,8,768]{3,2,1,0:T(8,128)S(1)}) custom-call(bf16[1,1024,776]{2,1,0:T(8,128)(2,1)S(1)} %bitcast.192, f32[4,768]{1,0:T(4,128)S(1)} %pad_maximum_fusion.9.taps_ref, f32[1,768]{1,0:T(1,128)S(1)} %broadcast_in_dim.36.bias_ref, f32[8,1]{1,0:T(8,128)S(1)} %copy.38.shift_ref, ...), custom_call_target="tpu_custom_call" | custom-call | flops 1024 | bytes 1024 | tf_op jit(solution)/shard_map/scan_forward/pallas_call | solution.py:162
  225.9 3.9 gate_stats.3
  233.7 5.5 row_grad.4.refs_2_
  239.2 9.2 %norm_part.2 = (bf16[4,2,64,2048]{3,2,1,0:T(8,128)(2,1)S(1)}, bf16[4,2,64,2048]{3,2,1,0:T(8,128)(2,1)}, f32[1,2048]{1,0:T(1,128)S(1)}) custom-call(s32[5]{0:T(128)S(1)} %stack.109.table_ref, bf16[2,8,64,512]{3,2,1,0:T(8,128)(2,1)S(1)} %get-tuple-element.182.d_gate_ref, bf16[2,8,64,776]{3,2,1,0:T(8,128)(2,1)S(1)} %bitcast.191, ...), custom_call_target="tpu_custom_call" | custom-call | flops 4 | bytes 4 | tf_op jit(solution)/shard_map/norm_part/pallas_call | solution.py:637
  259.1 5.9 %collective-permute-done.17 = bf16[64,2048]{1,0:T(8,128)(2,1)S(1)} collective-permute-done((bf16[64,2048]{1,0:T(8,128)(2,1)S(1)}, bf16[64,2048]{1,0:T(8,128)(2,1)S(1)}, u32[]{:S(2)}, u32[]{:S(2)}) %collective-permute-start.17) | collective-permute-done | bytes 262176 | tf_op jit(solution)/shard_map/ppermute | solution.py:695
  267.6 7.2 %gate_back.3 = (bf16[512,1024]{1,0:T(8,128)(2,1)S(1)}, bf16[2,8,64,512]{3,2,1,0:T(8,128)(2,1)S(1)}, bf16[2,8,64,512]{3,2,1,0:T(8,128)(2,1)S(1)}, bf16[4,2,64,204...) custom-call(s32[5]{0:T(128)S(1)} %stack.109.table_ref, ...), custom_call_target="tpu_custom_call" | custom-call | flops 8 | bytes 8 | tf_op jit(solution)/shard_map/gate_back/pallas_call | solution.py:526
  286.0 5.6 row_grad.5
  297.8 4.7 row_grad.6
  305.5 4.5 collective-permute-done.22
  310.0 20.5 %scan_backward.3 = (bf16[1,1024,776]{2,1,0:T(8,128)(2,1)S(1)}, f32[8,768]{1,0:T(8,128)S(1)}, f32[1,512]{1,0:T(1,128)S(1)}, f32[2,8,1]{2,1,0:T(8,128)S(1)}) custom-call(bf16[1,1024,776]{2,1,0:T(8,128)(2,1)S(1)} %bitcast.193, bf16[1,1024,512]{2,1,0:T(8,128)(2,1)S(1)} %bitcast.203, f32[1,4,128,512]{3,2,1,0:T(8,128)S(1)} %copy-done.48, ...), custom_call_target="tpu_custom_call" | custom-call | flops 1024 | bytes 1024 | tf_op jit(solution)/shard_map/scan_backward/pallas_call | solution.py:328
  331.7 18.3 %collective-permute-done.27 = bf16[2,128,2048]{2,1,0:T(8,128)(2,1)S(1)} collective-permute-done((bf16[2,128,2048]{2,1,0:T(8,128)(2,1)S(1)}, bf16[2,128,2048]{2,1,0:T(8,128)(2,1)S(1)}, u32[]{:S(2)}, u32[]{:S(2)}) %collective-permute-start.27) | collective-permute-done | bytes 1048608 | tf_op jit(solution)/shard_map/ppermute | solution.py:702
  355.3 9.1 %norm_part.3 = (bf16[4,2,64,2048]{3,2,1,0:T(8,128)(2,1)S(1)}, bf16[4,2,64,2048]{3,2,1,0:T(8,128)(2,1)}, f32[1,2048]{1,0:T(1,128)S(1)}) custom-call(s32[5]{0:T(128)S(1)} %stack.109.table_ref, bf16[2,8,64,512]{3,2,1,0:T(8,128)(2,1)S(1)} %copy-done.26, bf16[2,8,64,776]{3,2,1,0:T(8,128)(2,1)S(1)} %bitcast.188, bf16[8,2,64,2048]{3,2,1,0:T(8,128)(2,1)S(1)} %copy-done.13, ...), custom_call_target="tpu_custom_call" | custom-call | flops 4 | bytes 4 | tf_op jit(solution)/shard_map/norm_part/pallas_call | solution.py:637
  366.2 4.4 all-to-all-start
  378.4 5.6 row_grad.7
  387.2 4.5 collective-permute-start.38
  397.5 41.7 %collective-permute-done.38 = bf16[64,2048]{1,0:T(8,128)(2,1)} collective-permute-done((bf16[64,2048]{1,0:T(8,128)(2,1)}, bf16[64,2048]{1,0:T(8,128)(2,1)}, u32[]{:S(2)}, u32[]{:S(2)}) %collective-permute-start.38) | collective-permute-done | bytes 262176 | tf_op jit(solution)/shard_map/ppermute | solution.py:695
  445.6 6.3 %collective-permute-done.34 = f32[28096]{0:T(1024)S(1)} collective-permute-done((f32[28096]{0:T(1024)S(1)}, f32[28096]{0:T(1024)S(1)}, u32[]{:S(2)}, u32[]{:S(2)}) %collective-permute-start.34) | collective-permute-done | bytes 112416 | tf_op jit(solution)/shard_map/ppermute | solution.py:698
  452.0 16.2 %collective-permute-done.35 = f32[28096]{0:T(1024)} collective-permute-done((f32[28096]{0:T(1024)S(1)}, f32[28096]{0:T(1024)}, u32[]{:S(2)}, u32[]{:S(2)}) %collective-permute-start.35) | collective-permute-done | bytes 112416 | tf_op jit(solution)/shard_map/ppermute | solution.py:698
  476.1 5.4 collective-permute-start.40
  484.8 5.5 all-to-all-start.1
  511.0 34.1 %collective-permute-done.44 = bf16[64,2048]{1,0:T(8,128)(2,1)} collective-permute-done((bf16[64,2048]{1,0:T(8,128)(2,1)}, bf16[64,2048]{1,0:T(8,128)(2,1)}, u32[]{:S(2)}, u32[]{:S(2)}) %collective-permute-start.44) | collective-permute-done | bytes 262176 | tf_op jit(solution)/shard_map/ppermute | solution.py:695
  (381 shorter events, 193.2 us)
Async XLA Ops:
  7.2 89.1 %all-gather.9.cloned.1.call-start = ((), (), s32[]{:S(2)}) async-start(), calls=%async_computation.4 | async-start | bytes 4718592 | tf_op jit(solution)/shard_map/all_gather | solution.py:718
  10.1 32.0 %collective-permute-start = (bf16[640,1024]{1,0:T(8,128)(2,1)}, bf16[640,1024]{1,0:T(8,128)(2,1)}, u32[]{:S(2)}, u32[]{:S(2)}) collective-permute-start(bf16[640,1024]{1,0:T(8,128)(2,1)} %pad_maximum_fusion.2), channel_id=1, source_target_pairs={{0,1},{1,0},{2,3},{3,2},{4,5},{5,4},{6,7},{7,6},{8,9},{9,8},{10,11... | collective-permute-start | bytes 3932168 | tf_op jit(solution)/shard_map/ppermute | solution.py:702
  15.7 25.6 %collective-permute-start.1 = (bf16[2,64,2048]{2,1,0:T(8,128)(2,1)S(1)}, bf16[2,64,2048]{2,1,0:T(8,128)(2,1)S(1)}, u32[]{:S(2)}, u32[]{:S(2)}) collective-permute-start(bf16[2,64,2048]{2,1,0:T(8,128)(2,1)S(1)} %constant_dynamic-slice_fusion.4), channel_id=1, source_target_pairs={{0,16},{16,0},{1,17},{17,1},{2,18},{18,2},{3,19},{19,3},{4,20},{20... | collective-permute-start | bytes 1572872 | tf_op jit(solution)/shard_map/ppermute | solution.py:695
  43.8 95.2 %all-gather.11.cloned.1.call-start = ((), (), s32[]{:S(2)}) async-start(), calls=%async_computation.5 | async-start | bytes 4718592 | tf_op jit(solution)/shard_map/all_gather | solution.py:718
  45.8 30.4 %collective-permute-start.2 = (bf16[648,1024]{1,0:T(8,128)(2,1)S(1)}, bf16[648,1024]{1,0:T(8,128)(2,1)S(1)}, u32[]{:S(2)}, u32[]{:S(2)}) collective-permute-start(bf16[648,1024]{1,0:T(8,128)(2,1)S(1)} %pad_maximum_fusion), channel_id=1, source_target_pairs={{0,1},{1,0},{2,3},{3,2},{4,5},{5,4},{6,7},{7,6},{8,9},{9,8},{10,11... | collective-permute-start | bytes 3981320 | tf_op jit(solution)/shard_map/ppermute | solution.py:702
  47.7 24.8 %collective-permute-start.3 = (bf16[2,64,2048]{2,1,0:T(8,128)(2,1)S(1)}, bf16[2,64,2048]{2,1,0:T(8,128)(2,1)S(1)}, u32[]{:S(2)}, u32[]{:S(2)}) collective-permute-start(bf16[2,64,2048]{2,1,0:T(8,128)(2,1)S(1)} %get-tuple-element.142), channel_id=1, source_target_pairs={{0,16},{16,0},{1,17},{17,1},{2,18},{18,2},{3,19},{19,3},{4,20},{20... | collective-permute-start | bytes 1572872 | tf_op jit(solution)/shard_map/ppermute | solution.py:695
  78.4 115.7 %all-gather.7.cloned.1.call-start = ((), (), s32[]{:S(2)}) async-start(), calls=%async_computation.3 | async-start | bytes 4718592 | tf_op jit(solution)/shard_map/all_gather | solution.py:718
  80.4 140.9 %all-gather.5.cloned.1.call-start = ((), (), s32[]{:S(2)}) async-start(), calls=%async_computation.2 | async-start | bytes 4718592 | tf_op jit(solution)/shard_map/all_gather | solution.py:718
  84.7 27.1 %collective-permute-start.4 = (bf16[512,2048]{1,0:T(8,128)(2,1)}, bf16[512,2048]{1,0:T(8,128)(2,1)}, u32[]{:S(2)}, u32[]{:S(2)}) collective-permute-start(bf16[512,2048]{1,0:T(8,128)(2,1)} %constant_dynamic-slice_fusion.2), channel_id=1, source_target_pairs={{0,1},{3,2},{4,5},{7,6},{8,9},{11,10},{12,13},{15,14},{16,17},{19,... | collective-permute-start | bytes 6291464 | tf_op jit(solution)/shard_map/ppermute | solution.py:837
  190.6 39.3 %collective-permute-start.12 = (bf16[2,64,2048]{2,1,0:T(8,128)(2,1)}, bf16[2,64,2048]{2,1,0:T(8,128)(2,1)}, u32[]{:S(2)}, u32[]{:S(2)}) collective-permute-start(bf16[2,64,2048]{2,1,0:T(8,128)(2,1)} %get-tuple-element.290), channel_id=1, source_target_pairs={{0,12},{4,8},{8,4},{12,0},{1,13},{5,9},{9,5},{13,1},{2,14},{6,10},... | collective-permute-start | bytes 1572872 | tf_op jit(solution)/shard_map/ppermute | solution.py:698
  191.0 38.8 %collective-permute-start.11 = (bf16[2,64,2048]{2,1,0:T(8,128)(2,1)}, bf16[2,64,2048]{2,1,0:T(8,128)(2,1)}, u32[]{:S(2)}, u32[]{:S(2)}) collective-permute-start(bf16[2,64,2048]{2,1,0:T(8,128)(2,1)} %get-tuple-element.291), channel_id=1, source_target_pairs={{0,8},{4,12},{8,0},{12,4},{1,9},{5,13},{9,1},{13,5},{2,10},{6,14},... | collective-permute-start | bytes 1572872 | tf_op jit(solution)/shard_map/ppermute | solution.py:698
  192.7 37.2 %collective-permute-start.10 = (bf16[2,64,2048]{2,1,0:T(8,128)(2,1)}, bf16[2,64,2048]{2,1,0:T(8,128)(2,1)}, u32[]{:S(2)}, u32[]{:S(2)}) collective-permute-start(bf16[2,64,2048]{2,1,0:T(8,128)(2,1)} %get-tuple-element.289), channel_id=1, source_target_pairs={{0,4},{4,0},{8,12},{12,8},{1,5},{5,1},{9,13},{13,9},{2,6},{6,2},{1... | collective-permute-start | bytes 1572872 | tf_op jit(solution)/shard_map/ppermute | solution.py:698
  249.7 29.4 %collective-permute-start.18 = (bf16[4,2,64,2048]{3,2,1,0:T(8,128)(2,1)}, bf16[4,2,64,2048]{3,2,1,0:T(8,128)(2,1)}, u32[]{:S(2)}, u32[]{:S(2)}) collective-permute-start(bf16[4,2,64,2048]{3,2,1,0:T(8,128)(2,1)} %get-tuple-element.186), channel_id=1, source_target_pairs={{0,2},{2,0},{1,3},{3,1},{4,6},{6,4},{5,7},{7,5},{8,10},{10,8},{9,1... | collective-permute-start | bytes 6291464 | tf_op jit(solution)/shard_map/ppermute | solution.py:692
  282.9 27.1 %collective-permute-start.22 = (bf16[2,64,2048]{2,1,0:T(8,128)(2,1)S(1)}, bf16[2,64,2048]{2,1,0:T(8,128)(2,1)S(1)}, u32[]{:S(2)}, u32[]{:S(2)}) collective-permute-start(bf16[2,64,2048]{2,1,0:T(8,128)(2,1)S(1)} %get-tuple-element.285), channel_id=1, source_target_pairs={{0,12},{4,8},{8,4},{12,0},{1,13},{5,9},{9,5},{13,1},{2,14},{6,10},... | collective-permute-start | bytes 1572872 | tf_op jit(solution)/shard_map/ppermute | solution.py:698
  302.8 28.9 %collective-permute-start.26 = (bf16[16,64,512]{2,1,0:T(8,128)(2,1)S(1)}, bf16[16,64,512]{2,1,0:T(8,128)(2,1)S(1)}, u32[]{:S(2)}, u32[]{:S(2)}) collective-permute-start(bf16[16,64,512]{2,1,0:T(8,128)(2,1)S(1)} %get-tuple-element.279), channel_id=1, source_target_pairs={{0,1},{1,0},{2,3},{3,2},{4,5},{5,4},{6,7},{7,6},{8,9},{9,8},{10,11... | collective-permute-start | bytes 3145736 | tf_op jit(solution)/shard_map/ppermute | solution.py:702
  304.5 45.5 %collective-permute-start.27 = (bf16[2,128,2048]{2,1,0:T(8,128)(2,1)S(1)}, bf16[2,128,2048]{2,1,0:T(8,128)(2,1)S(1)}, u32[]{:S(2)}, u32[]{:S(2)}) collective-permute-start(bf16[2,128,2048]{2,1,0:T(8,128)(2,1)S(1)} %get-tuple-element.277), channel_id=1, source_target_pairs={{0,1},{1,0},{2,3},{3,2},{4,5},{5,4},{6,7},{7,6},{8,9},{9,8},{10,11... | collective-permute-start | bytes 3145736 | tf_op jit(solution)/shard_map/ppermute | solution.py:702
  304.9 25.6 %collective-permute-start.23 = (bf16[2,64,2048]{2,1,0:T(8,128)(2,1)S(1)}, bf16[2,64,2048]{2,1,0:T(8,128)(2,1)S(1)}, u32[]{:S(2)}, u32[]{:S(2)}) collective-permute-start(bf16[2,64,2048]{2,1,0:T(8,128)(2,1)S(1)} %get-tuple-element.283), channel_id=1, source_target_pairs={{0,4},{4,0},{8,12},{12,8},{1,5},{5,1},{9,13},{13,9},{2,6},{6,2},{1... | collective-permute-start | bytes 1572872 | tf_op jit(solution)/shard_map/ppermute | solution.py:698
  305.3 25.3 %collective-permute-start.24 = (bf16[2,64,2048]{2,1,0:T(8,128)(2,1)S(1)}, bf16[2,64,2048]{2,1,0:T(8,128)(2,1)S(1)}, u32[]{:S(2)}, u32[]{:S(2)}) collective-permute-start(bf16[2,64,2048]{2,1,0:T(8,128)(2,1)S(1)} %get-tuple-element.282), channel_id=1, source_target_pairs={{0,8},{4,12},{8,0},{12,4},{1,9},{5,13},{9,1},{13,5},{2,10},{6,14},... | collective-permute-start | bytes 1572872 | tf_op jit(solution)/shard_map/ppermute | solution.py:698
  365.8 26.0 %collective-permute-start.29 = (bf16[4,2,64,2048]{3,2,1,0:T(8,128)(2,1)}, bf16[4,2,64,2048]{3,2,1,0:T(8,128)(2,1)}, u32[]{:S(2)}, u32[]{:S(2)}) collective-permute-start(bf16[4,2,64,2048]{3,2,1,0:T(8,128)(2,1)} %get-tuple-element.227), channel_id=1, source_target_pairs={{0,2},{2,0},{1,3},{3,1},{4,6},{6,4},{5,7},{7,5},{8,10},{10,8},{9,1... | collective-permute-start | bytes 6291464 | tf_op jit(solution)/shard_map/ppermute | solution.py:692
  366.2 85.8 %all-to-all-start = ((bf16[16,64,512]{2,1,0:T(8,128)(2,1)}), bf16[16,64,512]{2,1,0:T(8,128)(2,1)}, u32[]{:S(2)}, u32[]{:S(2)}) async-start(bf16[16,64,512]{2,1,0:T(8,128)(2,1)} %add_convert_fusion.7), calls=%async_computation | async-start | bytes 2097152 | tf_op jit(solution)/shard_map/all_to_all | solution.py:948
  371.9 73.1 %collective-permute-start.37 = (bf16[2,128,2048]{2,1,0:T(8,128)(2,1)S(1)}, bf16[2,128,2048]{2,1,0:T(8,128)(2,1)}, u32[]{:S(2)}, u32[]{:S(2)}) collective-permute-start(bf16[2,128,2048]{2,1,0:T(8,128)(2,1)S(1)} %add_convert_fusion.6), channel_id=1, source_target_pairs={{16,0},{20,4},{24,8},{28,12},{2,18},{6,22},{10,26},{14,30},{17,1},... | collective-permute-start | bytes 3145736 | tf_op jit(solution)/shard_map/ppermute | solution.py:1020
  385.6 60.0 %collective-permute-start.28 = (bf16[16,64,776]{2,1,0:T(8,128)(2,1)}, bf16[16,64,776]{2,1,0:T(8,128)(2,1)}, u32[]{:S(2)}, u32[]{:S(2)}) collective-permute-start(bf16[16,64,776]{2,1,0:T(8,128)(2,1)} %get-tuple-element.272), channel_id=1, source_target_pairs={{0,1},{1,0},{2,3},{3,2},{4,5},{5,4},{6,7},{7,6},{8,9},{9,8},{10,11... | collective-permute-start | bytes 4767752 | tf_op jit(solution)/shard_map/ppermute | solution.py:702
  387.2 52.0 %collective-permute-start.38 = (bf16[64,2048]{1,0:T(8,128)(2,1)}, bf16[64,2048]{1,0:T(8,128)(2,1)}, u32[]{:S(2)}, u32[]{:S(2)}) collective-permute-start(bf16[64,2048]{1,0:T(8,128)(2,1)} %get-tuple-element.331), channel_id=1, source_target_pairs={{0,16},{16,0},{1,17},{17,1},{2,18},{18,2},{3,19},{19,3},{4,20},{20... | collective-permute-start | bytes 786440 | tf_op jit(solution)/shard_map/ppermute | solution.py:695
  391.8 50.2 %collective-permute-start.39 = (bf16[64,2048]{1,0:T(8,128)(2,1)}, bf16[64,2048]{1,0:T(8,128)(2,1)}, u32[]{:S(2)}, u32[]{:S(2)}) collective-permute-start(bf16[64,2048]{1,0:T(8,128)(2,1)} %get-tuple-element.329), channel_id=1, source_target_pairs={{0,16},{16,0},{1,17},{17,1},{2,18},{18,2},{3,19},{19,3},{4,20},{20... | collective-permute-start | bytes 786440 | tf_op jit(solution)/shard_map/ppermute | solution.py:695
  395.8 46.2 %collective-permute-start.33 = (f32[28096]{0:T(1024)S(1)}, f32[28096]{0:T(1024)S(1)}, u32[]{:S(2)}, u32[]{:S(2)}) collective-permute-start(f32[28096]{0:T(1024)S(1)} %concatenate.92), channel_id=1, source_target_pairs={{0,2},{2,0},{1,3},{3,1},{4,6},{6,4},{5,7},{7,5},{8,10},{10,8},{9,1... | collective-permute-start | bytes 337160 | tf_op jit(solution)/shard_map/ppermute | solution.py:692
  439.2 31.1 %collective-permute-start.30 = (bf16[2,64,2048]{2,1,0:T(8,128)(2,1)}, bf16[2,64,2048]{2,1,0:T(8,128)(2,1)}, u32[]{:S(2)}, u32[]{:S(2)}) collective-permute-start(bf16[2,64,2048]{2,1,0:T(8,128)(2,1)} %get-tuple-element.275), channel_id=1, source_target_pairs={{0,4},{4,0},{8,12},{12,8},{1,5},{5,1},{9,13},{13,9},{2,6},{6,2},{1... | collective-permute-start | bytes 1572872 | tf_op jit(solution)/shard_map/ppermute | solution.py:698
  442.0 28.3 %collective-permute-start.31 = (bf16[2,64,2048]{2,1,0:T(8,128)(2,1)}, bf16[2,64,2048]{2,1,0:T(8,128)(2,1)}, u32[]{:S(2)}, u32[]{:S(2)}) collective-permute-start(bf16[2,64,2048]{2,1,0:T(8,128)(2,1)} %get-tuple-element.274), channel_id=1, source_target_pairs={{0,8},{4,12},{8,0},{12,4},{1,9},{5,13},{9,1},{13,5},{2,10},{6,14},... | collective-permute-start | bytes 1572872 | tf_op jit(solution)/shard_map/ppermute | solution.py:698
  442.0 28.3 %collective-permute-start.32 = (bf16[2,64,2048]{2,1,0:T(8,128)(2,1)}, bf16[2,64,2048]{2,1,0:T(8,128)(2,1)}, u32[]{:S(2)}, u32[]{:S(2)}) collective-permute-start(bf16[2,64,2048]{2,1,0:T(8,128)(2,1)} %get-tuple-element.273), channel_id=1, source_target_pairs={{0,12},{4,8},{8,4},{12,0},{1,13},{5,9},{9,5},{13,1},{2,14},{6,10},... | collective-permute-start | bytes 1572872 | tf_op jit(solution)/shard_map/ppermute | solution.py:698
  474.0 32.1 %collective-permute-start.43 = (bf16[128,2048]{1,0:T(8,128)(2,1)}, bf16[128,2048]{1,0:T(8,128)(2,1)}, u32[]{:S(2)}, u32[]{:S(2)}) collective-permute-start(bf16[128,2048]{1,0:T(8,128)(2,1)} %get-tuple-element.322), channel_id=1, source_target_pairs={{0,2},{4,6},{8,10},{12,14},{18,18},{22,22},{26,26},{30,30},{1,3},{... | collective-permute-start | bytes 1572872 | tf_op jit(solution)/shard_map/ppermute | solution.py:1040
  476.1 30.0 %collective-permute-start.40 = (bf16[128,2048]{1,0:T(8,128)(2,1)}, bf16[128,2048]{1,0:T(8,128)(2,1)}, u32[]{:S(2)}, u32[]{:S(2)}) collective-permute-start(bf16[128,2048]{1,0:T(8,128)(2,1)} %get-tuple-element.321), channel_id=1, source_target_pairs={{0,0},{4,4},{8,8},{12,12},{18,16},{22,20},{26,24},{30,28},{1,1},{5... | collective-permute-start | bytes 1572872 | tf_op jit(solution)/shard_map/ppermute | solution.py:1039
  484.8 63.9 %all-to-all-start.1 = ((bf16[16,64,776]{2,1,0:T(8,128)(2,1)}), bf16[16,64,776]{2,1,0:T(8,128)(2,1)S(1)}, u32[]{:S(2)}, u32[]{:S(2)}) async-start(bf16[16,64,776]{2,1,0:T(8,128)(2,1)} %add_convert_fusion.4), calls=%async_computation.1 | async-start | bytes 3670016 | tf_op jit(solution)/shard_map/all_to_all | solution.py:948
  492.8 52.3 %collective-permute-start.44 = (bf16[64,2048]{1,0:T(8,128)(2,1)}, bf16[64,2048]{1,0:T(8,128)(2,1)}, u32[]{:S(2)}, u32[]{:S(2)}) collective-permute-start(bf16[64,2048]{1,0:T(8,128)(2,1)} %get-tuple-element.328), channel_id=1, source_target_pairs={{0,16},{16,0},{1,17},{17,1},{2,18},{18,2},{3,19},{19,3},{4,20},{20... | collective-permute-start | bytes 786440 | tf_op jit(solution)/shard_map/ppermute | solution.py:695
  (106 other events, 649.7 us)
Sparse Core Ops, SparseCore 0:
  43.9 40.5 all-gather.8
  86.1 30.1 all-gather.10
  117.9 29.1 all-gather.6
  148.5 29.1 all-gather.4

commit v2 on v1

--- a/solution.py
+++ b/solution.py
@@ -151,7 +151,7 @@
     state[...] = held * grown_wide[span - 1 : span, :] + fresh
 
 
-def scan_forward(raw, at, taps, bias, shift, log_rate, skip_wide):
+def scan_forward(raw, at, taps, bias, shift, log_rate, skip_wide, wait=()):
     _, length, width = raw.shape
     seqs = 1
     heads = shift.shape[0]
@@ -159,8 +159,10 @@
     wide = inner + 2 * STATE
     spans = length // SPAN
     whole = lambda shape: pl.BlockSpec(shape, lambda s, i: (0,) * len(shape))
-    return pl.pallas_call(
+    return call_after(
+        wait,
         functools.partial(scan_forward_body, heads),
+        (raw, taps, bias, shift, log_rate, skip_wide),
         grid=(seqs, spans),
         in_specs=[
             pl.BlockSpec((None, SPAN, width), lambda s, i: (at, i, 0)),
@@ -182,9 +184,9 @@
         ],
         scratch_shapes=[pltpu.VMEM((STATE, inner), F32), pltpu.VMEM((SPAN + 8, wide), F32)],
         compiler_params=kernel_params(),
-        cost_estimate=light_cost(length),
+        cost_estimate=light_cost(10),
         name="scan_forward",
-    )(raw, taps, bias, shift, log_rate, skip_wide)
+    )
 
 
 def scan_backward_body(
@@ -316,7 +318,7 @@
     return jnp.concatenate([columns, jnp.zeros((span, 128 - heads), F32)], 1).T[:heads]
 
 
-def scan_backward(raw, at, down, starts, edges, taps, bias, shift, log_rate, skip_wide):
+def scan_backward(raw, at, down, starts, edges, taps, bias, shift, log_rate, skip_wide, wait=()):
     _, length, width = raw.shape
     seqs = 1
     heads = shift.shape[0]
@@ -325,8 +327,10 @@
     spans = length // SPAN
     whole = lambda shape: pl.BlockSpec(shape, lambda s, i: (0,) * len(shape))
     turned = lambda s, i: (s, spans - 1 - i, 0)
-    return pl.pallas_call(
+    return call_after(
+        wait,
         functools.partial(scan_backward_body, heads),
+        (raw, down, starts, edges, taps, bias, shift, log_rate, skip_wide),
         grid=(seqs, spans),
         in_specs=[
             pl.BlockSpec((None, SPAN, width), lambda s, i: (at, spans - 1 - i, 0)),
@@ -357,17 +361,26 @@
             pltpu.VMEM((SPAN + 8, wide), F32),
         ],
         compiler_params=kernel_params(),
-        cost_estimate=light_cost(length),
+        cost_estimate=light_cost(22),
         name="scan_backward",
-    )(raw, down, starts, edges, taps, bias, shift, log_rate, skip_wide)
-
+    )
 
 def kernel_params():
-    return pltpu.CompilerParams(vmem_limit_bytes=30 * 1024 * 1024)
-
-
-def light_cost(count):
-    return pl.CostEstimate(flops=count, bytes_accessed=count, transcendentals=0)
+    return pltpu.CompilerParams(vmem_limit_bytes=58 * 1024 * 1024)
+
+
+def call_after(wait, body, values, in_specs, **rest):
+    held = [pl.BlockSpec(memory_space=pl.ANY)] * len(wait)
+
+    def inner_body(*refs):
+        body(*refs[: len(values)], *refs[len(values) + len(wait) :])
+
+    return pl.pallas_call(inner_body, in_specs=list(in_specs) + held, **rest)(*values, *wait)
+
+
+def light_cost(micros):
+    work = int(micros * 1e9 * 1.0)
+    return pl.CostEstimate(flops=work, bytes_accessed=work // 400, transcendentals=0)
 
 
 def project_body(inner, tokens_ref, weight_ref, gate_ref, raw_ref, turned_ref):
@@ -380,15 +393,17 @@
         turned_ref[half] = pair.T
 
 
-def project_tokens(values, weight, inner):
+def project_tokens(values, weight, inner, wait=()):
     team, _, tokens, model = values.shape
     width = weight.shape[0]
 
     def natural(size):
         return pl.BlockSpec((2, 2, tokens, size), lambda i: (0, i, 0, 0))
 
-    return pl.pallas_call(
+    return call_after(
+        wait,
         functools.partial(project_body, inner),
+        (values, weight),
         grid=(team // 2,),
         in_specs=[
             pl.BlockSpec((2, 2, tokens, model), lambda i: (i, 0, 0, 0)),
@@ -405,9 +420,9 @@
             jax.ShapeDtypeStruct((2, model, team * tokens), BF16),
         ],
         compiler_params=kernel_params(),
-        cost_estimate=light_cost(team),
+        cost_estimate=light_cost(11),
         name="project_tokens",
-    )(values, weight)
+    )
 
 
 def by_member(ref):
@@ -435,14 +450,16 @@
     sums_ref[...] = as_columns_back(jnp.concatenate([square, cross], 1))
 
 
-def gate_stats(grad, weight, mixed, gate, gain):
+def gate_stats(grad, weight, mixed, gate, gain, wait=()):
     team, _, tokens, model = grad.shape
     inner = weight.shape[0]
     pair = 2
     rows = pair * 2 * tokens
     natural = pl.BlockSpec((2, pair, tokens, inner), lambda i: (0, i, 0, 0))
-    return pl.pallas_call(
+    return call_after(
+        wait,
         gate_stats_body,
+        (grad, weight, mixed, gate, gain),
         grid=(team // pair,),
         in_specs=[
             pl.BlockSpec((pair, 2, tokens, model), lambda i: (i, 0, 0, 0)),
@@ -460,23 +477,12 @@
             jax.ShapeDtypeStruct((2, team * 2 * tokens), F32),
         ],
         compiler_params=kernel_params(),
-        cost_estimate=light_cost(team),
+        cost_estimate=light_cost(7),
         name="gate_stats",
-    )(grad, weight, mixed, gate, gain)
-
-
-def put_by_core(own, keep_ref, send_ref, rows):
-    tokens = keep_ref.shape[1]
-    first, second = rows[: 2 * tokens], rows[2 * tokens :]
-    kept = jnp.where(own == 0, first, second)
-    sent = jnp.where(own == 0, second, first)
-    for half in range(2):
-        keep_ref[half] = kept[half * tokens : (half + 1) * tokens].astype(BF16)
-        send_ref[half] = sent[half * tokens : (half + 1) * tokens].astype(BF16)
+    )
 
 
 def gate_back_body(
-    table_ref,
     mixed_ref,
     gate_ref,
     down_ref,
@@ -486,8 +492,7 @@
     turned_ref,
     d_mixed_ref,
     d_gate_ref,
-    keep_ref,
-    send_ref,
+    out_ref,
     d_gain_ref,
 ):
     @pl.when(pl.program_id(0) == 0)
@@ -507,56 +512,50 @@
     scaled = unit * scale
     gated_wide = scaled * gain
     turned_ref[...] = gated_wide.T.astype(BF16)
-    out = dot_plain(gated_wide.astype(BF16), weight_ref[...])
-    put_by_core(table_ref[0], keep_ref, send_ref, out)
+    out_ref[...] = dot_plain(gated_wide.astype(BF16), weight_ref[...]).astype(BF16)
     d_unit = down * gain * scale - unit * pull
     put_by_member(d_mixed_ref, d_unit * act)
     put_by_member(d_gate_ref, d_unit * mixed * (sig * (1.0 + gate * (1.0 - sig))))
     d_gain_ref[...] += jnp.sum(down * scaled, axis=0, keepdims=True)
 
 
-def gate_back(table, mixed, gate, down, sums, gain, weight):
+def gate_back(mixed, gate, down, sums, gain, weight, wait=()):
     _, team, tokens, inner = down.shape
     model = weight.shape[1]
-    chips = team // 2
     rows = 4 * tokens
-    natural = pl.BlockSpec((2, 2, tokens, inner), lambda i, t: (0, t[1 + i], 0, 0))
-    block = pl.BlockSpec((None, 2, tokens, model), lambda i, t: (i, 0, 0, 0))
-    one = pl.BlockSpec((1, inner), lambda i, t: (0, 0))
-    return pl.pallas_call(
+    natural = pl.BlockSpec((2, 2, tokens, inner), lambda i: (0, i, 0, 0))
+    one = pl.BlockSpec((1, inner), lambda i: (0, 0))
+    return call_after(
+        wait,
         gate_back_body,
-        grid_spec=pltpu.PrefetchScalarGridSpec(
-            num_scalar_prefetch=1,
-            grid=(chips,),
-            in_specs=[
-                natural,
-                natural,
-                natural,
-                pl.BlockSpec((2, rows), lambda i, t: (0, t[1 + i])),
-                one,
-                pl.BlockSpec((inner, model), lambda i, t: (0, 0)),
-            ],
-            out_specs=[
-                pl.BlockSpec((inner, rows), lambda i, t: (0, t[1 + i])),
-                natural,
-                natural,
-                block,
-                block,
-                one,
-            ],
-        ),
+        (mixed, gate, down, sums, gain, weight),
+        grid=(team // 2,),
+        in_specs=[
+            natural,
+            natural,
+            natural,
+            pl.BlockSpec((2, rows), lambda i: (0, i)),
+            one,
+            pl.BlockSpec((inner, model), lambda i: (0, 0)),
+        ],
+        out_specs=[
+            pl.BlockSpec((inner, rows), lambda i: (0, i)),
+            natural,
+            natural,
+            pl.BlockSpec((rows, model), lambda i: (i, 0)),
+            one,
+        ],
         out_shape=[
             jax.ShapeDtypeStruct((inner, team * 2 * tokens), BF16),
             jax.ShapeDtypeStruct((2, team, tokens, inner), BF16),
             jax.ShapeDtypeStruct((2, team, tokens, inner), BF16),
-            jax.ShapeDtypeStruct((chips, 2, tokens, model), BF16),
-            jax.ShapeDtypeStruct((chips, 2, tokens, model), BF16),
+            jax.ShapeDtypeStruct((team * 2 * tokens, model), BF16),
             jax.ShapeDtypeStruct((1, inner), F32),
         ],
         compiler_params=kernel_params(),
-        cost_estimate=light_cost(team),
+        cost_estimate=light_cost(8),
         name="gate_back",
-    )(table, mixed, gate, down, sums, gain, weight)
+    )
 
 
 def row_grad_body(pairs, cols, has_base, *refs):
@@ -580,7 +579,7 @@
     out_ref[...] = total.astype(out_ref.dtype)
 
 
-def row_grad(operands, kind, cols=None, base=None):
+def row_grad(operands, kind, cols=None, base=None, wait=()):
     rows = operands[0][0].shape[1]
     width = operands[0][1].shape[1]
     got = width if cols is None else cols[1] - cols[0]
@@ -595,67 +594,65 @@
     if base is not None:
         specs.append(pl.BlockSpec((tile, width), lambda i: (i, 0)))
         args.append(base)
-    return pl.pallas_call(
+    return call_after(
+        wait,
         functools.partial(row_grad_body, len(operands), cols, base is not None),
+        tuple(args),
         grid=(rows // tile,),
         in_specs=specs,
         out_specs=pl.BlockSpec((tile, got), lambda i: (i, 0)),
         out_shape=jax.ShapeDtypeStruct((rows, got), kind),
         compiler_params=kernel_params(),
-        cost_estimate=light_cost(rows),
+        cost_estimate=light_cost(8),
         name="row_grad",
-    )(*args)
-
-
-def norm_part_body(
-    table_ref, d_gate_ref, d_raw_ref, normed_ref, weight_ref, keep_ref, send_ref, gain_ref
-):
+    )
+
+
+def norm_part_body(d_gate_ref, d_raw_ref, normed_ref, weight_ref, out_ref, gain_ref):
     @pl.when(pl.program_id(0) == 0)
     def _():
         gain_ref[...] = jnp.zeros_like(gain_ref)
 
     inner = d_gate_ref.shape[-1]
-    tokens = keep_ref.shape[1]
-    model = keep_ref.shape[2]
     part = dot_plain(by_member(d_gate_ref), weight_ref[:inner, :])
     part = part + dot_plain(by_member(d_raw_ref), weight_ref[inner:, :])
-    normed = normed_ref[...].reshape(4 * tokens, model).astype(F32)
+    normed = normed_ref[...].reshape(out_ref.shape).astype(F32)
     gain_ref[...] += jnp.sum(part * normed, axis=0, keepdims=True)
-    put_by_core(table_ref[0], keep_ref, send_ref, part)
-
-
-def norm_part(table, d_gate, d_raw, normed, weight):
+    out_ref[...] = part.astype(BF16)
+
+
+def norm_part(d_gate, d_raw, normed, weight, wait=()):
     _, team, tokens, inner = d_gate.shape
-    chips = team // 2
     width = d_raw.shape[-1]
     model = weight.shape[1]
+    rows = 4 * tokens
 
     def natural(size):
-        return pl.BlockSpec((2, 2, tokens, size), lambda i, t: (0, t[1 + i], 0, 0))
-
-    block = pl.BlockSpec((None, 2, tokens, model), lambda i, t: (i, 0, 0, 0))
-    return pl.pallas_call(
+        return pl.BlockSpec((2, 2, tokens, size), lambda i: (0, i, 0, 0))
+
+    return call_after(
+        wait,
         norm_part_body,
-        grid_spec=pltpu.PrefetchScalarGridSpec(
-            num_scalar_prefetch=1,
-            grid=(chips,),
-            in_specs=[
-                natural(inner),
-                natural(width),
-                pl.BlockSpec((2, 2, tokens, model), lambda i, t: (t[1 + i], 0, 0, 0)),
-                pl.BlockSpec((inner + width, model), lambda i, t: (0, 0)),
-            ],
-            out_specs=[block, block, pl.BlockSpec((1, model), lambda i, t: (0, 0))],
-        ),
+        (d_gate, d_raw, normed, weight),
+        grid=(team // 2,),
+        in_specs=[
+            natural(inner),
+            natural(width),
+            pl.BlockSpec((2, 2, tokens, model), lambda i: (i, 0, 0, 0)),
+            pl.BlockSpec((inner + width, model), lambda i: (0, 0)),
+        ],
+        out_specs=[
+            pl.BlockSpec((rows, model), lambda i: (i, 0)),
+            pl.BlockSpec((1, model), lambda i: (0, 0)),
+        ],
         out_shape=[
-            jax.ShapeDtypeStruct((chips, 2, tokens, model), BF16),
-            jax.ShapeDtypeStruct((chips, 2, tokens, model), BF16),
+            jax.ShapeDtypeStruct((team * 2 * tokens, model), BF16),
             jax.ShapeDtypeStruct((1, model), F32),
         ],
         compiler_params=kernel_params(),
-        cost_estimate=light_cost(chips),
+        cost_estimate=light_cost(11),
         name="norm_part",
-    )(table, d_gate, d_raw, normed, weight)
+    )
 
 
 TEAM = ("chip", "core")
@@ -663,16 +660,19 @@
 EVERY = ALL + ("wsh",)
 
 
-def after(values, *done):
-    leaves, tree = jax.tree.flatten(values)
-    others = jax.tree.leaves(done)
-    out = lax.optimization_barrier(tuple(leaves) + tuple(others))
-    return jax.tree.unflatten(tree, out[: len(leaves)])
-
-
 def join(*values):
     leaves, tree = jax.tree.flatten(values)
-    return jax.tree.unflatten(tree, lax.optimization_barrier(tuple(leaves)))
+    anywhere = [pl.BlockSpec(memory_space=pl.ANY)] * len(leaves)
+    out = pl.pallas_call(
+        lambda *refs: None,
+        in_specs=anywhere,
+        out_specs=anywhere,
+        out_shape=[jax.ShapeDtypeStruct(v.shape, v.dtype) for v in leaves],
+        input_output_aliases={k: k for k in range(len(leaves))},
+        cost_estimate=light_cost(0),
+        name="join",
+    )(*leaves)
+    return jax.tree.unflatten(tree, out)
 
 
 class Layout:
@@ -724,17 +724,13 @@
     return jnp.concatenate([first, second], 0)
 
 
-def core_sum(keep, came):
-    return (keep.astype(F32) + came.astype(F32)).astype(BF16)
-
-
-def chip_parts(added, lay):
-    return [added[0]] + [lay.chip_flip(added[bits], bits) for bits in range(1, lay.chips)]
-
-
-def chip_sum(parts, lay):
-    own = add_all([part.astype(F32) for part in parts]).astype(BF16)
-    return pick(own, lay.half, 0), pick(own, 1 - lay.half, 0)
+def team_sum(part, lay):
+    own = lax.psum_scatter(part, TEAM, scatter_dimension=0, tiled=True)
+    return own.reshape(2, own.shape[0] // 2, own.shape[1])
+
+
+def two_halves(own, lay):
+    return pick(own, lay.half, 0), lay.other_half(pick(own, 1 - lay.half, 0))
 
 
 def columns_in_place(local, came, lay):
@@ -757,17 +753,6 @@
     while len(parts) > 1:
         parts = [parts[k] + parts[k + 1] for k in range(0, len(parts), 2)]
     return parts[0]
-
-
-class Order:
-    def __init__(self):
-        self.last = ()
-
-    def __call__(self, step, first, *rest):
-        first = after(first, self.last)
-        out = step(first, *rest)
-        self.last = (jax.tree.leaves(out)[0],)
-        return out
 
 
 def shards(
@@ -815,18 +800,18 @@
 
     cut = (inner // 128 + 1) * 128
     keep, away = split_halves(normed, lay)
-    came_first, came = join(to_wsh(local[:cut]), lay.other_half(away))
     keep_grad, away_grad = split_halves(cotangent, lay)
+    came_first, came, later, away_grad = join(
+        to_wsh(local[:cut]), lay.other_half(away), local[cut:], away_grad
+    )
     normeds = [team_gather(keep[0], came[0], lay)]
-    came_last, came_grad = join(
-        to_wsh(after(local[cut:], came_first)), lay.other_half(after(away_grad, came))
-    )
-    weight = columns_in_place(local, [(0, came_first), (cut, came_last)], lay)
     rows_held = INNER // lay.wsh
     owner = (block * inner) // rows_held
     at_row = jnp.where(owner == lay.wplace, block * inner - owner * rows_held, 0)
-    rows_here = after(columns(out_proj, at_row, inner, 0), came_last)
-    w_out = jnp.where(owner == lay.wplace, rows_here, jnp.zeros_like(rows_here))
+    rows_here = columns(out_proj, at_row, inner, 0)
+    came_last, came_grad, rows_here = join(to_wsh(later), lay.other_half(away_grad), rows_here)
+    weight = columns_in_place(local, [(0, came_first), (cut, came_last)], lay)
+    out_pieces = []
     for shift in range(1, lay.wsh):
         pairs = []
         for place in range(lay.team):
@@ -834,11 +819,17 @@
             holder = (head_block * inner) // rows_held
             source = place * lay.wsh + holder
             pairs.append((source, place * lay.wsh + (holder + shift) % lay.wsh))
-        w_out = w_out + lax.ppermute(rows_here, TEAM + ("wsh",), pairs)
-    keep_grad = after(keep_grad, came_last)
+        out_pieces.append(lax.ppermute(rows_here, TEAM + ("wsh",), pairs))
+
+    def own_rows(first, *rest):
+        total = jnp.where(owner == lay.wplace, rows_here, jnp.zeros_like(rows_here)) + first
+        for piece in rest:
+            total = total + piece
+        return total
+
     grads = [team_gather(keep_grad[0], came_grad[0], lay)]
     for s in range(1, count):
-        normeds.append(team_gather(*after((keep[s], came[s]), came_last), lay))
+        normeds.append(team_gather(keep[s], came[s], lay))
         grads.append(team_gather(keep_grad[s], came_grad[s], lay))
 
     taps = jnp.concatenate(
@@ -850,7 +841,6 @@
     skip_own = jnp.repeat(columns(d_skip, block * heads, heads, 0), HEADDIM)[None]
     gain_own = columns(gate_gain, block * inner, inner, 0)[None]
     params = (taps, bias[None], shift_own, rate_own, skip_own)
-    table = jnp.stack([lay.core] + [lay.chip ^ d for d in range(lay.chips)]).astype(jnp.int32)
 
     kernel = conv_weight.shape[0]
     shapes = [norm_gain.shape, conv_weight.shape, conv_bias.shape]
@@ -889,54 +879,47 @@
     natural = (2, team, tokens)
     out_rows = INNER // (lay.parts * lay.wsh)
     in_rows = model // (lay.parts * lay.wsh)
-    run = Order()
 
     gates, raws, turned_normed = [], [], []
     mixed, starts, edges, downs = [], [], [], []
     turned_gated, d_gates, d_raws, small_scan = [], [], [], []
 
-    def project_step(at):
-        gate, raw, flat = run(lambda v: project_tokens(v, weight, inner), normeds[at])
+    def project_step(at, wait=()):
+        gate, raw, flat = project_tokens(normeds[at], weight, inner, wait)
         gates.append(gate)
         raws.append(raw.reshape(1, length, raw.shape[-1]))
         turned_normed.append(flat)
 
-    def forward_step(at):
-        got = run(lambda p: scan_forward(raws[at], 0, p, *params[1:]), params[0])
+    def forward_step(at, wait=()):
+        got = scan_forward(raws[at], 0, *params, wait=wait)
         mixed.append(got[0].reshape(natural + (inner,)))
         starts.append(got[1])
         edges.append(got[2])
 
-    def stats_step(at):
-        down, own = run(lambda m: gate_stats(grads[at], w_out, m, gates[at], gain_own), mixed[at])
+    def stats_step(at, wait=()):
+        down, own = gate_stats(grads[at], w_out, mixed[at], gates[at], gain_own, wait)
         downs.append(down)
         return own
 
-    def back_step(at, sums):
-        flat, d_mixed, d_gate, keep, send, gain = run(
-            lambda v: gate_back(table, mixed[at], gates[at], downs[at], v, gain_own, w_out), sums
+    def back_step(at, sums, wait=()):
+        flat, d_mixed, d_gate, out, gain = gate_back(
+            mixed[at], gates[at], downs[at], sums, gain_own, w_out, wait
         )
         turned_gated.append(flat[None])
         d_gates.append(d_gate)
-        return d_mixed, keep, send, gain
-
-    def scan_step(at, d_mixed):
-        d_raw, *small = run(
-            lambda d: scan_backward(
-                raws[at], 0, d.reshape(1, length, inner), starts[at], edges[at], *params
-            ),
-            d_mixed,
+        return d_mixed, out, gain
+
+    def scan_step(at, d_mixed, wait=()):
+        d_mixed = d_mixed.reshape(1, length, inner)
+        d_raw, *small = scan_backward(
+            raws[at], 0, d_mixed, starts[at], edges[at], *params, wait=wait
         )
         d_raws.append(d_raw[0])
         small_scan.append(small)
 
-    def norm_step(at):
-        return run(
-            lambda v: norm_part(
-                table, d_gates[at], v.reshape(natural + (v.shape[-1],)), normeds[at], weight
-            ),
-            d_raws[at],
-        )
+    def norm_step(at, wait=()):
+        d_raw = d_raws[at].reshape(natural + (d_raws[at].shape[-1],))
+        return norm_part(d_gates[at], d_raw, normeds[at], weight, wait)
 
     def owned_parts(part):
         blocks = part.reshape(lay.parts, lay.wsh, in_rows, part.shape[1])
@@ -953,61 +936,7 @@
             total = total + part.astype(F32)
         return total.astype(BF16)
 
-    def chip_step(keep, came):
-        return run(lambda v: chip_parts(core_sum(keep, v), lay), came)
-
-    def finish(parts):
-        mine, away = run(lambda v: chip_sum([v] + parts[1:], lay), parts[0])
-        return mine, lay.other_half(away)
-
-    project_step(0)
-    forward_step(0)
-    parts = run(lambda v: team_parts(v, lay), stats_step(0))
-    sums = run(add_all, parts)
-    d_mixed0, out_keep0, send, gain0 = back_step(0, sums)
-    out_came0 = lay.other_core(send)
-    scan_step(0, d_mixed0)
-    out_parts0 = chip_step(out_keep0, out_came0)
-    project_step(1)
-    forward_step(1)
-    own = stats_step(1)
-    sum0 = finish(out_parts0)
-    parts = run(lambda v: team_parts(v, lay), own)
-    scan_base = run(lambda v: row_grad([(turned_normed[0], v)], F32), d_raws[0])
-    keep0, send, norm_gain0 = norm_step(0)
-    came0 = lay.other_core(send)
-    parts, sum0 = join(parts, sum0)
-    sums = run(add_all, parts)
-    d_mixed1, out_keep1, send, gain1 = back_step(1, sums)
-    norm_parts0 = chip_step(keep0, came0)
-    out_came1 = lay.other_core(send)
-    flat_gates = [d.reshape(length, inner) for d in d_gates]
-    gate_grad = run(
-        lambda v: row_grad([(turned_normed[0], v), (turned_normed[1], flat_gates[1])], BF16),
-        flat_gates[0],
-    )
-    out_parts1 = chip_step(out_keep1, out_came1)
-    gate_kept, gate_came = run(owned_parts, gate_grad)
     flat_grads = [g.reshape(length, model) for g in grads]
-    out_grad = run(
-        lambda v: row_grad([(v, flat_grads[0]), (turned_gated[1], flat_grads[1])], BF16),
-        turned_gated[0],
-    )
-    blocks = out_grad.reshape(2, lay.wsh, out_rows, model)
-
-    def out_split(values):
-        kept = pick(values, lay.wplace, 1)
-        away = [pick(values, (lay.wplace + d) % lay.wsh, 1) for d in range(1, lay.wsh)]
-        return kept, [lay.wsh_shift(a, d + 1) for d, a in enumerate(away)]
-
-    out_kept, out_came = run(out_split, blocks)
-    scan_step(1, d_mixed1)
-    norm_parts0, out_parts1, gate_came, out_came, run.last = join(
-        norm_parts0, out_parts1, gate_came, out_came, run.last
-    )
-    norm0 = finish(norm_parts0)
-    gate_kept = run(add_owned, gate_kept, gate_came)
-    out_kept = run(add_owned, out_kept, out_came)
     cross, first_pairs, second_pairs = [], [], []
     for half in range(2):
         for chip in range(lay.chips):
@@ -1017,47 +946,86 @@
             cross.append((peer, source))
             first_pairs.append((source, 2 * head_block))
             second_pairs.append((source, 2 * head_block + 1))
+
+    def out_split(values):
+        values = values.reshape(2, lay.wsh, out_rows, model)
+        kept = pick(values, lay.wplace, 1)
+        away = [pick(values, (lay.wplace + d) % lay.wsh, 1) for d in range(1, lay.wsh)]
+        return kept, [lay.wsh_shift(a, d + 1) for d, a in enumerate(away)]
+
+    def over_groups(values):
+        parts = []
+        for bits in range(lay.wsh):
+            moved = values
+            if bits:
+                pairs = [(i, i ^ bits) for i in range(lay.wsh)]
+                moved = lax.ppermute(values, "wsh", pairs)
+            both = [(h * lay.wsh + i, (1 - h) * lay.wsh + (i ^ bits)) for h in range(2) for i in range(lay.wsh)]
+            parts += [moved, lax.ppermute(values, ("half", "wsh"), both)]
+        return parts
+
+    project_step(0)
+    forward_step(0)
+    out_pieces, mixed[0] = join(out_pieces, mixed[0])
+    w_out = own_rows(*out_pieces)
+    sums = add_all(team_parts(stats_step(0), lay))
+    d_mixed0, out, gain0 = back_step(0, sums)
+    out0 = team_sum(out, lay)
+    scan_step(0, d_mixed0)
+    project_step(1, (small_scan[0][1],))
+    forward_step(1)
+    own = stats_step(1)
+    parts = team_parts(own, lay)
+    part, norm_gain0 = norm_step(0, (own,))
+    norm0 = team_sum(part, lay)
+    sums = add_all(parts)
+    d_mixed1, out, gain1 = back_step(1, sums, (norm_gain0,))
+    out1 = team_sum(out, lay)
+    flat_gates = [d.reshape(length, inner) for d in d_gates]
+    gate_grad = row_grad(
+        [(turned_normed[0], flat_gates[0]), (turned_normed[1], flat_gates[1])], BF16
+    )
+    gate_kept, gate_came = owned_parts(gate_grad)
+    out_grad = row_grad(
+        [(turned_gated[0], flat_grads[0]), (turned_gated[1], flat_grads[1])],
+        BF16,
+        wait=(gate_kept,),
+    )
+    out_kept, out_came = out_split(out_grad)
+    scan_base = row_grad([(turned_normed[0], d_raws[0])], F32, wait=(out_kept,))
+    gate_came, sum0, d_mixed1, scan_base = join(
+        gate_came, two_halves(out0, lay), d_mixed1, scan_base
+    )
+    by_gate = to_owners(add_owned(gate_kept, gate_came))
+    scan_step(1, d_mixed1)
+    part, norm_gain1 = norm_step(1)
+    norm1 = team_sum(part, lay)
+    out_came, sum1, norm_gain1 = join(out_came, two_halves(out1, lay), norm_gain1)
+    scan_grad = row_grad(
+        [(turned_normed[1], d_raws[1])], BF16, None, scan_base, wait=(norm_gain1,)
+    )
+    scan_kept, scan_came = owned_parts(scan_grad)
+    out_kept = add_owned(out_kept, out_came)
     out_came = lax.ppermute(out_kept, ALL, cross)
-    sum1 = finish(out_parts1)
-    keep1, send, norm_gain1 = norm_step(1)
-    came1 = lay.other_core(send)
-    scan_grad = run(lambda v: row_grad([(turned_normed[1], v)], BF16, None, scan_base), d_raws[1])
-    scan_kept, scan_came = run(owned_parts, scan_grad)
-    norm_parts1 = chip_step(keep1, came1)
-    by_gate = to_owners(gate_kept)
-    small = run(lambda v: pack_small(v), norm_gain1)
-    small = run(lambda v: v + lay.other_core(v), small)
-    small = [small] + [lay.chip_flip(small, b) for b in range(1, lay.chips)]
-    scan_came, norm_parts1, by_gate, small, out_came, norm0, sum1, run.last = join(
-        scan_came, norm_parts1, by_gate, small, out_came, norm0, sum1, run.last
-    )
-    scan_kept = run(add_owned, scan_kept, scan_came)
-    by_scan = to_owners(scan_kept)
-    norm1 = finish(norm_parts1)
-    small = run(add_all, small)
-    out_held = run(lambda v: (v.astype(F32) + out_came.astype(F32)).astype(BF16), out_kept)
+    small = add_all(team_parts(pack_small(norm_gain1), lay))
+    scan_came, norm0, small = join(scan_came, two_halves(norm0, lay), small)
+    by_scan = to_owners(add_owned(scan_kept, scan_came))
+    out_held = (out_kept.astype(F32) + out_came.astype(F32)).astype(BF16)
     out_first = lax.ppermute(out_held[0], ALL, first_pairs)
     out_second = lax.ppermute(out_held[1], ALL, second_pairs)
-    small = run(lambda v: v + lay.other_half(v), small)
-    bit = 1
-    while bit < lay.wsh:
-        small = run(
-            lambda v: v + lax.ppermute(v, "wsh", [(i, i ^ bit) for i in range(lay.wsh)]), small
-        )
-        bit *= 2
-    out_proj_grad = run(lambda v: v.astype(F32) + out_second.astype(F32), out_first)
+    norm1 = two_halves(norm1, lay)
+    small = add_all(over_groups(small))
+    out_proj_grad = out_first.astype(F32) + out_second.astype(F32)
 
     def whole_place(first, second):
         mine = jnp.stack([first[0], second[0]], 0)
         other = jnp.stack([first[1], second[1]], 0)
         return both_halves(mine, other, lay)
 
-    block_out = run(
-        lambda v: (hidden_wide + whole_place((v, sum0[1]), sum1).astype(F32)).astype(BF16), sum0[0]
-    )
-
-    def hidden_step(value):
-        d_scaled = whole_place((value, norm0[1]), norm1).astype(F32) * norm_gain
+    block_out = (hidden_wide + whole_place(sum0, sum1).astype(F32)).astype(BF16)
+
+    def hidden_step():
+        d_scaled = whole_place(norm0, norm1).astype(F32) * norm_gain
         inward = jnp.mean(d_scaled * hidden_wide, axis=-1, keepdims=True)
         return (
             cotangent.astype(F32)
@@ -1065,7 +1033,7 @@
             - hidden_wide * (norm_scale * norm_scale * norm_scale * inward)
         )
 
-    hidden_grad = run(hidden_step, norm0[0])
+    hidden_grad = hidden_step()
 
     def assemble(scan_parts):
         def owned(parts):
@@ -1084,7 +1052,7 @@
             1,
         )
 
-    in_proj_grad = run(assemble, by_scan)
+    in_proj_grad = assemble(by_scan)
     ngain_all, conv_all, cbias_all, shift_all, rate_all, skip_all, ggain_all = unpack_small(small)
     return (
         block_out,

time: 569 us -> 492 us (0.86)
  waiting for transfers between devices: 208 us -> 127 us
  Pallas kernels: 137 us -> 181 us
  local copies, waits for them, and re-layouts: 87.8 us -> 62.4 us
  starting transfers between devices: 70.6 us -> 58.5 us
    ppermute x7 -> x6, waiting for transfers between devices: 127 us -> 49 us  [other_half(): return lax.ppermute(values, 'half', [(0, 1), (1, 0)])]
    unnamed x170 -> x100, local copies, waits for them, and re-layouts: 54.3 us -> 6.05 us
    pallas_call x16 -> x22, Pallas kernels: 137 us -> 181 us  [the longest x16 181 us: call_after(): pl.pallas_call(inner_body, in_specs=list(in_specs) + held, **rest)]
    ppermute x21 -> x9, waiting for transfers between devices: 37.4 us -> 6.51 us  [chip_flip(): lax.ppermute(values, 'chip', [(i, i ^ bits) for i in range(self.chips)])]
    ppermute x2 -> x4, waiting for transfers between devices: 18 us -> 44.3 us  [the longest x2 44.2 us: over_groups(): parts += [moved, lax.ppermute(values, ('half', 'wsh'), both)]]
    ppermute x1, waiting for transfers between devices: 0.01 us -> 13.9 us  [shards(): out_came = lax.ppermute(out_kept, ALL, cross)]
    convert_element_type x10 -> x1, other arithmetic: 16.2 us -> 2.58 us  [shards(): out_held = (out_kept.astype(F32) + out_came.astype(F32)).astype(BF16)]
    ppermute x5, waiting for transfers between devices: 22.9 us -> 9.7 us  [wsh_shift(): lax.ppermute(values, 'wsh', [(i, (i + shift) % size) for i in range(size)])]
  transfers between devices with their start and end apart: 51 -> 40, of which waited for: 24 -> 18; matrix products, arithmetic and copies ran while one was open for 10% -> 17% of each run, Pallas kernels for 20% -> 38%
where the time goes in v2:
time: 492 us; the launch traced here: 483 us
  Pallas kernels  181 us (37%)
  waiting for transfers between devices  127 us (26%)
  local copies, waits for them, and re-layouts  62.4 us (13%)
  starting transfers between devices  58.5 us (12%)
  other arithmetic  38.2 us (8%)
  between operations  15.3 us (3%)
    pallas_call x16, Pallas kernels, call_after(): pl.pallas_call(inner_body, in_specs=list(in_specs) + held, **rest)  181 us
    ppermute x6, waiting for transfers between devices, other_half(): return lax.ppermute(values, 'half', [(0, 1), (1, 0)])  49 us
    ppermute x2, waiting for transfers between devices, over_groups(): parts += [moved, lax.ppermute(values, ('half', 'wsh'), both)]  44.2 us
    ppermute x6, starting transfers between devices, other_half(): return lax.ppermute(values, 'half', [(0, 1), (1, 0)])  18.3 us
    squeeze x6, local copies, waits for them, and re-layouts, pick(): return lax.dynamic_index_in_dim(values, at, axis, keepdims=False)  14.1 us
    ppermute x1, waiting for transfers between devices, shards(): out_came = lax.ppermute(out_kept, ALL, cross)  13.9 us
    ppermute x9, starting transfers between devices, chip_flip(): lax.ppermute(values, 'chip', [(i, i ^ bits) for i in range(self.chips)])  10.5 us
  transfers between devices with their start and end apart: 40, of which 18 were waited for; matrix products, arithmetic and copies ran while one was open for 17% of the time, Pallas kernels for 38%

profile of v2, /device:TPU:0, one launch (start us, length us, event | category | flops | bytes accessed | tf_op | source)
XLA Modules:
  0.0 482.6 jit_solution(10363918501404094897)
XLA Ops:
  25.5 16.3 %collective-permute-done.1.refs_1_ = bf16[2,64,2048]{2,1,0:T(8,128)(2,1)S(1)} collective-permute-done((bf16[2,64,2048]{2,1,0:T(8,128)(2,1)}, bf16[2,64,2048]{2,1,0:T(8,128)(2,1)S(1)}, u32[]{:S(2)}, u32[]{:S(2)}) %collective-permute-start.1) | collective-permute-done | bytes 524320 | tf_op jit(solution)/shard_map/ppermute | solution.py:695
  52.3 3.2 constant_dynamic-slice_fusion.2.refs_2_
  55.5 17.4 %collective-permute-done.3.refs_1_ = bf16[2,64,2048]{2,1,0:T(8,128)(2,1)} collective-permute-done((bf16[2,64,2048]{2,1,0:T(8,128)(2,1)}, bf16[2,64,2048]{2,1,0:T(8,128)(2,1)}, u32[]{:S(2)}, u32[]{:S(2)}) %collective-permute-start.3) | collective-permute-done | bytes 524320 | tf_op jit(solution)/shard_map/ppermute | solution.py:695
  72.9 3.8 collective-permute-done.2.refs_0_
  94.1 4.5 collective-permute-start.4
  101.2 11.6 %project_tokens.2 = (bf16[2,8,64,512]{3,2,1,0:T(8,128)(2,1)}, bf16[2,8,64,776]{3,2,1,0:T(8,128)(2,1)}, bf16[2,2048,512]{2,1,0:T(8,128)(2,1)}) custom-call(bf16[8,2,64,2048]{3,2,1,0:T(8,128)(2,1)} %all-gather.5.cloned.1.call-done.refs_0_.refs_2_, bf16[1288,2048]{1,0:T(8,128)(2,1)} %constant_dynamic-update-slice_fusion.1.refs_1_.refs_3_), custom_call_target="tpu_custom_call" | custom-call | flops 11000000512 | bytes 27500000 | tf_op jit(solution)/shard_map/project_tokens/pallas_call | solution.py:378
  112.7 10.9 %scan_forward.2 = (bf16[1,1024,512]{2,1,0:T(8,128)(2,1)}, f32[1,4,128,512]{3,2,1,0:T(8,128)}, f32[1,4,8,768]{3,2,1,0:T(8,128)}) custom-call(bf16[1,1024,776]{2,1,0:T(8,128)(2,1)} %bitcast.189, f32[4,768]{1,0:T(4,128)} %pad_maximum_fusion.9.refs_1_.refs_4_, f32[1,768]{1,0:T(1,128)} %broadcast_in_dim.35.refs_2_.refs_5_, f32[8,1]{1,0:T(8,128)} %copy.69.refs_3_.refs_6_, ...), custom_call_target="tpu_custom_call" | custom-call | flops 10000000000 | bytes 25000000 | tf_op jit(solution)/shard_map/scan_forward/pallas_call | solution.py:378
  126.8 7.6 %gate_stats.2 = (f32[2,8,64,512]{3,2,1,0:T(8,128)}, f32[2,1024]{1,0:T(2,128)}) custom-call(bf16[8,2,64,2048]{3,2,1,0:T(8,128)(2,1)} %all-gather.7.cloned.1.call-done.refs_0_, bf16[512,2048]{1,0:T(8,128)(2,1)} %select_add_fusion.refs_1_.refs_5_, bf16[2,8,64,512]{3,2,1,0:T(8,128)(2,1)} %get-tuple-element.80.refs_2_.refs_0_, ...), custom_call_target="tpu_custom_call" | custom-call | flops 7000000000 | bytes 17500000 | tf_op jit(solution)/shard_map/gate_stats/pallas_call | solution.py:378
  143.9 8.7 %gate_back.2 = (bf16[512,1024]{1,0:T(8,128)(2,1)}, bf16[2,8,64,512]{3,2,1,0:T(8,128)(2,1)}, bf16[2,8,64,512]{3,2,1,0:T(8,128)(2,1)}, bf16[1024,2048]{1,0:T(8,128)(2,1)}, f32[1,512]{1,0:T(1,128)}) custom-call(bf16[2,8,64,512]{3,2,1,0:T(8,128)(2,1)} %get-tuple-element.80.refs_2_.refs_0_, bf16[2,8,64,512]{3,2,1,0:T(8,128)(2,1)} %get-tuple-element.81.refs_3_.refs_1_, ...), custom_call_target="tpu_custom_call" | custom-call | flops 8000000000 | bytes 20000000 | tf_op jit(solution)/shard_map/gate_back/pallas_call | solution.py:378
  152.8 22.2 %scan_backward.2 = (bf16[1,1024,776]{2,1,0:T(8,128)(2,1)}, f32[8,768]{1,0:T(8,128)}, f32[1,512]{1,0:T(1,128)}, f32[2,8,1]{2,1,0:T(8,128)}) custom-call(bf16[1,1024,776]{2,1,0:T(8,128)(2,1)} %bitcast.190, bf16[1,1024,512]{2,1,0:T(8,128)(2,1)} %bitcast.197, f32[1,4,128,512]{3,2,1,0:T(8,128)} %get-tuple-element.88.refs_2_, ...), custom_call_target="tpu_custom_call" | custom-call | flops 22000001024 | bytes 55000000 | tf_op jit(solution)/shard_map/scan_backward/pallas_call | solution.py:378
  175.0 11.6 %project_tokens.3 = (bf16[2,8,64,512]{3,2,1,0:T(8,128)(2,1)}, bf16[2,8,64,776]{3,2,1,0:T(8,128)(2,1)}, bf16[2,2048,512]{2,1,0:T(8,128)(2,1)}) custom-call(bf16[8,2,64,2048]{3,2,1,0:T(8,128)(2,1)} %all-gather.9.cloned.1.call-done.refs_0_.refs_2_, bf16[1288,2048]{1,0:T(8,128)(2,1)} %constant_dynamic-update-slice_fusion.1.refs_1_.refs_3_, ...), custom_call_target="tpu_custom_call" | custom-call | flops 11000000512 | bytes 27500000 | tf_op jit(solution)/shard_map/project_tokens/pallas_call | solution.py:378
  186.6 10.9 %scan_forward.3 = (bf16[1,1024,512]{2,1,0:T(8,128)(2,1)}, f32[1,4,128,512]{3,2,1,0:T(8,128)}, f32[1,4,8,768]{3,2,1,0:T(8,128)}) custom-call(bf16[1,1024,776]{2,1,0:T(8,128)(2,1)} %bitcast.183, f32[4,768]{1,0:T(4,128)} %pad_maximum_fusion.9.refs_1_.refs_4_, f32[1,768]{1,0:T(1,128)} %broadcast_in_dim.35.refs_2_.refs_5_, f32[8,1]{1,0:T(8,128)} %copy.69.refs_3_.refs_6_, ...), custom_call_target="tpu_custom_call" | custom-call | flops 10000000000 | bytes 25000000 | tf_op jit(solution)/shard_map/scan_forward/pallas_call | solution.py:378
  197.5 7.4 %gate_stats.3 = (f32[2,8,64,512]{3,2,1,0:T(8,128)}, f32[2,1024]{1,0:T(2,128)}) custom-call(bf16[8,2,64,2048]{3,2,1,0:T(8,128)(2,1)} %all-gather.11.cloned.1.call-done.refs_0_, bf16[512,2048]{1,0:T(8,128)(2,1)} %select_add_fusion.refs_1_.refs_5_, bf16[2,8,64,512]{3,2,1,0:T(8,128)(2,1)} %bitcast.195, ...), custom_call_target="tpu_custom_call" | custom-call | flops 7000000000 | bytes 17500000 | tf_op jit(solution)/shard_map/gate_stats/pallas_call | solution.py:378
  210.4 11.4 %norm_part.2 = (bf16[1024,2048]{1,0:T(8,128)(2,1)}, f32[1,2048]{1,0:T(1,128)}) custom-call(bf16[2,8,64,512]{3,2,1,0:T(8,128)(2,1)} %get-tuple-element.86.refs_0_, bf16[2,8,64,776]{3,2,1,0:T(8,128)(2,1)} %bitcast.185, bf16[8,2,64,2048]{3,2,1,0:T(8,128)(2,1)} %all-gather.5.cloned.1.call-done.refs_0_.refs_2_, ...), custom_call_target="tpu_custom_call" | custom-call | flops 11000000512 | bytes 27500000 | tf_op jit(solution)/shard_map/norm_part/pallas_call | solution.py:378
  222.5 8.9 %gate_back.3 = (bf16[512,1024]{1,0:T(8,128)(2,1)}, bf16[2,8,64,512]{3,2,1,0:T(8,128)(2,1)}, bf16[2,8,64,512]{3,2,1,0:T(8,128)(2,1)}, bf16[1024,2048]{1,0:T(8,128)(2,1)}, f32[1,512]{1,0:T(1,128)}) custom-call(bf16[2,8,64,512]{3,2,1,0:T(8,128)(2,1)} %bitcast.196, bf16[2,8,64,512]{3,2,1,0:T(8,128)(2,1)} %get-tuple-element.94.refs_3_.refs_1_, ...), custom_call_target="tpu_custom_call" | custom-call | flops 8000000000 | bytes 20000000 | tf_op jit(solution)/shard_map/gate_back/pallas_call | solution.py:378
  232.2 8.6 %row_grad.4 = bf16[2048,512]{1,0:T(8,128)(2,1)} custom-call(bf16[2,2048,512]{2,1,0:T(8,128)(2,1)} %get-tuple-element.76.refs_0_, bf16[1024,512]{1,0:T(8,128)(2,1)} %bitcast.192, bf16[2,2048,512]{2,1,0:T(8,128)(2,1)} %get-tuple-element.91.refs_2_.refs_0_, bf16[1024,512]{1,0:T(8,128)(2,1)} %bitcast.193), custom_call_target="tpu_custom_call" | custom-call | flops 8000000000 | bytes 20000000 | tf_op jit(solution)/shard_map/row_grad/pallas_call | solution.py:378
  243.6 9.6 %row_grad.5 = bf16[512,2048]{1,0:T(8,128)(2,1)} custom-call(bf16[1,512,1024]{2,1,0:T(8,128)(2,1)} %bitcast.191, bf16[1024,2048]{1,0:T(8,128)(2,1)} %bitcast.181, bf16[1,512,1024]{2,1,0:T(8,128)(2,1)} %bitcast.194, bf16[1024,2048]{1,0:T(8,128)(2,1)} %bitcast.182, bf16[16,64,512]{2,1,0:T(8,128)(2,1)} %get-tuple-element.138.refs_4_), custom_call_target="tpu_custom_call" | custom-call | flops 8000000000 | bytes 20000000 | tf_op jit(solution)/shard_map/row_grad/pallas_call | solution.py:378
  262.4 8.8 %row_grad.6.refs_4_ = f32[2048,776]{1,0:T(8,128)} custom-call(bf16[2,2048,512]{2,1,0:T(8,128)(2,1)} %get-tuple-element.76.refs_0_, bf16[1024,776]{1,0:T(8,128)(2,1)} %bitcast.186, bf16[2,128,2048]{2,1,0:T(8,128)(2,1)} %get-tuple-element.135.refs_2_), custom_call_target="tpu_custom_call" | custom-call | flops 8000000000 | bytes 20000000 | tf_op jit(solution)/shard_map/row_grad/pallas_call | solution.py:378
  274.7 22.2 %scan_backward.3 = (bf16[1,1024,776]{2,1,0:T(8,128)(2,1)}, f32[8,768]{1,0:T(8,128)}, f32[1,512]{1,0:T(1,128)}, f32[2,8,1]{2,1,0:T(8,128)}) custom-call(bf16[1,1024,776]{2,1,0:T(8,128)(2,1)} %bitcast.184, bf16[1,1024,512]{2,1,0:T(8,128)(2,1)} %bitcast.163, f32[1,4,128,512]{3,2,1,0:T(8,128)} %get-tuple-element.107.refs_2_, ...), custom_call_target="tpu_custom_call" | custom-call | flops 22000001024 | bytes 55000000 | tf_op jit(solution)/shard_map/scan_backward/pallas_call | solution.py:378
  296.9 11.5 %norm_part.3 = (bf16[1024,2048]{1,0:T(8,128)(2,1)}, f32[1,2048]{1,0:T(1,128)}) custom-call(bf16[2,8,64,512]{3,2,1,0:T(8,128)(2,1)} %get-tuple-element.99.refs_0_, bf16[2,8,64,776]{3,2,1,0:T(8,128)(2,1)} %bitcast.187, bf16[8,2,64,2048]{3,2,1,0:T(8,128)(2,1)} %all-gather.9.cloned.1.call-done.refs_0_.refs_2_, ...), custom_call_target="tpu_custom_call" | custom-call | flops 11000000512 | bytes 27500000 | tf_op jit(solution)/shard_map/norm_part/pallas_call | solution.py:378
  313.1 5.6 %all-to-all-start = ((bf16[16,64,512]{2,1,0:T(8,128)(2,1)}), bf16[16,64,512]{2,1,0:T(8,128)(2,1)}, u32[]{:S(2)}, u32[]{:S(2)}) async-start(bf16[16,64,512]{2,1,0:T(8,128)(2,1)} %add_convert_fusion.2), calls=%async_computation.4 | async-start | bytes 2097152 | tf_op jit(solution)/shard_map/all_to_all | solution.py:931
  320.0 6.3 %collective-permute-done.16.refs_2_ = bf16[64,2048]{1,0:T(8,128)(2,1)S(1)} collective-permute-done((bf16[64,2048]{1,0:T(8,128)(2,1)}, bf16[64,2048]{1,0:T(8,128)(2,1)S(1)}, u32[]{:S(2)}, u32[]{:S(2)}) %collective-permute-start.16) | collective-permute-done | bytes 262176 | tf_op jit(solution)/shard_map/ppermute | solution.py:695
  330.8 9.5 %row_grad.7 = bf16[2048,776]{1,0:T(8,128)(2,1)} custom-call(bf16[2,2048,512]{2,1,0:T(8,128)(2,1)} %get-tuple-element.91.refs_2_.refs_0_, bf16[1024,776]{1,0:T(8,128)(2,1)} %bitcast.188, f32[2048,776]{1,0:T(8,128)} %get-tuple-element.114.refs_2_, f32[1,2048]{1,0:T(1,128)} %get-tuple-element.115.refs_3_), custom_call_target="tpu_custom_call" | custom-call | flops 8000000000 | bytes 20000000 | tf_op jit(solution)/shard_map/row_grad/pallas_call | solution.py:378
  343.4 3.4 collective-permute-start.20
  351.7 10.3 %collective-permute-start.18 = (bf16[64,2048]{1,0:T(8,128)(2,1)S(1)}, bf16[64,2048]{1,0:T(8,128)(2,1)S(1)}, u32[]{:S(2)}, u32[]{:S(2)}) collective-permute-start(bf16[64,2048]{1,0:T(8,128)(2,1)S(1)} %get-tuple-element.177), channel_id=1, source_target_pairs={{0,16},{16,0},{1,17},{17,1},{2,18},{18,2},{3,19},{19,3},{4,20},{20... | collective-permute-start | bytes 786440 | tf_op jit(solution)/shard_map/ppermute | solution.py:695
  363.6 13.9 %collective-permute-done.27 = bf16[2,128,2048]{2,1,0:T(8,128)(2,1)} collective-permute-done((bf16[2,128,2048]{2,1,0:T(8,128)(2,1)S(1)}, bf16[2,128,2048]{2,1,0:T(8,128)(2,1)}, u32[]{:S(2)}, u32[]{:S(2)}) %collective-permute-start.27) | collective-permute-done | bytes 1048608 | tf_op jit(solution)/shard_map/ppermute | solution.py:1009
  380.2 5.6 %collective-permute-done.17.refs_0_ = bf16[16,64,776]{2,1,0:T(8,128)(2,1)S(1)} collective-permute-done((bf16[16,64,776]{2,1,0:T(8,128)(2,1)}, bf16[16,64,776]{2,1,0:T(8,128)(2,1)S(1)}, u32[]{:S(2)}, u32[]{:S(2)}) %collective-permute-start.17) | collective-permute-done | bytes 1589280 | tf_op jit(solution)/shard_map/ppermute | solution.py:702
  387.0 3.9 fusion
  390.9 3.9 all-to-all-start.1
  403.6 41.4 %collective-permute-done.26 = f32[28096]{0:T(1024)S(1)} collective-permute-done((f32[28096]{0:T(1024)S(1)}, f32[28096]{0:T(1024)S(1)}, u32[]{:S(2)}, u32[]{:S(2)}) %collective-permute-start.26) | collective-permute-done | bytes 112416 | tf_op jit(solution)/shard_map/ppermute | solution.py:964
  461.2 3.4 concatenate.95
  464.6 6.4 %collective-permute-done.23 = bf16[64,2048]{1,0:T(8,128)(2,1)} collective-permute-done((bf16[64,2048]{1,0:T(8,128)(2,1)}, bf16[64,2048]{1,0:T(8,128)(2,1)}, u32[]{:S(2)}, u32[]{:S(2)}) %collective-permute-start.23) | collective-permute-done | bytes 262176 | tf_op jit(solution)/shard_map/ppermute | solution.py:695
  (283 shorter events, 136.8 us)
Async XLA Ops:
  7.2 94.0 %all-gather.5.cloned.1.call-start = ((), (), s32[]{:S(2)}) async-start(), calls=%async_computation.6 | async-start | bytes 4718592 | tf_op jit(solution)/shard_map/all_gather | solution.py:718
  10.1 32.0 %collective-permute-start = (bf16[640,1024]{1,0:T(8,128)(2,1)}, bf16[640,1024]{1,0:T(8,128)(2,1)}, u32[]{:S(2)}, u32[]{:S(2)}) collective-permute-start(bf16[640,1024]{1,0:T(8,128)(2,1)} %pad_maximum_fusion.2), channel_id=1, source_target_pairs={{0,1},{1,0},{2,3},{3,2},{4,5},{5,4},{6,7},{7,6},{8,9},{9,8},{10,11... | collective-permute-start | bytes 3932168 | tf_op jit(solution)/shard_map/ppermute | solution.py:702
  16.1 25.7 %collective-permute-start.1 = (bf16[2,64,2048]{2,1,0:T(8,128)(2,1)}, bf16[2,64,2048]{2,1,0:T(8,128)(2,1)S(1)}, u32[]{:S(2)}, u32[]{:S(2)}) collective-permute-start(bf16[2,64,2048]{2,1,0:T(8,128)(2,1)} %constant_dynamic-slice_fusion.4), channel_id=1, source_target_pairs={{0,16},{16,0},{1,17},{17,1},{2,18},{18,2},{3,19},{19,3},{4,20},{20... | collective-permute-start | bytes 1572872 | tf_op jit(solution)/shard_map/ppermute | solution.py:695
  46.4 80.3 %all-gather.7.cloned.1.call-start = ((), (), s32[]{:S(2)}) async-start(), calls=%async_computation.7 | async-start | bytes 4718592 | tf_op jit(solution)/shard_map/all_gather | solution.py:718
  46.5 30.2 %collective-permute-start.2 = (bf16[648,1024]{1,0:T(8,128)(2,1)S(1)}, bf16[648,1024]{1,0:T(8,128)(2,1)}, u32[]{:S(2)}, u32[]{:S(2)}) collective-permute-start(bf16[648,1024]{1,0:T(8,128)(2,1)S(1)} %copy-done.5), channel_id=1, source_target_pairs={{0,1},{1,0},{2,3},{3,2},{4,5},{5,4},{6,7},{7,6},{8,9},{9,8},{10,11... | collective-permute-start | bytes 3981320 | tf_op jit(solution)/shard_map/ppermute | solution.py:702
  47.8 25.0 %collective-permute-start.3 = (bf16[2,64,2048]{2,1,0:T(8,128)(2,1)}, bf16[2,64,2048]{2,1,0:T(8,128)(2,1)}, u32[]{:S(2)}, u32[]{:S(2)}) collective-permute-start(bf16[2,64,2048]{2,1,0:T(8,128)(2,1)} %get-tuple-element.74), channel_id=1, source_target_pairs={{0,16},{16,0},{1,17},{17,1},{2,18},{18,2},{3,19},{19,3},{4,20},{20... | collective-permute-start | bytes 1572872 | tf_op jit(solution)/shard_map/ppermute | solution.py:695
  79.8 95.3 %all-gather.9.cloned.1.call-start = ((), (), s32[]{:S(2)}) async-start(), calls=%async_computation.8 | async-start | bytes 4718592 | tf_op jit(solution)/shard_map/all_gather | solution.py:718
  80.7 116.7 %all-gather.11.cloned.1.call-start = ((), (), s32[]{:S(2)}) async-start(), calls=%async_computation.9 | async-start | bytes 4718592 | tf_op jit(solution)/shard_map/all_gather | solution.py:718
  81.7 176.2 %reduce-scatter.5.cloned.1.call-start = ((), (), s32[]{:S(2)}) async-start(), calls=%async_computation.10 | async-start | bytes 4718592 | tf_op jit(solution)/shard_map/reduce_scatter | solution.py:728
  94.1 29.5 %collective-permute-start.4 = (bf16[512,2048]{1,0:T(8,128)(2,1)S(1)}, bf16[512,2048]{1,0:T(8,128)(2,1)}, u32[]{:S(2)}, u32[]{:S(2)}) collective-permute-start(bf16[512,2048]{1,0:T(8,128)(2,1)S(1)} %copy-done), channel_id=1, source_target_pairs={{0,1},{3,2},{4,5},{7,6},{8,9},{11,10},{12,13},{15,14},{16,17},{19,... | collective-permute-start | bytes 6291464 | tf_op jit(solution)/shard_map/ppermute | solution.py:822
  152.6 155.9 %reduce-scatter.7.cloned.1.call-start = ((), (), s32[]{:S(2)}) async-start(), calls=%async_computation.11 | async-start | bytes 4718592 | tf_op jit(solution)/shard_map/reduce_scatter | solution.py:728
  206.9 14.9 %collective-permute-start.12 = (f32[2,1024]{1,0:T(2,128)S(1)}, f32[2,1024]{1,0:T(2,128)S(1)}, u32[]{:S(2)}, u32[]{:S(2)}) collective-permute-start(f32[2,1024]{1,0:T(2,128)S(1)} %add.223), channel_id=1, source_target_pairs={{0,12},{4,8},{8,4},{12,0},{1,13},{5,9},{9,5},{13,1},{2,14},{6,10},... | collective-permute-start | bytes 24584 | tf_op jit(solution)/shard_map/ppermute | solution.py:698
  208.4 13.4 %collective-permute-start.11 = (f32[2,1024]{1,0:T(2,128)S(1)}, f32[2,1024]{1,0:T(2,128)S(1)}, u32[]{:S(2)}, u32[]{:S(2)}) collective-permute-start(f32[2,1024]{1,0:T(2,128)S(1)} %add.223), channel_id=1, source_target_pairs={{0,8},{4,12},{8,0},{12,4},{1,9},{5,13},{9,1},{13,5},{2,10},{6,14},... | collective-permute-start | bytes 24584 | tf_op jit(solution)/shard_map/ppermute | solution.py:698
  208.9 12.9 %collective-permute-start.10 = (f32[2,1024]{1,0:T(2,128)S(1)}, f32[2,1024]{1,0:T(2,128)S(1)}, u32[]{:S(2)}, u32[]{:S(2)}) collective-permute-start(f32[2,1024]{1,0:T(2,128)S(1)} %add.223), channel_id=1, source_target_pairs={{0,4},{4,0},{8,12},{12,8},{1,5},{5,1},{9,13},{13,9},{2,6},{6,2},{1... | collective-permute-start | bytes 24584 | tf_op jit(solution)/shard_map/ppermute | solution.py:698
  231.4 115.4 %reduce-scatter.9.cloned.1.call-start = ((), (), s32[]{:S(2)}) async-start(), calls=%async_computation.12 | async-start | bytes 4718592 | tf_op jit(solution)/shard_map/reduce_scatter | solution.py:728
  232.2 223.5 %reduce-scatter.11.cloned.1.call-start = ((), (), s32[]{:S(2)}) async-start(), calls=%async_computation.13 | async-start | bytes 4718592 | tf_op jit(solution)/shard_map/reduce_scatter | solution.py:728
  243.6 27.9 %collective-permute-start.13 = (bf16[16,64,512]{2,1,0:T(8,128)(2,1)S(1)}, bf16[16,64,512]{2,1,0:T(8,128)(2,1)S(1)}, u32[]{:S(2)}, u32[]{:S(2)}) collective-permute-start(bf16[16,64,512]{2,1,0:T(8,128)(2,1)S(1)} %get-tuple-element.137), channel_id=1, source_target_pairs={{0,1},{1,0},{2,3},{3,2},{4,5},{5,4},{6,7},{7,6},{8,9},{9,8},{10,11... | collective-permute-start | bytes 3145736 | tf_op jit(solution)/shard_map/ppermute | solution.py:702
  255.9 64.1 %collective-permute-start.15 = (bf16[2,128,2048]{2,1,0:T(8,128)(2,1)S(1)}, bf16[2,128,2048]{2,1,0:T(8,128)(2,1)}, u32[]{:S(2)}, u32[]{:S(2)}) collective-permute-start(bf16[2,128,2048]{2,1,0:T(8,128)(2,1)S(1)} %get-tuple-element.136), channel_id=1, source_target_pairs={{0,1},{1,0},{2,3},{3,2},{4,5},{5,4},{6,7},{7,6},{8,9},{9,8},{10,11... | collective-permute-start | bytes 3145736 | tf_op jit(solution)/shard_map/ppermute | solution.py:702
  259.8 14.2 %collective-permute-start.14 = (bf16[64,2048]{1,0:T(8,128)(2,1)}, bf16[64,2048]{1,0:T(8,128)(2,1)S(1)}, u32[]{:S(2)}, u32[]{:S(2)}) collective-permute-start(bf16[64,2048]{1,0:T(8,128)(2,1)} %get-tuple-element.179), channel_id=1, source_target_pairs={{0,16},{16,0},{1,17},{17,1},{2,18},{18,2},{3,19},{19,3},{4,20},{20... | collective-permute-start | bytes 786440 | tf_op jit(solution)/shard_map/ppermute | solution.py:695
  310.5 15.8 %collective-permute-start.16 = (bf16[64,2048]{1,0:T(8,128)(2,1)}, bf16[64,2048]{1,0:T(8,128)(2,1)S(1)}, u32[]{:S(2)}, u32[]{:S(2)}) collective-permute-start(bf16[64,2048]{1,0:T(8,128)(2,1)} %get-tuple-element.181), channel_id=1, source_target_pairs={{0,16},{16,0},{1,17},{17,1},{2,18},{18,2},{3,19},{19,3},{4,20},{20... | collective-permute-start | bytes 786440 | tf_op jit(solution)/shard_map/ppermute | solution.py:695
  313.1 77.7 %all-to-all-start = ((bf16[16,64,512]{2,1,0:T(8,128)(2,1)}), bf16[16,64,512]{2,1,0:T(8,128)(2,1)}, u32[]{:S(2)}, u32[]{:S(2)}) async-start(bf16[16,64,512]{2,1,0:T(8,128)(2,1)} %add_convert_fusion.2), calls=%async_computation.4 | async-start | bytes 2097152 | tf_op jit(solution)/shard_map/all_to_all | solution.py:931
  327.8 15.4 %collective-permute-start.19 = (f32[28096]{0:T(1024)S(1)}, f32[28096]{0:T(1024)S(1)}, u32[]{:S(2)}, u32[]{:S(2)}) collective-permute-start(f32[28096]{0:T(1024)S(1)} %concatenate.93), channel_id=1, source_target_pairs={{0,2},{2,0},{1,3},{3,1},{4,6},{6,4},{5,7},{7,5},{8,10},{10,8},{9,1... | collective-permute-start | bytes 337160 | tf_op jit(solution)/shard_map/ppermute | solution.py:692
  329.5 48.0 %collective-permute-start.27 = (bf16[2,128,2048]{2,1,0:T(8,128)(2,1)S(1)}, bf16[2,128,2048]{2,1,0:T(8,128)(2,1)}, u32[]{:S(2)}, u32[]{:S(2)}) collective-permute-start(bf16[2,128,2048]{2,1,0:T(8,128)(2,1)S(1)} %add_convert_fusion.1), channel_id=1, source_target_pairs={{16,0},{20,4},{24,8},{28,12},{2,18},{6,22},{10,26},{14,30},{17,1},... | collective-permute-start | bytes 3145736 | tf_op jit(solution)/shard_map/ppermute | solution.py:1009
  343.2 42.6 %collective-permute-start.17 = (bf16[16,64,776]{2,1,0:T(8,128)(2,1)}, bf16[16,64,776]{2,1,0:T(8,128)(2,1)S(1)}, u32[]{:S(2)}, u32[]{:S(2)}) collective-permute-start(bf16[16,64,776]{2,1,0:T(8,128)(2,1)} %dynamic-slice_bitcast_fusion), channel_id=1, source_target_pairs={{0,1},{1,0},{2,3},{3,2},{4,5},{5,4},{6,7},{7,6},{8,9},{9,8},{10,11... | collective-permute-start | bytes 4767752 | tf_op jit(solution)/shard_map/ppermute | solution.py:702
  343.3 18.7 %collective-permute-start.21 = (f32[28096]{0:T(1024)S(1)}, f32[28096]{0:T(1024)S(1)}, u32[]{:S(2)}, u32[]{:S(2)}) collective-permute-start(f32[28096]{0:T(1024)S(1)} %add.239), channel_id=1, source_target_pairs={{0,8},{4,12},{8,0},{12,4},{1,9},{5,13},{9,1},{13,5},{2,10},{6,14},... | collective-permute-start | bytes 337160 | tf_op jit(solution)/shard_map/ppermute | solution.py:698
  343.4 18.6 %collective-permute-start.20 = (f32[28096]{0:T(1024)S(1)}, f32[28096]{0:T(1024)}, u32[]{:S(2)}, u32[]{:S(2)}) collective-permute-start(f32[28096]{0:T(1024)S(1)} %add.239), channel_id=1, source_target_pairs={{0,4},{4,0},{8,12},{12,8},{1,5},{5,1},{9,13},{13,9},{2,6},{6,2},{1... | collective-permute-start | bytes 337160 | tf_op jit(solution)/shard_map/ppermute | solution.py:698
  351.7 28.5 %collective-permute-start.18 = (bf16[64,2048]{1,0:T(8,128)(2,1)S(1)}, bf16[64,2048]{1,0:T(8,128)(2,1)S(1)}, u32[]{:S(2)}, u32[]{:S(2)}) collective-permute-start(bf16[64,2048]{1,0:T(8,128)(2,1)S(1)} %get-tuple-element.177), channel_id=1, source_target_pairs={{0,16},{16,0},{1,17},{17,1},{2,18},{18,2},{3,19},{19,3},{4,20},{20... | collective-permute-start | bytes 786440 | tf_op jit(solution)/shard_map/ppermute | solution.py:695
  390.9 62.5 %all-to-all-start.1 = ((bf16[16,64,776]{2,1,0:T(8,128)(2,1)}), bf16[16,64,776]{2,1,0:T(8,128)(2,1)S(1)}, u32[]{:S(2)}, u32[]{:S(2)}) async-start(bf16[16,64,776]{2,1,0:T(8,128)(2,1)} %fusion), calls=%async_computation.5 | async-start | bytes 3670016 | tf_op jit(solution)/shard_map/all_to_all | solution.py:931
  398.1 47.0 %collective-permute-start.26 = (f32[28096]{0:T(1024)S(1)}, f32[28096]{0:T(1024)S(1)}, u32[]{:S(2)}, u32[]{:S(2)}) collective-permute-start(f32[28096]{0:T(1024)S(1)} %copy-done.28), channel_id=1, source_target_pairs={{0,17},{1,16},{16,1},{17,0},{2,19},{3,18},{18,3},{19,2},{4,21},{5,... | collective-permute-start | bytes 337160 | tf_op jit(solution)/shard_map/ppermute | solution.py:964
  399.1 45.9 %collective-permute-start.25 = (f32[28096]{0:T(1024)S(1)}, f32[28096]{0:T(1024)S(1)}, u32[]{:S(2)}, u32[]{:S(2)}) collective-permute-start(f32[28096]{0:T(1024)S(1)} %copy-done.28), channel_id=1, source_target_pairs={{0,1},{1,0},{2,3},{3,2},{4,5},{5,4},{6,7},{7,6},{8,9},{9,8},{10,11... | collective-permute-start | bytes 337160 | tf_op jit(solution)/shard_map/ppermute | solution.py:962
  401.4 46.5 %collective-permute-start.24 = (f32[28096]{0:T(1024)S(1)}, f32[28096]{0:T(1024)S(1)}, u32[]{:S(2)}, u32[]{:S(2)}) collective-permute-start(f32[28096]{0:T(1024)S(1)} %copy-done.28), channel_id=1, source_target_pairs={{0,16},{1,17},{16,0},{17,1},{2,18},{3,19},{18,2},{19,3},{4,20},{5,... | collective-permute-start | bytes 337160 | tf_op jit(solution)/shard_map/ppermute | solution.py:964
  457.4 13.7 %collective-permute-start.23 = (bf16[64,2048]{1,0:T(8,128)(2,1)}, bf16[64,2048]{1,0:T(8,128)(2,1)}, u32[]{:S(2)}, u32[]{:S(2)}) collective-permute-start(bf16[64,2048]{1,0:T(8,128)(2,1)} %get-tuple-element.176), channel_id=1, source_target_pairs={{0,16},{16,0},{1,17},{17,1},{2,18},{18,2},{3,19},{19,3},{4,20},{20... | collective-permute-start | bytes 786440 | tf_op jit(solution)/shard_map/ppermute | solution.py:695
  (60 other events, 286.4 us)
Sparse Core Ops, SparseCore 0:
  46.5 39.7 all-gather.4
  88.5 30.4 all-gather.6
  120.6 29.4 all-gather.8
  151.6 29.1 all-gather.10
  182.9 47.6 reduce-scatter.4
  232.8 49.3 reduce-scatter.6
  284.4 60.1 reduce-scatter.8
  346.9 65.2 reduce-scatter.10

commit v3 on v2

--- a/solution.py
+++ b/solution.py
@@ -85,6 +85,7 @@
 
 def scan_forward_body(
     heads,
+    half_ref,
     raw_ref,
     taps_ref,
     bias_ref,
@@ -151,21 +152,23 @@
     state[...] = held * grown_wide[span - 1 : span, :] + fresh
 
 
-def scan_forward(raw, at, taps, bias, shift, log_rate, skip_wide, wait=()):
+def scan_forward(half, raw, at, taps, bias, shift, log_rate, skip_wide, wait=()):
     _, length, width = raw.shape
     seqs = 1
     heads = shift.shape[0]
     inner = heads * HEADDIM
     wide = inner + 2 * STATE
     spans = length // SPAN
-    whole = lambda shape: pl.BlockSpec(shape, lambda s, i: (0,) * len(shape))
+    whole = lambda shape: pl.BlockSpec(shape, lambda s, i, t: (0,) * len(shape))
+    lies = lambda i, t: (i + t[0] * (spans // 2)) % spans
     return call_after(
         wait,
         functools.partial(scan_forward_body, heads),
-        (raw, taps, bias, shift, log_rate, skip_wide),
+        (half, raw, taps, bias, shift, log_rate, skip_wide),
+        scalars=1,
         grid=(seqs, spans),
         in_specs=[
-            pl.BlockSpec((None, SPAN, width), lambda s, i: (at, i, 0)),
+            pl.BlockSpec((None, SPAN, width), lambda s, i, t: (at, lies(i, t), 0)),
             whole(taps.shape),
             whole(bias.shape),
             whole(shift.shape),
@@ -173,9 +176,9 @@
             whole(skip_wide.shape),
         ],
         out_specs=[
-            pl.BlockSpec((None, SPAN, inner), lambda s, i: (s, i, 0)),
-            pl.BlockSpec((None, None, STATE, inner), lambda s, i: (s, i, 0, 0)),
-            pl.BlockSpec((None, None, 8, wide), lambda s, i: (s, i, 0, 0)),
+            pl.BlockSpec((None, SPAN, inner), lambda s, i, t: (s, lies(i, t), 0)),
+            pl.BlockSpec((None, None, STATE, inner), lambda s, i, t: (s, i, 0, 0)),
+            pl.BlockSpec((None, None, 8, wide), lambda s, i, t: (s, i, 0, 0)),
         ],
         out_shape=[
             jax.ShapeDtypeStruct((seqs, length, inner), BF16),
@@ -191,6 +194,7 @@
 
 def scan_backward_body(
     heads,
+    half_ref,
     raw_ref,
     down_ref,
     start_ref,
@@ -318,25 +322,27 @@
     return jnp.concatenate([columns, jnp.zeros((span, 128 - heads), F32)], 1).T[:heads]
 
 
-def scan_backward(raw, at, down, starts, edges, taps, bias, shift, log_rate, skip_wide, wait=()):
+def scan_backward(half, raw, at, down, starts, edges, taps, bias, shift, log_rate, skip_wide, wait=()):
     _, length, width = raw.shape
     seqs = 1
     heads = shift.shape[0]
     inner = heads * HEADDIM
     wide = inner + 2 * STATE
     spans = length // SPAN
-    whole = lambda shape: pl.BlockSpec(shape, lambda s, i: (0,) * len(shape))
-    turned = lambda s, i: (s, spans - 1 - i, 0)
+    whole = lambda shape: pl.BlockSpec(shape, lambda s, i, t: (0,) * len(shape))
+    lies = lambda i, t: (spans - 1 - i + t[0] * (spans // 2)) % spans
+    turned = lambda s, i, t: (s, lies(i, t), 0)
     return call_after(
         wait,
         functools.partial(scan_backward_body, heads),
-        (raw, down, starts, edges, taps, bias, shift, log_rate, skip_wide),
+        (half, raw, down, starts, edges, taps, bias, shift, log_rate, skip_wide),
+        scalars=1,
         grid=(seqs, spans),
         in_specs=[
-            pl.BlockSpec((None, SPAN, width), lambda s, i: (at, spans - 1 - i, 0)),
+            pl.BlockSpec((None, SPAN, width), lambda s, i, t: (at, lies(i, t), 0)),
             pl.BlockSpec((None, SPAN, inner), turned),
-            pl.BlockSpec((None, None, STATE, inner), lambda s, i: (s, spans - 1 - i, 0, 0)),
-            pl.BlockSpec((None, None, 8, wide), lambda s, i: (s, spans - 1 - i, 0, 0)),
+            pl.BlockSpec((None, None, STATE, inner), lambda s, i, t: (s, spans - 1 - i, 0, 0)),
+            pl.BlockSpec((None, None, 8, wide), lambda s, i, t: (s, spans - 1 - i, 0, 0)),
             whole(taps.shape),
             whole(bias.shape),
             whole(shift.shape),
@@ -369,13 +375,23 @@
     return pltpu.CompilerParams(vmem_limit_bytes=58 * 1024 * 1024)
 
 
-def call_after(wait, body, values, in_specs, **rest):
+def call_after(wait, body, values, in_specs, scalars=0, **rest):
     held = [pl.BlockSpec(memory_space=pl.ANY)] * len(wait)
 
     def inner_body(*refs):
         body(*refs[: len(values)], *refs[len(values) + len(wait) :])
 
-    return pl.pallas_call(inner_body, in_specs=list(in_specs) + held, **rest)(*values, *wait)
+    if scalars:
+        rest["grid_spec"] = pltpu.PrefetchScalarGridSpec(
+            num_scalar_prefetch=scalars,
+            grid=rest.pop("grid"),
+            in_specs=list(in_specs) + held,
+            out_specs=rest.pop("out_specs"),
+            scratch_shapes=rest.pop("scratch_shapes"),
+        )
+    else:
+        rest["in_specs"] = list(in_specs) + held
+    return pl.pallas_call(inner_body, **rest)(*values, *wait)
 
 
 def light_cost(micros):
@@ -383,35 +399,45 @@
     return pl.CostEstimate(flops=work, bytes_accessed=work // 400, transcendentals=0)
 
 
-def project_body(inner, tokens_ref, weight_ref, gate_ref, raw_ref, turned_ref):
-    _, _, tokens, model = tokens_ref.shape
-    values = tokens_ref[...].reshape(4 * tokens, model)
+def both_parts(near_ref, far_ref):
+    return jnp.concatenate(
+        [ref[member] for member in range(near_ref.shape[0]) for ref in (near_ref, far_ref)], 0
+    )
+
+
+def gathered(values, at):
+    _, _, tokens, width = values.shape
+    return pl.BlockSpec((2, None, tokens, width), lambda i: (i, at, 0, 0))
+
+
+def project_body(inner, near_ref, far_ref, weight_ref, gate_ref, raw_ref, turned_ref):
+    values = both_parts(near_ref, far_ref)
     put_by_member(gate_ref, dot_lanes(values, weight_ref[:inner, :]))
     put_by_member(raw_ref, dot_lanes(values, weight_ref[inner:, :]))
-    for half in range(2):
-        pair = jnp.concatenate([tokens_ref[core, half] for core in range(2)], 0)
-        turned_ref[half] = pair.T
-
-
-def project_tokens(values, weight, inner, wait=()):
-    team, _, tokens, model = values.shape
+    for half, ref in enumerate((near_ref, far_ref)):
+        turned_ref[half] = jnp.concatenate([ref[0], ref[1]], 0).T
+
+
+def project_tokens(near, far, at, weight, inner, wait=()):
+    team, _, tokens, model = near.shape
     width = weight.shape[0]
 
-    def natural(size):
+    def halves(size):
         return pl.BlockSpec((2, 2, tokens, size), lambda i: (0, i, 0, 0))
 
     return call_after(
         wait,
         functools.partial(project_body, inner),
-        (values, weight),
+        (near, far, weight),
         grid=(team // 2,),
         in_specs=[
-            pl.BlockSpec((2, 2, tokens, model), lambda i: (i, 0, 0, 0)),
+            gathered(near, at),
+            gathered(far, at),
             pl.BlockSpec((width, model), lambda i: (0, 0)),
         ],
         out_specs=[
-            natural(inner),
-            natural(width - inner),
+            halves(inner),
+            halves(width - inner),
             pl.BlockSpec((2, model, 2 * tokens), lambda i: (0, 0, i)),
         ],
         out_shape=[
@@ -439,9 +465,8 @@
             ref[half, member] = rows[at : at + tokens].astype(ref.dtype)
 
 
-def gate_stats_body(grad_ref, weight_ref, mixed_ref, gate_ref, gain_ref, down_ref, sums_ref):
-    pair, _, tokens, model = grad_ref.shape
-    d_gated = dot_lanes(grad_ref[...].reshape(pair * 2 * tokens, model), weight_ref[...])
+def gate_stats_body(near_ref, far_ref, weight_ref, mixed_ref, gate_ref, gain_ref, down_ref, sums_ref):
+    d_gated = dot_lanes(both_parts(near_ref, far_ref), weight_ref[...])
     gate = by_member(gate_ref).astype(F32)
     unit = by_member(mixed_ref).astype(F32) * gate * sigmoid(gate)
     put_by_member(down_ref, d_gated)
@@ -450,8 +475,8 @@
     sums_ref[...] = as_columns_back(jnp.concatenate([square, cross], 1))
 
 
-def gate_stats(grad, weight, mixed, gate, gain, wait=()):
-    team, _, tokens, model = grad.shape
+def gate_stats(near, near_at, far, far_at, weight, mixed, gate, gain, wait=()):
+    team, _, tokens, model = near.shape
     inner = weight.shape[0]
     pair = 2
     rows = pair * 2 * tokens
@@ -459,10 +484,11 @@
     return call_after(
         wait,
         gate_stats_body,
-        (grad, weight, mixed, gate, gain),
+        (near, far, weight, mixed, gate, gain),
         grid=(team // pair,),
         in_specs=[
-            pl.BlockSpec((pair, 2, tokens, model), lambda i: (i, 0, 0, 0)),
+            gathered(near, near_at),
+            gathered(far, far_at),
             pl.BlockSpec((inner, model), lambda i: (0, 0)),
             natural,
             natural,
@@ -511,7 +537,10 @@
     unit = mixed * act
     scaled = unit * scale
     gated_wide = scaled * gain
-    turned_ref[...] = gated_wide.T.astype(BF16)
+    tokens = mixed_ref.shape[2]
+    for half in range(2):
+        rows = [gated_wide[(2 * m + half) * tokens : (2 * m + half + 1) * tokens] for m in range(2)]
+        turned_ref[half] = jnp.concatenate(rows, 0).T.astype(BF16)
     out_ref[...] = dot_plain(gated_wide.astype(BF16), weight_ref[...]).astype(BF16)
     d_unit = down * gain * scale - unit * pull
     put_by_member(d_mixed_ref, d_unit * act)
@@ -539,14 +568,14 @@
             pl.BlockSpec((inner, model), lambda i: (0, 0)),
         ],
         out_specs=[
-            pl.BlockSpec((inner, rows), lambda i: (0, i)),
+            pl.BlockSpec((2, inner, 2 * tokens), lambda i: (0, 0, i)),
             natural,
             natural,
             pl.BlockSpec((rows, model), lambda i: (i, 0)),
             one,
         ],
         out_shape=[
-            jax.ShapeDtypeStruct((inner, team * 2 * tokens), BF16),
+            jax.ShapeDtypeStruct((2, inner, team * tokens), BF16),
             jax.ShapeDtypeStruct((2, team, tokens, inner), BF16),
             jax.ShapeDtypeStruct((2, team, tokens, inner), BF16),
             jax.ShapeDtypeStruct((team * 2 * tokens, model), BF16),
@@ -603,12 +632,12 @@
         out_specs=pl.BlockSpec((tile, got), lambda i: (i, 0)),
         out_shape=jax.ShapeDtypeStruct((rows, got), kind),
         compiler_params=kernel_params(),
-        cost_estimate=light_cost(8),
+        cost_estimate=light_cost(0),
         name="row_grad",
     )
 
 
-def norm_part_body(d_gate_ref, d_raw_ref, normed_ref, weight_ref, out_ref, gain_ref):
+def norm_part_body(d_gate_ref, d_raw_ref, near_ref, far_ref, weight_ref, out_ref, gain_ref):
     @pl.when(pl.program_id(0) == 0)
     def _():
         gain_ref[...] = jnp.zeros_like(gain_ref)
@@ -616,12 +645,12 @@
     inner = d_gate_ref.shape[-1]
     part = dot_plain(by_member(d_gate_ref), weight_ref[:inner, :])
     part = part + dot_plain(by_member(d_raw_ref), weight_ref[inner:, :])
-    normed = normed_ref[...].reshape(out_ref.shape).astype(F32)
+    normed = both_parts(near_ref, far_ref).astype(F32)
     gain_ref[...] += jnp.sum(part * normed, axis=0, keepdims=True)
     out_ref[...] = part.astype(BF16)
 
 
-def norm_part(d_gate, d_raw, normed, weight, wait=()):
+def norm_part(d_gate, d_raw, near, far, at, weight, wait=()):
     _, team, tokens, inner = d_gate.shape
     width = d_raw.shape[-1]
     model = weight.shape[1]
@@ -633,12 +662,13 @@
     return call_after(
         wait,
         norm_part_body,
-        (d_gate, d_raw, normed, weight),
+        (d_gate, d_raw, near, far, weight),
         grid=(team // 2,),
         in_specs=[
             natural(inner),
             natural(width),
-            pl.BlockSpec((2, 2, tokens, model), lambda i: (i, 0, 0, 0)),
+            gathered(near, at),
+            gathered(far, at),
             pl.BlockSpec((inner + width, model), lambda i: (0, 0)),
         ],
         out_specs=[
@@ -650,9 +680,71 @@
             jax.ShapeDtypeStruct((1, model), F32),
         ],
         compiler_params=kernel_params(),
-        cost_estimate=light_cost(11),
+        cost_estimate=light_cost(0),
         name="norm_part",
     )
+
+
+def out_grad_body(seqs, *refs):
+    lefts = refs[:seqs]
+    near_ref, far_ref, out_ref = refs[seqs:]
+    depth = lefts[0].shape[2]
+    tile = out_ref.shape[1]
+    total = None
+    for s in range(seqs):
+        for half, ref in enumerate((near_ref, far_ref)):
+            term = dot_plain(lefts[s][half], ref[:, s].reshape(depth, tile))
+            total = term if total is None else total + term
+    out_ref[...] = total.astype(out_ref.dtype)
+
+
+def out_grad_part(lefts, near, far, wait=()):
+    team, seqs, tokens, model = near.shape
+    inner = lefts[0].shape[1]
+    tile = 256
+    part = pl.BlockSpec((team, seqs, tokens, tile), lambda i: (0, 0, 0, i))
+    return call_after(
+        wait,
+        functools.partial(out_grad_body, seqs),
+        (*lefts, near, far),
+        grid=(model // tile,),
+        in_specs=[pl.BlockSpec(left.shape, lambda i: (0, 0, 0)) for left in lefts] + [part, part],
+        out_specs=pl.BlockSpec((inner, tile), lambda i: (0, i)),
+        out_shape=jax.ShapeDtypeStruct((inner, model), BF16),
+        compiler_params=kernel_params(),
+        cost_estimate=light_cost(8),
+        name="out_grad_part",
+    )
+
+
+def owned_rows_body(order, inner, gate_ref, scan_ref, out_ref):
+    team = len(order)
+    width = scan_ref.shape[-1]
+    steps = width - inner - 2 * STATE
+    shared = None
+    for place, member in enumerate(order):
+        gate = gate_ref[0, member].astype(F32) + gate_ref[1, member].astype(F32)
+        scan = scan_ref[0, member].astype(F32) + scan_ref[1, member].astype(F32)
+        out_ref[:, place * inner : (place + 1) * inner] = gate
+        out_ref[:, (team + place) * inner : (team + place + 1) * inner] = scan[:, :inner]
+        term = scan[:, inner : inner + 2 * STATE]
+        shared = term if shared is None else shared + term
+        at = 2 * team * inner + 2 * STATE + place * steps
+        out_ref[:, at : at + steps] = scan[:, inner + 2 * STATE :]
+    out_ref[:, 2 * team * inner : 2 * team * inner + 2 * STATE] = shared
+
+
+def owned_rows(order, gate, scan):
+    _, team, rows, inner = gate.shape
+    steps = scan.shape[-1] - inner - 2 * STATE
+    total = team * (2 * inner + steps) + 2 * STATE
+    return pl.pallas_call(
+        functools.partial(owned_rows_body, order, inner),
+        out_shape=jax.ShapeDtypeStruct((rows, total), F32),
+        compiler_params=kernel_params(),
+        cost_estimate=light_cost(3),
+        name="owned_rows",
+    )(gate, scan)
 
 
 TEAM = ("chip", "core")
@@ -713,9 +805,8 @@
     return keep, away
 
 
-def team_gather(keep, came, lay):
-    pair = jnp.where(lay.half == 0, jnp.stack([keep, came]), jnp.stack([came, keep]))
-    return lax.all_gather(pair, TEAM, axis=0)
+def team_gather(values):
+    return lax.all_gather(values, TEAM, axis=0)
 
 
 def both_halves(mine, other, lay):
@@ -724,24 +815,23 @@
     return jnp.concatenate([first, second], 0)
 
 
-def team_sum(part, lay):
+def team_sum(part):
     own = lax.psum_scatter(part, TEAM, scatter_dimension=0, tiled=True)
     return own.reshape(2, own.shape[0] // 2, own.shape[1])
 
 
 def two_halves(own, lay):
-    return pick(own, lay.half, 0), lay.other_half(pick(own, 1 - lay.half, 0))
+    return own[0], lay.other_half(own[1])
 
 
 def columns_in_place(local, came, lay):
-    wide = local.shape[1]
-    full = jnp.zeros((local.shape[0], lay.wsh * wide), local.dtype)
-    full = lax.dynamic_update_slice_in_dim(full, local, lay.wplace * wide, 1)
-    for start, pieces in came:
-        for shift, piece in enumerate(pieces):
-            at = ((lay.wplace - shift - 1) % lay.wsh) * wide
-            full = lax.dynamic_update_slice(full, piece, (start, at))
-    return full
+    blocks = []
+    for place in range(lay.wsh):
+        block = local
+        for shift, piece in enumerate(came):
+            block = jnp.where((lay.wplace - shift - 1) % lay.wsh == place, piece, block)
+        blocks.append(block)
+    return jnp.concatenate(blocks, 1)
 
 
 def team_parts(values, lay):
@@ -804,13 +894,17 @@
     came_first, came, later, away_grad = join(
         to_wsh(local[:cut]), lay.other_half(away), local[cut:], away_grad
     )
-    normeds = [team_gather(keep[0], came[0], lay)]
+    normed_near = team_gather(keep)
+    normed_far = team_gather(came)
     rows_held = INNER // lay.wsh
     owner = (block * inner) // rows_held
     at_row = jnp.where(owner == lay.wplace, block * inner - owner * rows_held, 0)
     rows_here = columns(out_proj, at_row, inner, 0)
-    came_last, came_grad, rows_here = join(to_wsh(later), lay.other_half(away_grad), rows_here)
-    weight = columns_in_place(local, [(0, came_first), (cut, came_last)], lay)
+    came_last, came_grad, rows_here, normed_near = join(
+        to_wsh(later), lay.other_half(away_grad), rows_here, normed_near
+    )
+    pieces = [jnp.concatenate(parts, 0) for parts in zip(came_first, came_last)]
+    weight = columns_in_place(local, pieces, lay)
     out_pieces = []
     for shift in range(1, lay.wsh):
         pairs = []
@@ -827,11 +921,6 @@
             total = total + piece
         return total
 
-    grads = [team_gather(keep_grad[0], came_grad[0], lay)]
-    for s in range(1, count):
-        normeds.append(team_gather(keep[s], came[s], lay))
-        grads.append(team_gather(keep_grad[s], came_grad[s], lay))
-
     taps = jnp.concatenate(
         [columns(conv_weight, block * inner, inner), conv_weight[:, INNER:]], 1
     )
@@ -841,6 +930,11 @@
     skip_own = jnp.repeat(columns(d_skip, block * heads, heads, 0), HEADDIM)[None]
     gain_own = columns(gate_gain, block * inner, inner, 0)[None]
     params = (taps, bias[None], shift_own, rate_own, skip_own)
+    normed_far, keep_grad, came_grad, weight, params, gain_own = join(
+        normed_far, keep_grad, came_grad, weight, params, gain_own
+    )
+    grad_near = team_gather(keep_grad)
+    grad_far = team_gather(came_grad)
 
     kernel = conv_weight.shape[0]
     shapes = [norm_gain.shape, conv_weight.shape, conv_bias.shape]
@@ -852,16 +946,35 @@
             full, values, block * values.shape[-1], values.ndim - 1
         )
 
-    def pack_small(norm_gain1):
+    def own_small(norm_gain1):
         d_taps, d_skip_wide, d_head = jax.tree.map(lambda *v: sum(v[1:], v[0]), *small_scan)
+        parts = [
+            (norm_gain0 + norm_gain1)[0] / norm_gain,
+            d_taps[: kernel + 1],
+            d_head[:, :, 0],
+            d_skip_wide.reshape(heads, HEADDIM).sum(1),
+            (gain0 + gain1)[0],
+        ]
+        return jnp.concatenate([p.reshape(-1) for p in parts])
+
+    def pack_small(own):
+        sizes = [model, (kernel + 1) * (inner + 2 * STATE), 2 * heads, heads, inner]
+        pieces, at = [], 0
+        for size in sizes:
+            pieces.append(own[at : at + size])
+            at += size
+        gain, d_taps, d_head, d_skip, d_gain = pieces
+        d_taps = d_taps.reshape(kernel + 1, inner + 2 * STATE)
+        d_taps = jnp.concatenate([placed(d_taps[:, :inner], INNER), d_taps[:, inner:]], 1)
+        d_head = placed(d_head.reshape(2, heads), dt_bias.shape[0])
         small = [
-            (norm_gain0 + norm_gain1)[0] / norm_gain,
-            jnp.concatenate([placed(d_taps[:kernel, :inner], INNER), d_taps[:kernel, inner:]], 1),
-            jnp.concatenate([placed(d_taps[kernel, :inner], INNER), d_taps[kernel, inner:]], 0),
-            placed(d_head[1, :, 0], dt_bias.shape[0]),
-            placed(d_head[0, :, 0], a_log.shape[0]),
-            placed(d_skip_wide.reshape(heads, HEADDIM).sum(1), d_skip.shape[0]),
-            placed((gain0 + gain1)[0], INNER),
+            gain,
+            d_taps[:kernel],
+            d_taps[kernel],
+            d_head[1],
+            d_head[0],
+            placed(d_skip, dt_bias.shape[0]),
+            placed(d_gain, INNER),
         ]
         return jnp.concatenate([s.reshape(-1) for s in small])
 
@@ -877,6 +990,7 @@
 
     team = lay.team
     natural = (2, team, tokens)
+    half_at = lay.half[None].astype(jnp.int32)
     out_rows = INNER // (lay.parts * lay.wsh)
     in_rows = model // (lay.parts * lay.wsh)
 
@@ -885,19 +999,21 @@
     turned_gated, d_gates, d_raws, small_scan = [], [], [], []
 
     def project_step(at, wait=()):
-        gate, raw, flat = project_tokens(normeds[at], weight, inner, wait)
+        gate, raw, flat = project_tokens(normed_near, normed_far, at, weight, inner, wait)
         gates.append(gate)
         raws.append(raw.reshape(1, length, raw.shape[-1]))
         turned_normed.append(flat)
 
     def forward_step(at, wait=()):
-        got = scan_forward(raws[at], 0, *params, wait=wait)
+        got = scan_forward(half_at, raws[at], 0, *params, wait=wait)
         mixed.append(got[0].reshape(natural + (inner,)))
         starts.append(got[1])
         edges.append(got[2])
 
     def stats_step(at, wait=()):
-        down, own = gate_stats(grads[at], w_out, mixed[at], gates[at], gain_own, wait)
+        down, own = gate_stats(
+            grad_near, at, grad_far, at, w_out, mixed[at], gates[at], gain_own, wait
+        )
         downs.append(down)
         return own
 
@@ -905,21 +1021,21 @@
         flat, d_mixed, d_gate, out, gain = gate_back(
             mixed[at], gates[at], downs[at], sums, gain_own, w_out, wait
         )
-        turned_gated.append(flat[None])
+        turned_gated.append(flat)
         d_gates.append(d_gate)
         return d_mixed, out, gain
 
     def scan_step(at, d_mixed, wait=()):
         d_mixed = d_mixed.reshape(1, length, inner)
         d_raw, *small = scan_backward(
-            raws[at], 0, d_mixed, starts[at], edges[at], *params, wait=wait
+            half_at, raws[at], 0, d_mixed, starts[at], edges[at], *params, wait=wait
         )
         d_raws.append(d_raw[0])
         small_scan.append(small)
 
     def norm_step(at, wait=()):
         d_raw = d_raws[at].reshape(natural + (d_raws[at].shape[-1],))
-        return norm_part(d_gates[at], d_raw, normeds[at], weight, wait)
+        return norm_part(d_gates[at], d_raw, normed_near, normed_far, at, weight, wait)
 
     def owned_parts(part):
         blocks = part.reshape(lay.parts, lay.wsh, in_rows, part.shape[1])
@@ -936,7 +1052,6 @@
             total = total + part.astype(F32)
         return total.astype(BF16)
 
-    flat_grads = [g.reshape(length, model) for g in grads]
     cross, first_pairs, second_pairs = [], [], []
     for half in range(2):
         for chip in range(lay.chips):
@@ -960,61 +1075,60 @@
             if bits:
                 pairs = [(i, i ^ bits) for i in range(lay.wsh)]
                 moved = lax.ppermute(values, "wsh", pairs)
-            both = [(h * lay.wsh + i, (1 - h) * lay.wsh + (i ^ bits)) for h in range(2) for i in range(lay.wsh)]
+            both = []
+            for i in range(lay.wsh):
+                both += [(i, lay.wsh + (i ^ bits)), (lay.wsh + i, i ^ bits)]
             parts += [moved, lax.ppermute(values, ("half", "wsh"), both)]
         return parts
 
     project_step(0)
     forward_step(0)
-    out_pieces, mixed[0] = join(out_pieces, mixed[0])
+    project_step(1, (edges[0],))
+    forward_step(1)
+    out_pieces, mixed[1] = join(out_pieces, mixed[1])
     w_out = own_rows(*out_pieces)
-    sums = add_all(team_parts(stats_step(0), lay))
-    d_mixed0, out, gain0 = back_step(0, sums)
-    out0 = team_sum(out, lay)
-    scan_step(0, d_mixed0)
-    project_step(1, (small_scan[0][1],))
-    forward_step(1)
-    own = stats_step(1)
+    own = stats_step(0)
     parts = team_parts(own, lay)
-    part, norm_gain0 = norm_step(0, (own,))
-    norm0 = team_sum(part, lay)
+    own1 = stats_step(1, (own,))
     sums = add_all(parts)
-    d_mixed1, out, gain1 = back_step(1, sums, (norm_gain0,))
-    out1 = team_sum(out, lay)
+    d_mixed0, out, gain0 = back_step(0, sums, (own1,))
+    out0 = team_sum(out)
+    d_mixed1, out, gain1 = back_step(1, add_all(team_parts(own1, lay)), (gain0,))
+    out1 = team_sum(out)
     flat_gates = [d.reshape(length, inner) for d in d_gates]
     gate_grad = row_grad(
         [(turned_normed[0], flat_gates[0]), (turned_normed[1], flat_gates[1])], BF16
     )
     gate_kept, gate_came = owned_parts(gate_grad)
-    out_grad = row_grad(
-        [(turned_gated[0], flat_grads[0]), (turned_gated[1], flat_grads[1])],
-        BF16,
-        wait=(gate_kept,),
-    )
+    out_grad = out_grad_part(turned_gated, grad_near, grad_far, wait=(gate_kept,))
     out_kept, out_came = out_split(out_grad)
-    scan_base = row_grad([(turned_normed[0], d_raws[0])], F32, wait=(out_kept,))
-    gate_came, sum0, d_mixed1, scan_base = join(
-        gate_came, two_halves(out0, lay), d_mixed1, scan_base
-    )
+    scan_step(0, d_mixed0, (out_kept,))
+    part, norm_gain0 = norm_step(0)
+    gate_came, out_came, d_mixed1, part = join(gate_came, out_came, d_mixed1, part)
+    norm0 = team_sum(part)
     by_gate = to_owners(add_owned(gate_kept, gate_came))
+    out_kept = add_owned(out_kept, out_came)
+    out_came = lax.ppermute(out_kept, ALL, cross)
+    sum0 = two_halves(out0, lay)
     scan_step(1, d_mixed1)
     part, norm_gain1 = norm_step(1)
-    norm1 = team_sum(part, lay)
-    out_came, sum1, norm_gain1 = join(out_came, two_halves(out1, lay), norm_gain1)
     scan_grad = row_grad(
-        [(turned_normed[1], d_raws[1])], BF16, None, scan_base, wait=(norm_gain1,)
+        [(turned_normed[0], d_raws[0]), (turned_normed[1], d_raws[1])], BF16, wait=(norm_gain1,)
     )
     scan_kept, scan_came = owned_parts(scan_grad)
-    out_kept = add_owned(out_kept, out_came)
-    out_came = lax.ppermute(out_kept, ALL, cross)
-    small = add_all(team_parts(pack_small(norm_gain1), lay))
-    scan_came, norm0, small = join(scan_came, two_halves(norm0, lay), small)
-    by_scan = to_owners(add_owned(scan_kept, scan_came))
+    by_gate, out_came, sum0, scan_kept, part = join(by_gate, out_came, sum0, scan_kept, part)
+    norm1 = team_sum(part)
     out_held = (out_kept.astype(F32) + out_came.astype(F32)).astype(BF16)
     out_first = lax.ppermute(out_held[0], ALL, first_pairs)
     out_second = lax.ppermute(out_held[1], ALL, second_pairs)
-    norm1 = two_halves(norm1, lay)
-    small = add_all(over_groups(small))
+    small = over_groups(own_small(norm_gain1))
+    scan_came, sum1, norm0, small = join(
+        scan_came, two_halves(out1, lay), two_halves(norm0, lay), small
+    )
+    by_scan = to_owners(add_owned(scan_kept, scan_came))
+    small = team_parts(pack_small(add_all(small)), lay)
+    by_scan, norm1, small = join(by_scan, two_halves(norm1, lay), small)
+    small = add_all(small)
     out_proj_grad = out_first.astype(F32) + out_second.astype(F32)
 
     def whole_place(first, second):
@@ -1035,24 +1149,12 @@
 
     hidden_grad = hidden_step()
 
-    def assemble(scan_parts):
-        def owned(parts):
-            view = parts.reshape(2, team, in_rows, parts.shape[-1])
-            return jnp.sum(view.astype(F32), axis=0)
-
-        by_block = [(b % lay.chips) * 2 + b // lay.chips for b in range(team)]
-        scan_sums = owned(scan_parts)
-        gate_sums = owned(by_gate)
-        bc_sum = jnp.sum(scan_sums[:, :, inner : inner + 2 * STATE], axis=0)
-        return jnp.concatenate(
-            [gate_sums[m] for m in by_block]
-            + [scan_sums[m, :, :inner] for m in by_block]
-            + [bc_sum]
-            + [scan_sums[m, :, inner + 2 * STATE :] for m in by_block],
-            1,
-        )
-
-    in_proj_grad = assemble(by_scan)
+    order = [(b % lay.chips) * 2 + b // lay.chips for b in range(team)]
+
+    def by_member_parts(parts):
+        return parts.reshape(2, team, in_rows, parts.shape[-1])
+
+    in_proj_grad = owned_rows(order, by_member_parts(by_gate), by_member_parts(by_scan))
     ngain_all, conv_all, cbias_all, shift_all, rate_all, skip_all, ggain_all = unpack_small(small)
     return (
         block_out,

time: 492 us -> 480 us (0.976)
  waiting for transfers between devices: 127 us -> 140 us
  local copies, waits for them, and re-layouts: 62.4 us -> 51 us
  other arithmetic: 38.2 us -> 32.9 us
    ppermute x2, waiting for transfers between devices: 44.2 us -> 0.01 us  [over_groups(): parts += [moved, lax.ppermute(values, ('half', 'wsh'), both)]]
    ppermute x1, waiting for transfers between devices: 0.01 us -> 28.5 us  [over_groups(): moved = lax.ppermute(values, 'wsh', pairs)]
    ppermute x9, waiting for transfers between devices: 6.51 us -> 25.9 us  [chip_flip(): lax.ppermute(values, 'chip', [(i, i ^ bits) for i in range(self.chips)])]
    all_gather x4, waiting for transfers between devices: 0.01 us -> 14.4 us  [team_gather(): return lax.all_gather(values, TEAM, axis=0)]
    ppermute x1, waiting for transfers between devices: 13.9 us -> 0.01 us  [shards(): out_came = lax.ppermute(out_kept, ALL, cross)]
    slice x4 -> x9, local copies, waits for them, and re-layouts: 0.15 us -> 7.44 us  [the longest x4 7.34 us: two_halves(): return (own[0], lay.other_half(own[1]))]
    another operation x9 -> x1, local copies, waits for them, and re-layouts: 6.8 us -> 0.08 us  [own_small(): return jnp.concatenate([p.reshape(-1) for p in parts])]
    unnamed x100 -> x115, local copies, waits for them, and re-layouts: 6.05 us -> 11.6 us
  transfers between devices with their start and end apart: 40 -> 40, of which waited for: 18 -> 16; matrix products, arithmetic and copies ran while one was open for 17% -> 12% of each run, Pallas kernels for 38% -> 34%
where the time goes in v3:
time: 480 us; the launch traced here: 475 us
  Pallas kernels  181 us (38%)
  waiting for transfers between devices  140 us (29%)
  starting transfers between devices  55.4 us (12%)
  local copies, waits for them, and re-layouts  51 us (11%)
  other arithmetic  32.9 us (7%)
  between operations  15.3 us (3%)
    pallas_call x15, Pallas kernels, call_after(): return pl.pallas_call(inner_body, **rest)(*values, *wait)  177 us
    ppermute x6, waiting for transfers between devices, other_half(): return lax.ppermute(values, 'half', [(0, 1), (1, 0)])  54.4 us
    ppermute x1, waiting for transfers between devices, over_groups(): moved = lax.ppermute(values, 'wsh', pairs)  28.5 us
    ppermute x9, waiting for transfers between devices, chip_flip(): lax.ppermute(values, 'chip', [(i, i ^ bits) for i in range(self.chips)])  25.9 us
    all_gather x4, waiting for transfers between devices, team_gather(): return lax.all_gather(values, TEAM, axis=0)  14.4 us
    ppermute x5, waiting for transfers between devices, wsh_shift(): lax.ppermute(values, 'wsh', [(i, (i + shift) % size) for i in range(size)])  13.4 us
    ppermute x6, starting transfers between devices, other_half(): return lax.ppermute(values, 'half', [(0, 1), (1, 0)])  13.3 us
    unnamed x115, local copies, waits for them, and re-layouts  11.6 us
  transfers between devices with their start and end apart: 40, of which 16 were waited for; matrix products, arithmetic and copies ran while one was open for 12% of the time, Pallas kernels for 34%

profile of v3, /device:TPU:0, one launch (start us, length us, event | category | flops | bytes accessed | tf_op | source)
XLA Modules:
  0.0 475.1 jit_solution(12354760554944935786)
XLA Ops:
  26.5 17.2 %collective-permute-done.1.refs_1_ = bf16[2,64,2048]{2,1,0:T(8,128)(2,1)} collective-permute-done((bf16[2,64,2048]{2,1,0:T(8,128)(2,1)}, bf16[2,64,2048]{2,1,0:T(8,128)(2,1)}, u32[]{:S(2)}, u32[]{:S(2)}) %collective-permute-start.1) | collective-permute-done | bytes 524320 | tf_op jit(solution)/shard_map/ppermute | solution.py:787
  57.4 3.3 constant_dynamic-slice_fusion.3.refs_2_
  61.8 17.6 %collective-permute-done.3.refs_1_ = bf16[2,64,2048]{2,1,0:T(8,128)(2,1)} collective-permute-done((bf16[2,64,2048]{2,1,0:T(8,128)(2,1)}, bf16[2,64,2048]{2,1,0:T(8,128)(2,1)}, u32[]{:S(2)}, u32[]{:S(2)}) %collective-permute-start.3) | collective-permute-done | bytes 524320 | tf_op jit(solution)/shard_map/ppermute | solution.py:787
  88.7 6.9 %all-gather.11.cloned.1.call-done = bf16[16,64,2048]{2,1,0:T(8,128)(2,1)} async-done(((bf16[2,64,2048]{2,1,0:T(8,128)(2,1)}), bf16[16,64,2048]{2,1,0:T(8,128)(2,1)}) %all-gather.11.cloned.1.call-update) | async-done | bytes 4194320 | tf_op jit(solution)/shard_map/all_gather | solution.py:809
  97.2 3.7 collective-permute-start.4
  100.9 11.5 %project_tokens.2 = (bf16[2,8,64,512]{3,2,1,0:T(8,128)(2,1)}, bf16[2,8,64,776]{3,2,1,0:T(8,128)(2,1)}, bf16[2,2048,512]{2,1,0:T(8,128)(2,1)}) custom-call(bf16[8,2,64,2048]{3,2,1,0:T(8,128)(2,1)} %get-tuple-element.97.refs_0_.refs_2_, bf16[8,2,64,2048]{3,2,1,0:T(8,128)(2,1)} %get-tuple-element.102.refs_1_.refs_3_, ...), custom_call_target="tpu_custom_call" | custom-call | flops 11000000512 | bytes 27500000 | tf_op jit(solution)/shard_map/project_tokens/pallas_call | solution.py:394
  112.4 10.9 %scan_forward.2 = (bf16[1,1024,512]{2,1,0:T(8,128)(2,1)}, f32[1,4,128,512]{3,2,1,0:T(8,128)}, f32[1,4,8,768]{3,2,1,0:T(8,128)}) custom-call(s32[1]{0:T(128)} %bitcast.9.refs_0_, bf16[1,1024,776]{2,1,0:T(8,128)(2,1)} %bitcast.109, f32[4,768]{1,0:T(4,128)} %get-tuple-element.106.refs_2_.refs_5_, f32[1,768]{1,0:T(1,128)} %get-tuple-element.107.refs_3_.refs_6_, ...), custom_call_target="tpu_custom_call" | custom-call | flops 10000000000 | bytes 25000000 | tf_op jit(solution)/shard_map/scan_forward/pallas_call | solution.py:394
  123.4 11.6 %project_tokens.3 = (bf16[2,8,64,512]{3,2,1,0:T(8,128)(2,1)}, bf16[2,8,64,776]{3,2,1,0:T(8,128)(2,1)}, bf16[2,2048,512]{2,1,0:T(8,128)(2,1)}) custom-call(bf16[8,2,64,2048]{3,2,1,0:T(8,128)(2,1)} %get-tuple-element.97.refs_0_.refs_2_, bf16[8,2,64,2048]{3,2,1,0:T(8,128)(2,1)} %get-tuple-element.102.refs_1_.refs_3_, ...), custom_call_target="tpu_custom_call" | custom-call | flops 11000000512 | bytes 27500000 | tf_op jit(solution)/shard_map/project_tokens/pallas_call | solution.py:394
  135.0 11.0 %scan_forward.3 = (bf16[1,1024,512]{2,1,0:T(8,128)(2,1)}, f32[1,4,128,512]{3,2,1,0:T(8,128)}, f32[1,4,8,768]{3,2,1,0:T(8,128)}) custom-call(s32[1]{0:T(128)} %bitcast.9.refs_0_, bf16[1,1024,776]{2,1,0:T(8,128)(2,1)} %bitcast.107, f32[4,768]{1,0:T(4,128)} %get-tuple-element.106.refs_2_.refs_5_, f32[1,768]{1,0:T(1,128)} %get-tuple-element.107.refs_3_.refs_6_, ...), custom_call_target="tpu_custom_call" | custom-call | flops 10000000000 | bytes 25000000 | tf_op jit(solution)/shard_map/scan_forward/pallas_call | solution.py:394
  150.5 7.5 %all-gather.15.cloned.1.call-done = bf16[16,64,2048]{2,1,0:T(8,128)(2,1)} async-done(((bf16[2,64,2048]{2,1,0:T(8,128)(2,1)}), bf16[16,64,2048]{2,1,0:T(8,128)(2,1)}) %all-gather.15.cloned.1.call-update) | async-done | bytes 4194320 | tf_op jit(solution)/shard_map/all_gather | solution.py:809
  157.9 7.4 %gate_stats.2 = (f32[2,8,64,512]{3,2,1,0:T(8,128)}, f32[2,1024]{1,0:T(2,128)}) custom-call(bf16[8,2,64,2048]{3,2,1,0:T(8,128)(2,1)} %bitcast.101, bf16[8,2,64,2048]{3,2,1,0:T(8,128)(2,1)} %bitcast.104, bf16[512,2048]{1,0:T(8,128)(2,1)} %select_add_fusion.refs_2_.refs_5_, bf16[2,8,64,512]{3,2,1,0:T(8,128)(2,1)} %bitcast.112, ...), custom_call_target="tpu_custom_call" | custom-call | flops 7000000000 | bytes 17500000 | tf_op jit(solution)/shard_map/gate_stats/pallas_call | solution.py:394
  170.9 7.4 %gate_stats.3 = (f32[2,8,64,512]{3,2,1,0:T(8,128)}, f32[2,1024]{1,0:T(2,128)}) custom-call(bf16[8,2,64,2048]{3,2,1,0:T(8,128)(2,1)} %bitcast.102, bf16[8,2,64,2048]{3,2,1,0:T(8,128)(2,1)} %bitcast.105, bf16[512,2048]{1,0:T(8,128)(2,1)} %select_add_fusion.refs_2_.refs_5_, bf16[2,8,64,512]{3,2,1,0:T(8,128)(2,1)} %get-tuple-element.123.refs_3_.refs_0_, ...), custom_call_target="tpu_custom_call" | custom-call | flops 7000000000 | bytes 17500000 | tf_op jit(solution)/shard_map/gate_stats/pallas_call | solution.py:394
  178.9 8.8 %gate_back.2 = (bf16[2,512,512]{2,1,0:T(8,128)(2,1)}, bf16[2,8,64,512]{3,2,1,0:T(8,128)(2,1)}, bf16[2,8,64,512]{3,2,1,0:T(8,128)(2,1)}, bf16[1024,2048]{1,0:T(8,128)(2,1)}, f32[1,512]{1,0:T(1,128)}) custom-call(bf16[2,8,64,512]{3,2,1,0:T(8,128)(2,1)} %bitcast.113, bf16[2,8,64,512]{3,2,1,0:T(8,128)(2,1)} %get-tuple-element.112.refs_4_.refs_1_, ...), custom_call_target="tpu_custom_call" | custom-call | flops 8000000000 | bytes 20000000 | tf_op jit(solution)/shard_map/gate_back/pallas_call | solution.py:394
  196.7 8.8 %gate_back.3 = (bf16[2,512,512]{2,1,0:T(8,128)(2,1)}, bf16[2,8,64,512]{3,2,1,0:T(8,128)(2,1)}, bf16[2,8,64,512]{3,2,1,0:T(8,128)(2,1)}, bf16[1024,2048]{1,0:T(8,128)(2,1)}, f32[1,512]{1,0:T(1,128)}) custom-call(bf16[2,8,64,512]{3,2,1,0:T(8,128)(2,1)} %get-tuple-element.123.refs_3_.refs_0_, bf16[2,8,64,512]{3,2,1,0:T(8,128)(2,1)} %get-tuple-element.124.refs_4_.refs_1_, ...), custom_call_target="tpu_custom_call" | custom-call | flops 8000000000 | bytes 20000000 | tf_op jit(solution)/shard_map/gate_back/pallas_call | solution.py:394
  205.6 8.7 %row_grad.2 = bf16[2048,512]{1,0:T(8,128)(2,1)} custom-call(bf16[2,2048,512]{2,1,0:T(8,128)(2,1)} %get-tuple-element.104.refs_0_, bf16[1024,512]{1,0:T(8,128)(2,1)} %bitcast.86, bf16[2,2048,512]{2,1,0:T(8,128)(2,1)} %get-tuple-element.127.refs_2_, bf16[1024,512]{1,0:T(8,128)(2,1)} %bitcast.85), custom_call_target="tpu_custom_call" | custom-call | tf_op jit(solution)/shard_map/row_grad/pallas_call | solution.py:394
  217.0 10.4 %out_grad_part.1 = bf16[512,2048]{1,0:T(8,128)(2,1)} custom-call(bf16[2,512,512]{2,1,0:T(8,128)(2,1)} %get-tuple-element.131.refs_0_, bf16[2,512,512]{2,1,0:T(8,128)(2,1)} %get-tuple-element.132.refs_1_, bf16[8,2,64,2048]{3,2,1,0:T(8,128)(2,1)} %bitcast.103, bf16[8,2,64,2048]{3,2,1,0:T(8,128)(2,1)} %bitcast.106, bf16[16,64,512]{2,1,0:T(8,128)(2,1)} %get-tuple-element.188.refs_4_), custom_call_target="tpu_custom_call" | custom-call | flops 8000000000 | bytes 20000000 | tf_op jit(solution)/shard_map/out_grad_part/pallas_call | solution.py:394
  232.3 22.2 %scan_backward.2 = (bf16[1,1024,776]{2,1,0:T(8,128)(2,1)}, f32[8,768]{1,0:T(8,128)}, f32[1,512]{1,0:T(1,128)}, f32[2,8,1]{2,1,0:T(8,128)}) custom-call(s32[1]{0:T(128)} %bitcast.9.refs_0_, bf16[1,1024,776]{2,1,0:T(8,128)(2,1)} %bitcast.110, bf16[1,1024,512]{2,1,0:T(8,128)(2,1)} %bitcast.111, f32[1,4,128,512]{3,2,1,0:T(8,128)} %get-tuple-element.135.refs_3_, ...), custom_call_target="tpu_custom_call" | custom-call | flops 22000001024 | bytes 55000000 | tf_op jit(solution)/shard_map/scan_backward/pallas_call | solution.py:394
  254.5 11.5 %norm_part.2 = (bf16[1024,2048]{1,0:T(8,128)(2,1)}, f32[1,2048]{1,0:T(1,128)}) custom-call(bf16[2,8,64,512]{3,2,1,0:T(8,128)(2,1)} %get-tuple-element.126.refs_0_, bf16[2,8,64,776]{3,2,1,0:T(8,128)(2,1)} %bitcast.80, bf16[8,2,64,2048]{3,2,1,0:T(8,128)(2,1)} %get-tuple-element.97.refs_0_.refs_2_, bf16[8,2,64,2048]{3,2,1,0:T(8,128)(2,1)} %get-tuple-element.102.refs_1_.refs_3_, ...), custom_call_target="tpu_custom_call" | custom-call | tf_op jit(solution)/shard_map/norm_part/pallas_call | solution.py:394
  266.1 10.3 %collective-permute-done.13.refs_0_ = bf16[16,64,512]{2,1,0:T(8,128)(2,1)S(1)} collective-permute-done((bf16[16,64,512]{2,1,0:T(8,128)(2,1)S(1)}, bf16[16,64,512]{2,1,0:T(8,128)(2,1)S(1)}, u32[]{:S(2)}, u32[]{:S(2)}) %collective-permute-start.13) | collective-permute-done | bytes 1048608 | tf_op jit(solution)/shard_map/ppermute | solution.py:794
  281.3 4.6 all-to-all-start
  289.8 3.6 collective-permute-start.16
  293.4 22.2 %scan_backward.3 = (bf16[1,1024,776]{2,1,0:T(8,128)(2,1)}, f32[8,768]{1,0:T(8,128)}, f32[1,512]{1,0:T(1,128)}, f32[2,8,1]{2,1,0:T(8,128)}) custom-call(s32[1]{0:T(128)} %bitcast.9.refs_0_, bf16[1,1024,776]{2,1,0:T(8,128)(2,1)} %bitcast.108, bf16[1,1024,512]{2,1,0:T(8,128)(2,1)} %bitcast.92, f32[1,4,128,512]{3,2,1,0:T(8,128)} %get-tuple-element.142.refs_3_, ...), custom_call_target="tpu_custom_call" | custom-call | flops 22000001024 | bytes 55000000 | tf_op jit(solution)/shard_map/scan_backward/pallas_call | solution.py:394
  315.6 11.5 %norm_part.3 = (bf16[1024,2048]{1,0:T(8,128)(2,1)}, f32[1,2048]{1,0:T(1,128)}) custom-call(bf16[2,8,64,512]{3,2,1,0:T(8,128)(2,1)} %get-tuple-element.130.refs_0_, bf16[2,8,64,776]{3,2,1,0:T(8,128)(2,1)} %bitcast.82, bf16[8,2,64,2048]{3,2,1,0:T(8,128)(2,1)} %get-tuple-element.97.refs_0_.refs_2_, bf16[8,2,64,2048]{3,2,1,0:T(8,128)(2,1)} %get-tuple-element.102.refs_1_.refs_3_, ...), custom_call_target="tpu_custom_call" | custom-call | tf_op jit(solution)/shard_map/norm_part/pallas_call | solution.py:394
  327.1 13.2 %row_grad.3 = bf16[2048,776]{1,0:T(8,128)(2,1)} custom-call(bf16[2,2048,512]{2,1,0:T(8,128)(2,1)} %get-tuple-element.104.refs_0_, bf16[1024,776]{1,0:T(8,128)(2,1)} %bitcast.81, bf16[2,2048,512]{2,1,0:T(8,128)(2,1)} %get-tuple-element.127.refs_2_, bf16[1024,776]{1,0:T(8,128)(2,1)} %bitcast.83, f32[1,2048]{1,0:T(1,128)} %get-tuple-element.145.refs_4_), custom_call_target="tpu_custom_call" | custom-call | tf_op jit(solution)/shard_map/row_grad/pallas_call | solution.py:394
  340.3 4.3 dynamic-slice_bitcast_fusion.1
  350.5 3.4 collective-permute-start.20
  361.0 28.5 %collective-permute-done.21.refs_7_ = f32[6424]{0:T(1024)S(1)} collective-permute-done((f32[6424]{0:T(1024)S(1)}, f32[6424]{0:T(1024)S(1)}, u32[]{:S(2)}, u32[]{:S(2)}) %collective-permute-start.21) | collective-permute-done | bytes 25728 | tf_op jit(solution)/shard_map/ppermute | solution.py:1077
  390.2 3.4 add_convert_fusion
  393.6 4.8 %all-to-all-start.1 = ((bf16[16,64,776]{2,1,0:T(8,128)(2,1)}), bf16[16,64,776]{2,1,0:T(8,128)(2,1)S(1)}, u32[]{:S(2)}, u32[]{:S(2)}) async-start(bf16[16,64,776]{2,1,0:T(8,128)(2,1)} %add_convert_fusion), calls=%async_computation.4 | async-start | bytes 3670016 | tf_op jit(solution)/shard_map/all_to_all | solution.py:1047
  412.3 20.4 %collective-permute-done.27.refs_6_ = f32[28096]{0:T(1024)} collective-permute-done((f32[28096]{0:T(1024)S(1)}, f32[28096]{0:T(1024)}, u32[]{:S(2)}, u32[]{:S(2)}) %collective-permute-start.27) | collective-permute-done | bytes 112416 | tf_op jit(solution)/shard_map/ppermute | solution.py:790
  435.1 17.9 %collective-permute-done.23.refs_2_ = bf16[64,2048]{1,0:T(8,128)(2,1)S(1)} collective-permute-done((bf16[64,2048]{1,0:T(8,128)(2,1)}, bf16[64,2048]{1,0:T(8,128)(2,1)S(1)}, u32[]{:S(2)}, u32[]{:S(2)}) %collective-permute-start.23) | collective-permute-done | bytes 262176 | tf_op jit(solution)/shard_map/ppermute | solution.py:787
  461.4 3.6 owned_rows.1
  (288 shorter events, 121.6 us)
Async XLA Ops:
  7.2 72.2 %all-gather.9.cloned.1.call-start = ((), (), s32[]{:S(2)}) async-start(), calls=%async_computation.10 | async-start | bytes 4718592 | tf_op jit(solution)/shard_map/all_gather | solution.py:809
  12.0 83.6 %all-gather.11.cloned.1.call-start = ((), (), s32[]{:S(2)}) async-start(), calls=%async_computation.11 | async-start | bytes 4718592 | tf_op jit(solution)/shard_map/all_gather | solution.py:809
  14.9 31.9 %collective-permute-start = (bf16[640,1024]{1,0:T(8,128)(2,1)}, bf16[640,1024]{1,0:T(8,128)(2,1)S(1)}, u32[]{:S(2)}, u32[]{:S(2)}) collective-permute-start(bf16[640,1024]{1,0:T(8,128)(2,1)} %pad_maximum_fusion.4), channel_id=1, source_target_pairs={{0,1},{1,0},{2,3},{3,2},{4,5},{5,4},{6,7},{7,6},{8,9},{9,8},{10,11... | collective-permute-start | bytes 3932168 | tf_op jit(solution)/shard_map/ppermute | solution.py:794
  17.8 25.9 %collective-permute-start.1 = (bf16[2,64,2048]{2,1,0:T(8,128)(2,1)}, bf16[2,64,2048]{2,1,0:T(8,128)(2,1)}, u32[]{:S(2)}, u32[]{:S(2)}) collective-permute-start(bf16[2,64,2048]{2,1,0:T(8,128)(2,1)} %get-tuple-element.200), channel_id=1, source_target_pairs={{0,16},{16,0},{1,17},{17,1},{2,18},{18,2},{3,19},{19,3},{4,20},{20... | collective-permute-start | bytes 1572872 | tf_op jit(solution)/shard_map/ppermute | solution.py:787
  47.9 102.5 %all-gather.13.cloned.1.call-start = ((), (), s32[]{:S(2)}) async-start(), calls=%async_computation.12 | async-start | bytes 4718592 | tf_op jit(solution)/shard_map/all_gather | solution.py:809
  48.0 31.3 %collective-permute-start.2 = (bf16[648,1024]{1,0:T(8,128)(2,1)}, bf16[648,1024]{1,0:T(8,128)(2,1)S(1)}, u32[]{:S(2)}, u32[]{:S(2)}) collective-permute-start(bf16[648,1024]{1,0:T(8,128)(2,1)} %get-tuple-element.95), channel_id=1, source_target_pairs={{0,1},{1,0},{2,3},{3,2},{4,5},{5,4},{6,7},{7,6},{8,9},{9,8},{10,11... | collective-permute-start | bytes 3981320 | tf_op jit(solution)/shard_map/ppermute | solution.py:794
  54.2 25.2 %collective-permute-start.3 = (bf16[2,64,2048]{2,1,0:T(8,128)(2,1)}, bf16[2,64,2048]{2,1,0:T(8,128)(2,1)}, u32[]{:S(2)}, u32[]{:S(2)}) collective-permute-start(bf16[2,64,2048]{2,1,0:T(8,128)(2,1)} %get-tuple-element.96), channel_id=1, source_target_pairs={{0,16},{16,0},{1,17},{17,1},{2,18},{18,2},{3,19},{19,3},{4,20},{20... | collective-permute-start | bytes 1572872 | tf_op jit(solution)/shard_map/ppermute | solution.py:787
  95.6 62.3 %all-gather.15.cloned.1.call-start = ((), (), s32[]{:S(2)}) async-start(), calls=%async_computation.13 | async-start | bytes 4718592 | tf_op jit(solution)/shard_map/all_gather | solution.py:809
  96.2 191.8 %reduce-scatter.5.cloned.1.call-start = ((), (), s32[]{:S(2)}) async-start(), calls=%async_computation.6 | async-start | bytes 4718592 | tf_op jit(solution)/shard_map/reduce_scatter | solution.py:819
  97.2 48.7 %collective-permute-start.4 = (bf16[512,2048]{1,0:T(8,128)(2,1)S(1)}, bf16[512,2048]{1,0:T(8,128)(2,1)S(1)}, u32[]{:S(2)}, u32[]{:S(2)}) collective-permute-start(bf16[512,2048]{1,0:T(8,128)(2,1)S(1)} %copy-done.2), channel_id=1, source_target_pairs={{0,1},{3,2},{4,5},{7,6},{8,9},{11,10},{12,13},{15,14},{16,17},{19,... | collective-permute-start | bytes 6291464 | tf_op jit(solution)/shard_map/ppermute | solution.py:916
  167.4 10.9 %collective-permute-start.8 = (f32[2,1024]{1,0:T(2,128)S(1)}, f32[2,1024]{1,0:T(2,128)S(1)}, u32[]{:S(2)}, u32[]{:S(2)}) collective-permute-start(f32[2,1024]{1,0:T(2,128)S(1)} %add.194), channel_id=1, source_target_pairs={{0,12},{4,8},{8,4},{12,0},{1,13},{5,9},{9,5},{13,1},{2,14},{6,10},... | collective-permute-start | bytes 24584 | tf_op jit(solution)/shard_map/ppermute | solution.py:790
  168.9 9.4 %collective-permute-start.7 = (f32[2,1024]{1,0:T(2,128)S(1)}, f32[2,1024]{1,0:T(2,128)S(1)}, u32[]{:S(2)}, u32[]{:S(2)}) collective-permute-start(f32[2,1024]{1,0:T(2,128)S(1)} %add.194), channel_id=1, source_target_pairs={{0,8},{4,12},{8,0},{12,4},{1,9},{5,13},{9,1},{13,5},{2,10},{6,14},... | collective-permute-start | bytes 24584 | tf_op jit(solution)/shard_map/ppermute | solution.py:790
  187.7 166.2 %reduce-scatter.7.cloned.1.call-start = ((), (), s32[]{:S(2)}) async-start(), calls=%async_computation.7 | async-start | bytes 4718592 | tf_op jit(solution)/shard_map/reduce_scatter | solution.py:819
  205.5 150.3 %reduce-scatter.9.cloned.1.call-start = ((), (), s32[]{:S(2)}) async-start(), calls=%async_computation.8 | async-start | bytes 4718592 | tf_op jit(solution)/shard_map/reduce_scatter | solution.py:819
  230.3 35.8 %collective-permute-start.14 = (bf16[2,128,2048]{2,1,0:T(8,128)(2,1)S(1)}, bf16[2,128,2048]{2,1,0:T(8,128)(2,1)S(1)}, u32[]{:S(2)}, u32[]{:S(2)}) collective-permute-start(bf16[2,128,2048]{2,1,0:T(8,128)(2,1)S(1)} %get-tuple-element.185), channel_id=1, source_target_pairs={{0,1},{1,0},{2,3},{3,2},{4,5},{5,4},{6,7},{7,6},{8,9},{9,8},{10,11... | collective-permute-start | bytes 3145736 | tf_op jit(solution)/shard_map/ppermute | solution.py:794
  231.7 44.7 %collective-permute-start.13 = (bf16[16,64,512]{2,1,0:T(8,128)(2,1)S(1)}, bf16[16,64,512]{2,1,0:T(8,128)(2,1)S(1)}, u32[]{:S(2)}, u32[]{:S(2)}) collective-permute-start(bf16[16,64,512]{2,1,0:T(8,128)(2,1)S(1)} %get-tuple-element.187), channel_id=1, source_target_pairs={{0,1},{1,0},{2,3},{3,2},{4,5},{5,4},{6,7},{7,6},{8,9},{9,8},{10,11... | collective-permute-start | bytes 3145736 | tf_op jit(solution)/shard_map/ppermute | solution.py:794
  281.3 63.3 %all-to-all-start = ((bf16[16,64,512]{2,1,0:T(8,128)(2,1)}), bf16[16,64,512]{2,1,0:T(8,128)(2,1)}, u32[]{:S(2)}, u32[]{:S(2)}) async-start(bf16[16,64,512]{2,1,0:T(8,128)(2,1)} %add_convert_fusion.3), calls=%async_computation | async-start | bytes 2097152 | tf_op jit(solution)/shard_map/all_to_all | solution.py:1047
  286.0 121.8 %reduce-scatter.11.cloned.1.call-start = ((), (), s32[]{:S(2)}) async-start(), calls=%async_computation.9 | async-start | bytes 4718592 | tf_op jit(solution)/shard_map/reduce_scatter | solution.py:819
  286.4 58.2 %collective-permute-start.15 = (bf16[2,128,2048]{2,1,0:T(8,128)(2,1)S(1)}, bf16[2,128,2048]{2,1,0:T(8,128)(2,1)S(1)}, u32[]{:S(2)}, u32[]{:S(2)}) collective-permute-start(bf16[2,128,2048]{2,1,0:T(8,128)(2,1)S(1)} %add_convert_fusion.2), channel_id=1, source_target_pairs={{16,0},{20,4},{24,8},{28,12},{2,18},{6,22},{10,26},{14,30},{17,1},... | collective-permute-start | bytes 3145736 | tf_op jit(solution)/shard_map/ppermute | solution.py:1111
  289.8 56.5 %collective-permute-start.16 = (bf16[64,2048]{1,0:T(8,128)(2,1)S(1)}, bf16[64,2048]{1,0:T(8,128)(2,1)S(1)}, u32[]{:S(2)}, u32[]{:S(2)}) collective-permute-start(bf16[64,2048]{1,0:T(8,128)(2,1)S(1)} %get-tuple-element.203), channel_id=1, source_target_pairs={{0,16},{16,0},{1,17},{17,1},{2,18},{18,2},{3,19},{19,3},{4,20},{20... | collective-permute-start | bytes 786440 | tf_op jit(solution)/shard_map/ppermute | solution.py:787
  347.7 41.8 %collective-permute-start.17 = (bf16[16,64,776]{2,1,0:T(8,128)(2,1)}, bf16[16,64,776]{2,1,0:T(8,128)(2,1)}, u32[]{:S(2)}, u32[]{:S(2)}) collective-permute-start(bf16[16,64,776]{2,1,0:T(8,128)(2,1)} %get-tuple-element.184), channel_id=1, source_target_pairs={{0,1},{1,0},{2,3},{3,2},{4,5},{5,4},{6,7},{7,6},{8,9},{9,8},{10,11... | collective-permute-start | bytes 4767752 | tf_op jit(solution)/shard_map/ppermute | solution.py:794
  349.5 40.0 %collective-permute-start.21 = (f32[6424]{0:T(1024)S(1)}, f32[6424]{0:T(1024)S(1)}, u32[]{:S(2)}, u32[]{:S(2)}) collective-permute-start(f32[6424]{0:T(1024)S(1)} %concatenate.43.refs_5_), channel_id=1, source_target_pairs={{0,1},{1,0},{2,3},{3,2},{4,5},{5,4},{6,7},{7,6},{8,9},{9,8},{10,11... | collective-permute-start | bytes 77096 | tf_op jit(solution)/shard_map/ppermute | solution.py:1077
  350.5 39.0 %collective-permute-start.20 = (f32[6424]{0:T(1024)S(1)}, f32[6424]{0:T(1024)S(1)}, u32[]{:S(2)}, u32[]{:S(2)}) collective-permute-start(f32[6424]{0:T(1024)S(1)} %concatenate.43.refs_5_), channel_id=1, source_target_pairs={{0,16},{16,0},{1,17},{17,1},{2,18},{18,2},{3,19},{19,3},{4,20},{20... | collective-permute-start | bytes 77096 | tf_op jit(solution)/shard_map/ppermute | solution.py:1081
  355.8 33.7 %collective-permute-start.18 = (bf16[64,2048]{1,0:T(8,128)(2,1)}, bf16[64,2048]{1,0:T(8,128)(2,1)S(1)}, u32[]{:S(2)}, u32[]{:S(2)}) collective-permute-start(bf16[64,2048]{1,0:T(8,128)(2,1)} %get-tuple-element.207), channel_id=1, source_target_pairs={{0,16},{16,0},{1,17},{17,1},{2,18},{18,2},{3,19},{19,3},{4,20},{20... | collective-permute-start | bytes 786440 | tf_op jit(solution)/shard_map/ppermute | solution.py:787
  357.6 31.9 %collective-permute-start.19 = (bf16[64,2048]{1,0:T(8,128)(2,1)S(1)}, bf16[64,2048]{1,0:T(8,128)(2,1)}, u32[]{:S(2)}, u32[]{:S(2)}) collective-permute-start(bf16[64,2048]{1,0:T(8,128)(2,1)S(1)} %get-tuple-element.205), channel_id=1, source_target_pairs={{0,16},{16,0},{1,17},{17,1},{2,18},{18,2},{3,19},{19,3},{4,20},{20... | collective-permute-start | bytes 786440 | tf_op jit(solution)/shard_map/ppermute | solution.py:787
  393.6 41.5 %all-to-all-start.1 = ((bf16[16,64,776]{2,1,0:T(8,128)(2,1)}), bf16[16,64,776]{2,1,0:T(8,128)(2,1)S(1)}, u32[]{:S(2)}, u32[]{:S(2)}) async-start(bf16[16,64,776]{2,1,0:T(8,128)(2,1)} %add_convert_fusion), calls=%async_computation.4 | async-start | bytes 3670016 | tf_op jit(solution)/shard_map/all_to_all | solution.py:1047
  400.9 8.8 %collective-permute-start.28 = (bf16[128,2048]{1,0:T(8,128)(2,1)}, bf16[128,2048]{1,0:T(8,128)(2,1)S(1)}, u32[]{:S(2)}, u32[]{:S(2)}) collective-permute-start(bf16[128,2048]{1,0:T(8,128)(2,1)} %get-tuple-element.189), channel_id=1, source_target_pairs={{0,0},{4,4},{8,8},{12,12},{18,16},{22,20},{26,24},{30,28},{1,1},{5... | collective-permute-start | bytes 1572872 | tf_op jit(solution)/shard_map/ppermute | solution.py:1122
  402.6 8.6 %collective-permute-start.29 = (bf16[128,2048]{1,0:T(8,128)(2,1)}, bf16[128,2048]{1,0:T(8,128)(2,1)S(1)}, u32[]{:S(2)}, u32[]{:S(2)}) collective-permute-start(bf16[128,2048]{1,0:T(8,128)(2,1)} %get-tuple-element.190), channel_id=1, source_target_pairs={{0,2},{4,6},{8,10},{12,14},{18,18},{22,22},{26,26},{30,30},{1,3},{... | collective-permute-start | bytes 1572872 | tf_op jit(solution)/shard_map/ppermute | solution.py:1123
  404.2 28.4 %collective-permute-start.27 = (f32[28096]{0:T(1024)S(1)}, f32[28096]{0:T(1024)}, u32[]{:S(2)}, u32[]{:S(2)}) collective-permute-start(f32[28096]{0:T(1024)S(1)} %add.218.refs_3_), channel_id=1, source_target_pairs={{0,12},{4,8},{8,4},{12,0},{1,13},{5,9},{9,5},{13,1},{2,14},{6,10},... | collective-permute-start | bytes 337160 | tf_op jit(solution)/shard_map/ppermute | solution.py:790
  406.9 28.3 %collective-permute-start.26 = (f32[28096]{0:T(1024)S(1)}, f32[28096]{0:T(1024)}, u32[]{:S(2)}, u32[]{:S(2)}) collective-permute-start(f32[28096]{0:T(1024)S(1)} %add.218.refs_3_), channel_id=1, source_target_pairs={{0,8},{4,12},{8,0},{12,4},{1,9},{5,13},{9,1},{13,5},{2,10},{6,14},... | collective-permute-start | bytes 337160 | tf_op jit(solution)/shard_map/ppermute | solution.py:790
  407.4 27.7 %collective-permute-start.25 = (f32[28096]{0:T(1024)S(1)}, f32[28096]{0:T(1024)}, u32[]{:S(2)}, u32[]{:S(2)}) collective-permute-start(f32[28096]{0:T(1024)S(1)} %add.218.refs_3_), channel_id=1, source_target_pairs={{0,4},{4,0},{8,12},{12,8},{1,5},{5,1},{9,13},{13,9},{2,6},{6,2},{1... | collective-permute-start | bytes 337160 | tf_op jit(solution)/shard_map/ppermute | solution.py:790
  409.7 43.4 %collective-permute-start.23 = (bf16[64,2048]{1,0:T(8,128)(2,1)}, bf16[64,2048]{1,0:T(8,128)(2,1)S(1)}, u32[]{:S(2)}, u32[]{:S(2)}) collective-permute-start(bf16[64,2048]{1,0:T(8,128)(2,1)} %get-tuple-element.201), channel_id=1, source_target_pairs={{0,16},{16,0},{1,17},{17,1},{2,18},{18,2},{3,19},{19,3},{4,20},{20... | collective-permute-start | bytes 786440 | tf_op jit(solution)/shard_map/ppermute | solution.py:787
  (68 other events, 504.9 us)
Sparse Core Ops, SparseCore 0:
  12.1 41.7 all-gather.8
  55.5 40.0 all-gather.10
  97.2 30.0 all-gather.12
  128.8 29.1 all-gather.14
  187.8 47.2 reduce-scatter.4
  237.2 49.6 reduce-scatter.6
  289.2 55.0 reduce-scatter.8
  347.2 51.8 reduce-scatter.10

commit v4 on v3

--- a/solution.py
+++ b/solution.py
@@ -582,7 +582,7 @@
             jax.ShapeDtypeStruct((1, inner), F32),
         ],
         compiler_params=kernel_params(),
-        cost_estimate=light_cost(8),
+        cost_estimate=light_cost(0),
         name="gate_back",
     )
 
@@ -1092,25 +1092,28 @@
     own1 = stats_step(1, (own,))
     sums = add_all(parts)
     d_mixed0, out, gain0 = back_step(0, sums, (own1,))
+    parts, out, gain0 = join(team_parts(own1, lay), out, gain0)
     out0 = team_sum(out)
-    d_mixed1, out, gain1 = back_step(1, add_all(team_parts(own1, lay)), (gain0,))
+    d_mixed1, out, gain1 = back_step(1, add_all(parts))
     out1 = team_sum(out)
     flat_gates = [d.reshape(length, inner) for d in d_gates]
     gate_grad = row_grad(
         [(turned_normed[0], flat_gates[0]), (turned_normed[1], flat_gates[1])], BF16
     )
     gate_kept, gate_came = owned_parts(gate_grad)
-    out_grad = out_grad_part(turned_gated, grad_near, grad_far, wait=(gate_kept,))
+    scan_step(0, d_mixed0, (gate_kept,))
+    gate_came, d_raws[0] = join(gate_came, d_raws[0])
+    by_gate = to_owners(add_owned(gate_kept, gate_came))
+    out_grad = out_grad_part(turned_gated, grad_near, grad_far, wait=(d_raws[0],))
     out_kept, out_came = out_split(out_grad)
-    scan_step(0, d_mixed0, (out_kept,))
-    part, norm_gain0 = norm_step(0)
-    gate_came, out_came, d_mixed1, part = join(gate_came, out_came, d_mixed1, part)
+    part, norm_gain0 = norm_step(0, (out_kept,))
+    d_mixed1, part = join(d_mixed1, part)
     norm0 = team_sum(part)
-    by_gate = to_owners(add_owned(gate_kept, gate_came))
+    sum0 = two_halves(out0, lay)
+    scan_step(1, d_mixed1)
+    out_came, d_raws[1] = join(out_came, d_raws[1])
     out_kept = add_owned(out_kept, out_came)
     out_came = lax.ppermute(out_kept, ALL, cross)
-    sum0 = two_halves(out0, lay)
-    scan_step(1, d_mixed1)
     part, norm_gain1 = norm_step(1)
     scan_grad = row_grad(
         [(turned_normed[0], d_raws[0]), (turned_normed[1], d_raws[1])], BF16, wait=(norm_gain1,)
@@ -1127,7 +1130,8 @@
     )
     by_scan = to_owners(add_owned(scan_kept, scan_came))
     small = team_parts(pack_small(add_all(small)), lay)
-    by_scan, norm1, small = join(by_scan, two_halves(norm1, lay), small)
+    by_scan, small = join(by_scan, small)
+    norm1 = two_halves(norm1, lay)
     small = add_all(small)
     out_proj_grad = out_first.astype(F32) + out_second.astype(F32)
 

time: 480 us -> 474 us (0.988)
  waiting for transfers between devices: 140 us -> 120 us
  local copies, waits for them, and re-layouts: 51 us -> 62.1 us
    ppermute x1, waiting for transfers between devices: 28.5 us -> 0.07 us  [over_groups(): moved = lax.ppermute(values, 'wsh', pairs)]
    ppermute x2, waiting for transfers between devices: 0.01 us -> 16.9 us  [over_groups(): parts += [moved, lax.ppermute(values, ('half', 'wsh'), both)]]
    reduce_scatter x4, waiting for transfers between devices: 0.03 us -> 15.5 us  [team_sum(): own = lax.psum_scatter(part, TEAM, scatter_dimension=0, tiled=True)]
    ppermute x5, waiting for transfers between devices: 13.4 us -> 4.82 us  [wsh_shift(): lax.ppermute(values, 'wsh', [(i, (i + shift) % size) for i in range(size)])]
    ppermute x6, waiting for transfers between devices: 54.4 us -> 46.2 us  [other_half(): return lax.ppermute(values, 'half', [(0, 1), (1, 0)])]
    ppermute x9, waiting for transfers between devices: 25.9 us -> 19.3 us  [chip_flip(): lax.ppermute(values, 'chip', [(i, i ^ bits) for i in range(self.chips)])]
    unnamed x115 -> x133, local copies, waits for them, and re-layouts: 11.6 us -> 14.8 us
  transfers between devices with their start and end apart: 40 -> 40, of which waited for: 16 -> 15; matrix products, arithmetic and copies ran while one was open for 12% -> 16% of each run, Pallas kernels for 34% -> 37%
where the time goes in v4:
time: 474 us; the launch traced here: 469 us
  Pallas kernels  181 us (38%)
  waiting for transfers between devices  120 us (25%)
  local copies, waits for them, and re-layouts  62.1 us (13%)
  starting transfers between devices  55.8 us (12%)
  other arithmetic  34.7 us (7%)
  between operations  15.3 us (3%)
    pallas_call x15, Pallas kernels, call_after(): return pl.pallas_call(inner_body, **rest)(*values, *wait)  177 us
    ppermute x6, waiting for transfers between devices, other_half(): return lax.ppermute(values, 'half', [(0, 1), (1, 0)])  46.2 us
    ppermute x9, waiting for transfers between devices, chip_flip(): lax.ppermute(values, 'chip', [(i, i ^ bits) for i in range(self.chips)])  19.3 us
    ppermute x2, waiting for transfers between devices, over_groups(): parts += [moved, lax.ppermute(values, ('half', 'wsh'), both)]  16.9 us
    reduce_scatter x4, waiting for transfers between devices, team_sum(): own = lax.psum_scatter(part, TEAM, scatter_dimension=0, tiled=True)  15.5 us
    unnamed x133, local copies, waits for them, and re-layouts  14.8 us
    all_gather x4, waiting for transfers between devices, team_gather(): return lax.all_gather(values, TEAM, axis=0)  14.7 us
    ppermute x6, starting transfers between devices, other_half(): return lax.ppermute(values, 'half', [(0, 1), (1, 0)])  13.2 us
  transfers between devices with their start and end apart: 40, of which 15 were waited for; matrix products, arithmetic and copies ran while one was open for 16% of the time, Pallas kernels for 37%

profile of v4, /device:TPU:0, one launch (start us, length us, event | category | flops | bytes accessed | tf_op | source)
XLA Modules:
  0.0 468.6 jit_solution(7654404058061371902)
XLA Ops:
  26.5 17.2 %collective-permute-done.1.refs_1_ = bf16[2,64,2048]{2,1,0:T(8,128)(2,1)} collective-permute-done((bf16[2,64,2048]{2,1,0:T(8,128)(2,1)}, bf16[2,64,2048]{2,1,0:T(8,128)(2,1)}, u32[]{:S(2)}, u32[]{:S(2)}) %collective-permute-start.1) | collective-permute-done | bytes 524320 | tf_op jit(solution)/shard_map/ppermute | solution.py:787
  57.2 3.3 constant_dynamic-slice_fusion.3.refs_2_
  61.7 17.5 %collective-permute-done.3.refs_1_ = bf16[2,64,2048]{2,1,0:T(8,128)(2,1)} collective-permute-done((bf16[2,64,2048]{2,1,0:T(8,128)(2,1)}, bf16[2,64,2048]{2,1,0:T(8,128)(2,1)}, u32[]{:S(2)}, u32[]{:S(2)}) %collective-permute-start.3) | collective-permute-done | bytes 524320 | tf_op jit(solution)/shard_map/ppermute | solution.py:787
  88.3 7.3 %all-gather.11.cloned.1.call-done = bf16[16,64,2048]{2,1,0:T(8,128)(2,1)} async-done(((bf16[2,64,2048]{2,1,0:T(8,128)(2,1)}), bf16[16,64,2048]{2,1,0:T(8,128)(2,1)}) %all-gather.11.cloned.1.call-update) | async-done | bytes 4194320 | tf_op jit(solution)/shard_map/all_gather | solution.py:809
  97.2 3.7 collective-permute-start.4
  100.9 11.5 %project_tokens.2 = (bf16[2,8,64,512]{3,2,1,0:T(8,128)(2,1)}, bf16[2,8,64,776]{3,2,1,0:T(8,128)(2,1)}, bf16[2,2048,512]{2,1,0:T(8,128)(2,1)}) custom-call(bf16[8,2,64,2048]{3,2,1,0:T(8,128)(2,1)} %get-tuple-element.103.refs_0_.refs_2_, bf16[8,2,64,2048]{3,2,1,0:T(8,128)(2,1)} %get-tuple-element.108.refs_1_.refs_3_, ...), custom_call_target="tpu_custom_call" | custom-call | flops 11000000512 | bytes 27500000 | tf_op jit(solution)/shard_map/project_tokens/pallas_call | solution.py:394
  112.4 10.9 %scan_forward.2 = (bf16[1,1024,512]{2,1,0:T(8,128)(2,1)}, f32[1,4,128,512]{3,2,1,0:T(8,128)}, f32[1,4,8,768]{3,2,1,0:T(8,128)}) custom-call(s32[1]{0:T(128)} %bitcast.9.refs_0_, bf16[1,1024,776]{2,1,0:T(8,128)(2,1)} %bitcast.113, f32[4,768]{1,0:T(4,128)} %get-tuple-element.112.refs_2_.refs_5_, f32[1,768]{1,0:T(1,128)} %get-tuple-element.113.refs_3_.refs_6_, ...), custom_call_target="tpu_custom_call" | custom-call | flops 10000000000 | bytes 25000000 | tf_op jit(solution)/shard_map/scan_forward/pallas_call | solution.py:394
  123.4 11.7 %project_tokens.3 = (bf16[2,8,64,512]{3,2,1,0:T(8,128)(2,1)}, bf16[2,8,64,776]{3,2,1,0:T(8,128)(2,1)}, bf16[2,2048,512]{2,1,0:T(8,128)(2,1)}) custom-call(bf16[8,2,64,2048]{3,2,1,0:T(8,128)(2,1)} %get-tuple-element.103.refs_0_.refs_2_, bf16[8,2,64,2048]{3,2,1,0:T(8,128)(2,1)} %get-tuple-element.108.refs_1_.refs_3_, ...), custom_call_target="tpu_custom_call" | custom-call | flops 11000000512 | bytes 27500000 | tf_op jit(solution)/shard_map/project_tokens/pallas_call | solution.py:394
  135.1 10.9 %scan_forward.3 = (bf16[1,1024,512]{2,1,0:T(8,128)(2,1)}, f32[1,4,128,512]{3,2,1,0:T(8,128)}, f32[1,4,8,768]{3,2,1,0:T(8,128)}) custom-call(s32[1]{0:T(128)} %bitcast.9.refs_0_, bf16[1,1024,776]{2,1,0:T(8,128)(2,1)} %bitcast.111, f32[4,768]{1,0:T(4,128)} %get-tuple-element.112.refs_2_.refs_5_, f32[1,768]{1,0:T(1,128)} %get-tuple-element.113.refs_3_.refs_6_, ...), custom_call_target="tpu_custom_call" | custom-call | flops 10000000000 | bytes 25000000 | tf_op jit(solution)/shard_map/scan_forward/pallas_call | solution.py:394
  150.5 7.5 %all-gather.15.cloned.1.call-done = bf16[16,64,2048]{2,1,0:T(8,128)(2,1)} async-done(((bf16[2,64,2048]{2,1,0:T(8,128)(2,1)}), bf16[16,64,2048]{2,1,0:T(8,128)(2,1)}) %all-gather.15.cloned.1.call-update) | async-done | bytes 4194320 | tf_op jit(solution)/shard_map/all_gather | solution.py:809
  158.0 7.4 %gate_stats.2 = (f32[2,8,64,512]{3,2,1,0:T(8,128)}, f32[2,1024]{1,0:T(2,128)}) custom-call(bf16[8,2,64,2048]{3,2,1,0:T(8,128)(2,1)} %bitcast.104, bf16[8,2,64,2048]{3,2,1,0:T(8,128)(2,1)} %bitcast.107, bf16[512,2048]{1,0:T(8,128)(2,1)} %select_add_fusion.refs_2_.refs_5_, bf16[2,8,64,512]{3,2,1,0:T(8,128)(2,1)} %bitcast.97, ...), custom_call_target="tpu_custom_call" | custom-call | flops 7000000000 | bytes 17500000 | tf_op jit(solution)/shard_map/gate_stats/pallas_call | solution.py:394
  165.6 7.4 %gate_stats.3 = (f32[2,8,64,512]{3,2,1,0:T(8,128)}, f32[2,1024]{1,0:T(2,128)}) custom-call(bf16[8,2,64,2048]{3,2,1,0:T(8,128)(2,1)} %bitcast.105, bf16[8,2,64,2048]{3,2,1,0:T(8,128)(2,1)} %bitcast.108, bf16[512,2048]{1,0:T(8,128)(2,1)} %select_add_fusion.refs_2_.refs_5_, bf16[2,8,64,512]{3,2,1,0:T(8,128)(2,1)} %get-tuple-element.129.refs_3_.refs_0_, ...), custom_call_target="tpu_custom_call" | custom-call | flops 7000000000 | bytes 17500000 | tf_op jit(solution)/shard_map/gate_stats/pallas_call | solution.py:394
  181.6 8.8 %gate_back.2 = (bf16[2,512,512]{2,1,0:T(8,128)(2,1)}, bf16[2,8,64,512]{3,2,1,0:T(8,128)(2,1)}, bf16[2,8,64,512]{3,2,1,0:T(8,128)(2,1)}, bf16[1024,2048]{1,0:T(8,128)(2,1)}, f32[1,512]{1,0:T(1,128)}) custom-call(bf16[2,8,64,512]{3,2,1,0:T(8,128)(2,1)} %bitcast.98, bf16[2,8,64,512]{3,2,1,0:T(8,128)(2,1)} %get-tuple-element.118.refs_4_.refs_1_, ...), custom_call_target="tpu_custom_call" | custom-call | tf_op jit(solution)/shard_map/gate_back/pallas_call | solution.py:394
  192.4 8.8 %gate_back.3 = (bf16[2,512,512]{2,1,0:T(8,128)(2,1)}, bf16[2,8,64,512]{3,2,1,0:T(8,128)(2,1)}, bf16[2,8,64,512]{3,2,1,0:T(8,128)(2,1)}, bf16[1024,2048]{1,0:T(8,128)(2,1)}, f32[1,512]{1,0:T(1,128)}) custom-call(bf16[2,8,64,512]{3,2,1,0:T(8,128)(2,1)} %get-tuple-element.129.refs_3_.refs_0_, bf16[2,8,64,512]{3,2,1,0:T(8,128)(2,1)} %get-tuple-element.130.refs_4_.refs_1_, ...), custom_call_target="tpu_custom_call" | custom-call | tf_op jit(solution)/shard_map/gate_back/pallas_call | solution.py:394
  201.3 8.7 %row_grad.2 = bf16[2048,512]{1,0:T(8,128)(2,1)} custom-call(bf16[2,2048,512]{2,1,0:T(8,128)(2,1)} %get-tuple-element.110.refs_0_, bf16[1024,512]{1,0:T(8,128)(2,1)} %bitcast.87, bf16[2,2048,512]{2,1,0:T(8,128)(2,1)} %get-tuple-element.133.refs_2_, bf16[1024,512]{1,0:T(8,128)(2,1)} %bitcast.86), custom_call_target="tpu_custom_call" | custom-call | tf_op jit(solution)/shard_map/row_grad/pallas_call | solution.py:394
  214.1 22.2 %scan_backward.2 = (bf16[1,1024,776]{2,1,0:T(8,128)(2,1)}, f32[8,768]{1,0:T(8,128)}, f32[1,512]{1,0:T(1,128)}, f32[2,8,1]{2,1,0:T(8,128)}) custom-call(s32[1]{0:T(128)} %bitcast.9.refs_0_, bf16[1,1024,776]{2,1,0:T(8,128)(2,1)} %bitcast.114, bf16[1,1024,512]{2,1,0:T(8,128)(2,1)} %bitcast.110, f32[1,4,128,512]{3,2,1,0:T(8,128)} %get-tuple-element.143.refs_3_, ...), custom_call_target="tpu_custom_call" | custom-call | flops 22000001024 | bytes 55000000 | tf_op jit(solution)/shard_map/scan_backward/pallas_call | solution.py:394
  237.4 10.4 %out_grad_part.1 = bf16[512,2048]{1,0:T(8,128)(2,1)} custom-call(bf16[2,512,512]{2,1,0:T(8,128)(2,1)} %get-tuple-element.146.refs_0_, bf16[2,512,512]{2,1,0:T(8,128)(2,1)} %get-tuple-element.147.refs_1_, bf16[8,2,64,2048]{3,2,1,0:T(8,128)(2,1)} %bitcast.106, bf16[8,2,64,2048]{3,2,1,0:T(8,128)(2,1)} %bitcast.109, ...), custom_call_target="tpu_custom_call" | custom-call | flops 8000000000 | bytes 20000000 | tf_op jit(solution)/shard_map/out_grad_part/pallas_call | solution.py:394
  250.8 11.5 %norm_part.2 = (bf16[1024,2048]{1,0:T(8,128)(2,1)}, f32[1,2048]{1,0:T(1,128)}) custom-call(bf16[2,8,64,512]{3,2,1,0:T(8,128)(2,1)} %get-tuple-element.132.refs_0_, bf16[2,8,64,776]{3,2,1,0:T(8,128)(2,1)} %bitcast.80, bf16[8,2,64,2048]{3,2,1,0:T(8,128)(2,1)} %get-tuple-element.103.refs_0_.refs_2_, ...), custom_call_target="tpu_custom_call" | custom-call | tf_op jit(solution)/shard_map/norm_part/pallas_call | solution.py:394
  265.2 4.6 all-to-all-start
  271.6 22.2 %scan_backward.3 = (bf16[1,1024,776]{2,1,0:T(8,128)(2,1)}, f32[8,768]{1,0:T(8,128)}, f32[1,512]{1,0:T(1,128)}, f32[2,8,1]{2,1,0:T(8,128)}) custom-call(s32[1]{0:T(128)} %bitcast.9.refs_0_, bf16[1,1024,776]{2,1,0:T(8,128)(2,1)} %bitcast.112, bf16[1,1024,512]{2,1,0:T(8,128)(2,1)} %bitcast.93, f32[1,4,128,512]{3,2,1,0:T(8,128)} %get-tuple-element.152.refs_3_, ...), custom_call_target="tpu_custom_call" | custom-call | flops 22000001024 | bytes 55000000 | tf_op jit(solution)/shard_map/scan_backward/pallas_call | solution.py:394
  301.3 3.6 collective-permute-start.16
  304.9 11.5 %norm_part.3 = (bf16[1024,2048]{1,0:T(8,128)(2,1)}, f32[1,2048]{1,0:T(1,128)}) custom-call(bf16[2,8,64,512]{3,2,1,0:T(8,128)(2,1)} %get-tuple-element.141.refs_0_, bf16[2,8,64,776]{3,2,1,0:T(8,128)(2,1)} %bitcast.82, bf16[8,2,64,2048]{3,2,1,0:T(8,128)(2,1)} %get-tuple-element.103.refs_0_.refs_2_, ...), custom_call_target="tpu_custom_call" | custom-call | tf_op jit(solution)/shard_map/norm_part/pallas_call | solution.py:394
  316.4 13.2 %row_grad.3 = bf16[2048,776]{1,0:T(8,128)(2,1)} custom-call(bf16[2,2048,512]{2,1,0:T(8,128)(2,1)} %get-tuple-element.110.refs_0_, bf16[1024,776]{1,0:T(8,128)(2,1)} %get-tuple-element.148.refs_4_.refs_1_, bf16[2,2048,512]{2,1,0:T(8,128)(2,1)} %get-tuple-element.133.refs_2_, bf16[1024,776]{1,0:T(8,128)(2,1)} %get-tuple-element.157.refs_3_, ...), custom_call_target="tpu_custom_call" | custom-call | tf_op jit(solution)/shard_map/row_grad/pallas_call | solution.py:394
  329.6 4.3 dynamic-slice_bitcast_fusion.1
  342.7 15.5 %reduce-scatter.9.cloned.1.call-done = bf16[128,2048]{1,0:T(8,128)(2,1)} async-done(((bf16[1024,2048]{1,0:T(8,128)(2,1)}), bf16[128,2048]{1,0:T(8,128)(2,1)}) %reduce-scatter.9.cloned.1.call-update) | async-done | bytes 524304 | tf_op jit(solution)/shard_map/reduce_scatter | solution.py:819
  365.0 12.0 %collective-permute-done.22.refs_8_ = f32[6424]{0:T(1024)S(1)} collective-permute-done((f32[6424]{0:T(1024)S(1)}, f32[6424]{0:T(1024)S(1)}, u32[]{:S(2)}, u32[]{:S(2)}) %collective-permute-start.22) | collective-permute-done | bytes 25728 | tf_op jit(solution)/shard_map/ppermute | solution.py:1081
  377.1 4.9 %collective-permute-done.20.refs_6_ = f32[6424]{0:T(1024)S(1)} collective-permute-done((f32[6424]{0:T(1024)S(1)}, f32[6424]{0:T(1024)S(1)}, u32[]{:S(2)}, u32[]{:S(2)}) %collective-permute-start.20) | collective-permute-done | bytes 25728 | tf_op jit(solution)/shard_map/ppermute | solution.py:1081
  382.8 3.3 add_convert_fusion
  386.1 5.7 %all-to-all-start.1 = ((bf16[16,64,776]{2,1,0:T(8,128)(2,1)}), bf16[16,64,776]{2,1,0:T(8,128)(2,1)S(1)}, u32[]{:S(2)}, u32[]{:S(2)}) async-start(bf16[16,64,776]{2,1,0:T(8,128)(2,1)} %add_convert_fusion), calls=%async_computation.5 | async-start | bytes 3670016 | tf_op jit(solution)/shard_map/all_to_all | solution.py:1047
  416.3 17.8 %collective-permute-done.27.refs_4_ = f32[28096]{0:T(1024)S(1)} collective-permute-done((f32[28096]{0:T(1024)S(1)}, f32[28096]{0:T(1024)S(1)}, u32[]{:S(2)}, u32[]{:S(2)}) %collective-permute-start.27) | collective-permute-done | bytes 112416 | tf_op jit(solution)/shard_map/ppermute | solution.py:790
  445.2 3.6 owned_rows.1
  448.8 8.6 %collective-permute-done.23 = bf16[64,2048]{1,0:T(8,128)(2,1)S(1)} collective-permute-done((bf16[64,2048]{1,0:T(8,128)(2,1)S(1)}, bf16[64,2048]{1,0:T(8,128)(2,1)S(1)}, u32[]{:S(2)}, u32[]{:S(2)}) %collective-permute-start.23) | collective-permute-done | bytes 262176 | tf_op jit(solution)/shard_map/ppermute | solution.py:787
  (308 shorter events, 135.8 us)
Async XLA Ops:
  7.2 72.0 %all-gather.9.cloned.1.call-start = ((), (), s32[]{:S(2)}) async-start(), calls=%async_computation.10 | async-start | bytes 4718592 | tf_op jit(solution)/shard_map/all_gather | solution.py:809
  12.0 83.6 %all-gather.11.cloned.1.call-start = ((), (), s32[]{:S(2)}) async-start(), calls=%async_computation.11 | async-start | bytes 4718592 | tf_op jit(solution)/shard_map/all_gather | solution.py:809
  14.9 31.9 %collective-permute-start = (bf16[640,1024]{1,0:T(8,128)(2,1)}, bf16[640,1024]{1,0:T(8,128)(2,1)S(1)}, u32[]{:S(2)}, u32[]{:S(2)}) collective-permute-start(bf16[640,1024]{1,0:T(8,128)(2,1)} %pad_maximum_fusion.4), channel_id=1, source_target_pairs={{0,1},{1,0},{2,3},{3,2},{4,5},{5,4},{6,7},{7,6},{8,9},{9,8},{10,11... | collective-permute-start | bytes 3932168 | tf_op jit(solution)/shard_map/ppermute | solution.py:794
  17.8 25.9 %collective-permute-start.1 = (bf16[2,64,2048]{2,1,0:T(8,128)(2,1)}, bf16[2,64,2048]{2,1,0:T(8,128)(2,1)}, u32[]{:S(2)}, u32[]{:S(2)}) collective-permute-start(bf16[2,64,2048]{2,1,0:T(8,128)(2,1)} %get-tuple-element.212), channel_id=1, source_target_pairs={{0,16},{16,0},{1,17},{17,1},{2,18},{18,2},{3,19},{19,3},{4,20},{20... | collective-permute-start | bytes 1572872 | tf_op jit(solution)/shard_map/ppermute | solution.py:787
  48.0 102.5 %all-gather.13.cloned.1.call-start = ((), (), s32[]{:S(2)}) async-start(), calls=%async_computation.12 | async-start | bytes 4718592 | tf_op jit(solution)/shard_map/all_gather | solution.py:809
  48.0 31.1 %collective-permute-start.2 = (bf16[648,1024]{1,0:T(8,128)(2,1)}, bf16[648,1024]{1,0:T(8,128)(2,1)S(1)}, u32[]{:S(2)}, u32[]{:S(2)}) collective-permute-start(bf16[648,1024]{1,0:T(8,128)(2,1)} %get-tuple-element.101), channel_id=1, source_target_pairs={{0,1},{1,0},{2,3},{3,2},{4,5},{5,4},{6,7},{7,6},{8,9},{9,8},{10,11... | collective-permute-start | bytes 3981320 | tf_op jit(solution)/shard_map/ppermute | solution.py:794
  54.0 25.2 %collective-permute-start.3 = (bf16[2,64,2048]{2,1,0:T(8,128)(2,1)}, bf16[2,64,2048]{2,1,0:T(8,128)(2,1)}, u32[]{:S(2)}, u32[]{:S(2)}) collective-permute-start(bf16[2,64,2048]{2,1,0:T(8,128)(2,1)} %get-tuple-element.102), channel_id=1, source_target_pairs={{0,16},{16,0},{1,17},{17,1},{2,18},{18,2},{3,19},{19,3},{4,20},{20... | collective-permute-start | bytes 1572872 | tf_op jit(solution)/shard_map/ppermute | solution.py:787
  95.6 62.3 %all-gather.15.cloned.1.call-start = ((), (), s32[]{:S(2)}) async-start(), calls=%async_computation.13 | async-start | bytes 4718592 | tf_op jit(solution)/shard_map/all_gather | solution.py:809
  96.2 203.3 %reduce-scatter.5.cloned.1.call-start = ((), (), s32[]{:S(2)}) async-start(), calls=%async_computation.6 | async-start | bytes 4718592 | tf_op jit(solution)/shard_map/reduce_scatter | solution.py:819
  97.2 48.8 %collective-permute-start.4 = (bf16[512,2048]{1,0:T(8,128)(2,1)S(1)}, bf16[512,2048]{1,0:T(8,128)(2,1)S(1)}, u32[]{:S(2)}, u32[]{:S(2)}) collective-permute-start(bf16[512,2048]{1,0:T(8,128)(2,1)S(1)} %copy-done), channel_id=1, source_target_pairs={{0,1},{3,2},{4,5},{7,6},{8,9},{11,10},{12,13},{15,14},{16,17},{19,... | collective-permute-start | bytes 6291464 | tf_op jit(solution)/shard_map/ppermute | solution.py:916
  177.5 12.9 %collective-permute-start.12 = (f32[2,1024]{1,0:T(2,128)S(1)}, f32[2,1024]{1,0:T(2,128)S(1)}, u32[]{:S(2)}, u32[]{:S(2)}) collective-permute-start(f32[2,1024]{1,0:T(2,128)S(1)} %add.198.refs_0_), channel_id=1, source_target_pairs={{0,12},{4,8},{8,4},{12,0},{1,13},{5,9},{9,5},{13,1},{2,14},{6,10},... | collective-permute-start | bytes 24584 | tf_op jit(solution)/shard_map/ppermute | solution.py:790
  178.9 11.4 %collective-permute-start.11 = (f32[2,1024]{1,0:T(2,128)S(1)}, f32[2,1024]{1,0:T(2,128)S(1)}, u32[]{:S(2)}, u32[]{:S(2)}) collective-permute-start(f32[2,1024]{1,0:T(2,128)S(1)} %add.198.refs_0_), channel_id=1, source_target_pairs={{0,8},{4,12},{8,0},{12,4},{1,9},{5,13},{9,1},{13,5},{2,10},{6,14},... | collective-permute-start | bytes 24584 | tf_op jit(solution)/shard_map/ppermute | solution.py:790
  191.1 149.7 %reduce-scatter.7.cloned.1.call-start = ((), (), s32[]{:S(2)}) async-start(), calls=%async_computation.7 | async-start | bytes 4718592 | tf_op jit(solution)/shard_map/reduce_scatter | solution.py:819
  201.2 156.9 %reduce-scatter.9.cloned.1.call-start = ((), (), s32[]{:S(2)}) async-start(), calls=%async_computation.8 | async-start | bytes 4718592 | tf_op jit(solution)/shard_map/reduce_scatter | solution.py:819
  212.7 23.6 %collective-permute-start.13 = (bf16[16,64,512]{2,1,0:T(8,128)(2,1)S(1)}, bf16[16,64,512]{2,1,0:T(8,128)(2,1)S(1)}, u32[]{:S(2)}, u32[]{:S(2)}) collective-permute-start(bf16[16,64,512]{2,1,0:T(8,128)(2,1)S(1)} %get-tuple-element.200), channel_id=1, source_target_pairs={{0,1},{1,0},{2,3},{3,2},{4,5},{5,4},{6,7},{7,6},{8,9},{9,8},{10,11... | collective-permute-start | bytes 3145736 | tf_op jit(solution)/shard_map/ppermute | solution.py:794
  265.2 68.7 %all-to-all-start = ((bf16[16,64,512]{2,1,0:T(8,128)(2,1)}), bf16[16,64,512]{2,1,0:T(8,128)(2,1)}, u32[]{:S(2)}, u32[]{:S(2)}) async-start(bf16[16,64,512]{2,1,0:T(8,128)(2,1)} %add_convert_fusion.3), calls=%async_computation | async-start | bytes 2097152 | tf_op jit(solution)/shard_map/all_to_all | solution.py:1047
  269.8 171.9 %reduce-scatter.11.cloned.1.call-start = ((), (), s32[]{:S(2)}) async-start(), calls=%async_computation.9 | async-start | bytes 4718592 | tf_op jit(solution)/shard_map/reduce_scatter | solution.py:819
  270.1 25.5 %collective-permute-start.14 = (bf16[2,128,2048]{2,1,0:T(8,128)(2,1)S(1)}, bf16[2,128,2048]{2,1,0:T(8,128)(2,1)S(1)}, u32[]{:S(2)}, u32[]{:S(2)}) collective-permute-start(bf16[2,128,2048]{2,1,0:T(8,128)(2,1)S(1)} %get-tuple-element.198), channel_id=1, source_target_pairs={{0,1},{1,0},{2,3},{3,2},{4,5},{5,4},{6,7},{7,6},{8,9},{9,8},{10,11... | collective-permute-start | bytes 3145736 | tf_op jit(solution)/shard_map/ppermute | solution.py:794
  298.2 37.4 %collective-permute-start.15 = (bf16[2,128,2048]{2,1,0:T(8,128)(2,1)S(1)}, bf16[2,128,2048]{2,1,0:T(8,128)(2,1)S(1)}, u32[]{:S(2)}, u32[]{:S(2)}) collective-permute-start(bf16[2,128,2048]{2,1,0:T(8,128)(2,1)S(1)} %add_convert_fusion.2), channel_id=1, source_target_pairs={{16,0},{20,4},{24,8},{28,12},{2,18},{6,22},{10,26},{14,30},{17,1},... | collective-permute-start | bytes 3145736 | tf_op jit(solution)/shard_map/ppermute | solution.py:1116
  301.3 37.1 %collective-permute-start.16 = (bf16[64,2048]{1,0:T(8,128)(2,1)S(1)}, bf16[64,2048]{1,0:T(8,128)(2,1)S(1)}, u32[]{:S(2)}, u32[]{:S(2)}) collective-permute-start(bf16[64,2048]{1,0:T(8,128)(2,1)S(1)} %get-tuple-element.215), channel_id=1, source_target_pairs={{0,16},{16,0},{1,17},{17,1},{2,18},{18,2},{3,19},{19,3},{4,20},{20... | collective-permute-start | bytes 786440 | tf_op jit(solution)/shard_map/ppermute | solution.py:787
  339.2 42.8 %collective-permute-start.17 = (bf16[16,64,776]{2,1,0:T(8,128)(2,1)}, bf16[16,64,776]{2,1,0:T(8,128)(2,1)}, u32[]{:S(2)}, u32[]{:S(2)}) collective-permute-start(bf16[16,64,776]{2,1,0:T(8,128)(2,1)} %get-tuple-element.196), channel_id=1, source_target_pairs={{0,1},{1,0},{2,3},{3,2},{4,5},{5,4},{6,7},{7,6},{8,9},{9,8},{10,11... | collective-permute-start | bytes 4767752 | tf_op jit(solution)/shard_map/ppermute | solution.py:794
  342.7 39.3 %collective-permute-start.18 = (bf16[64,2048]{1,0:T(8,128)(2,1)}, bf16[64,2048]{1,0:T(8,128)(2,1)S(1)}, u32[]{:S(2)}, u32[]{:S(2)}) collective-permute-start(bf16[64,2048]{1,0:T(8,128)(2,1)} %get-tuple-element.219), channel_id=1, source_target_pairs={{0,16},{16,0},{1,17},{17,1},{2,18},{18,2},{3,19},{19,3},{4,20},{20... | collective-permute-start | bytes 786440 | tf_op jit(solution)/shard_map/ppermute | solution.py:787
  360.0 22.0 %collective-permute-start.19 = (bf16[64,2048]{1,0:T(8,128)(2,1)}, bf16[64,2048]{1,0:T(8,128)(2,1)S(1)}, u32[]{:S(2)}, u32[]{:S(2)}) collective-permute-start(bf16[64,2048]{1,0:T(8,128)(2,1)} %get-tuple-element.217), channel_id=1, source_target_pairs={{0,16},{16,0},{1,17},{17,1},{2,18},{18,2},{3,19},{19,3},{4,20},{20... | collective-permute-start | bytes 786440 | tf_op jit(solution)/shard_map/ppermute | solution.py:787
  362.5 14.4 %collective-permute-start.22 = (f32[6424]{0:T(1024)S(1)}, f32[6424]{0:T(1024)S(1)}, u32[]{:S(2)}, u32[]{:S(2)}) collective-permute-start(f32[6424]{0:T(1024)S(1)} %concatenate.43.refs_5_), channel_id=1, source_target_pairs={{0,17},{16,1},{1,16},{17,0},{2,19},{18,3},{3,18},{19,2},{4,21},{20... | collective-permute-start | bytes 77096 | tf_op jit(solution)/shard_map/ppermute | solution.py:1081
  364.2 12.9 %collective-permute-start.21 = (f32[6424]{0:T(1024)S(1)}, f32[6424]{0:T(1024)S(1)}, u32[]{:S(2)}, u32[]{:S(2)}) collective-permute-start(f32[6424]{0:T(1024)S(1)} %concatenate.43.refs_5_), channel_id=1, source_target_pairs={{0,1},{1,0},{2,3},{3,2},{4,5},{5,4},{6,7},{7,6},{8,9},{9,8},{10,11... | collective-permute-start | bytes 77096 | tf_op jit(solution)/shard_map/ppermute | solution.py:1077
  386.1 50.2 %all-to-all-start.1 = ((bf16[16,64,776]{2,1,0:T(8,128)(2,1)}), bf16[16,64,776]{2,1,0:T(8,128)(2,1)S(1)}, u32[]{:S(2)}, u32[]{:S(2)}) async-start(bf16[16,64,776]{2,1,0:T(8,128)(2,1)} %add_convert_fusion), calls=%async_computation.5 | async-start | bytes 3670016 | tf_op jit(solution)/shard_map/all_to_all | solution.py:1047
  394.4 15.1 %collective-permute-start.28 = (bf16[128,2048]{1,0:T(8,128)(2,1)}, bf16[128,2048]{1,0:T(8,128)(2,1)S(1)}, u32[]{:S(2)}, u32[]{:S(2)}) collective-permute-start(bf16[128,2048]{1,0:T(8,128)(2,1)} %get-tuple-element.201), channel_id=1, source_target_pairs={{0,0},{4,4},{8,8},{12,12},{18,16},{22,20},{26,24},{30,28},{1,1},{5... | collective-permute-start | bytes 1572872 | tf_op jit(solution)/shard_map/ppermute | solution.py:1125
  396.2 13.3 %collective-permute-start.29 = (bf16[128,2048]{1,0:T(8,128)(2,1)S(1)}, bf16[128,2048]{1,0:T(8,128)(2,1)}, u32[]{:S(2)}, u32[]{:S(2)}) collective-permute-start(bf16[128,2048]{1,0:T(8,128)(2,1)S(1)} %get-tuple-element.202), channel_id=1, source_target_pairs={{0,2},{4,6},{8,10},{12,14},{18,18},{22,22},{26,26},{30,30},{1,3},{... | collective-permute-start | bytes 1572872 | tf_op jit(solution)/shard_map/ppermute | solution.py:1126
  411.6 22.5 %collective-permute-start.27 = (f32[28096]{0:T(1024)S(1)}, f32[28096]{0:T(1024)S(1)}, u32[]{:S(2)}, u32[]{:S(2)}) collective-permute-start(f32[28096]{0:T(1024)S(1)} %add.219.refs_1_), channel_id=1, source_target_pairs={{0,12},{4,8},{8,4},{12,0},{1,13},{5,9},{9,5},{13,1},{2,14},{6,10},... | collective-permute-start | bytes 337160 | tf_op jit(solution)/shard_map/ppermute | solution.py:790
  414.6 21.1 %collective-permute-start.26 = (f32[28096]{0:T(1024)S(1)}, f32[28096]{0:T(1024)S(1)}, u32[]{:S(2)}, u32[]{:S(2)}) collective-permute-start(f32[28096]{0:T(1024)S(1)} %add.219.refs_1_), channel_id=1, source_target_pairs={{0,8},{4,12},{8,0},{12,4},{1,9},{5,13},{9,1},{13,5},{2,10},{6,14},... | collective-permute-start | bytes 337160 | tf_op jit(solution)/shard_map/ppermute | solution.py:790
  415.1 21.1 %collective-permute-start.25 = (f32[28096]{0:T(1024)S(1)}, f32[28096]{0:T(1024)}, u32[]{:S(2)}, u32[]{:S(2)}) collective-permute-start(f32[28096]{0:T(1024)S(1)} %add.219.refs_1_), channel_id=1, source_target_pairs={{0,4},{4,0},{8,12},{12,8},{1,5},{5,1},{9,13},{13,9},{2,6},{6,2},{1... | collective-permute-start | bytes 337160 | tf_op jit(solution)/shard_map/ppermute | solution.py:790
  442.8 14.5 %collective-permute-start.23 = (bf16[64,2048]{1,0:T(8,128)(2,1)S(1)}, bf16[64,2048]{1,0:T(8,128)(2,1)S(1)}, u32[]{:S(2)}, u32[]{:S(2)}) collective-permute-start(bf16[64,2048]{1,0:T(8,128)(2,1)S(1)} %get-tuple-element.214), channel_id=1, source_target_pairs={{0,16},{16,0},{1,17},{17,1},{2,18},{18,2},{3,19},{19,3},{4,20},{20... | collective-permute-start | bytes 786440 | tf_op jit(solution)/shard_map/ppermute | solution.py:787
  (76 other events, 500.1 us)
Sparse Core Ops, SparseCore 0:
  12.1 41.7 all-gather.8
  55.5 40.0 all-gather.10
  97.2 30.0 all-gather.12
  128.8 29.1 all-gather.14
  191.2 47.3 reduce-scatter.4
  240.7 60.0 reduce-scatter.6
  303.1 55.0 reduce-scatter.8
  360.4 76.1 reduce-scatter.10
